TPU v7x, 32 devices: a whole 2x2x4 slice. The times are simulated.
32 devices in a mesh: dp: 2 (over core), expert: 16 (over z, y, x).
Axes of the slice: x: 2, y: 2, z: 4, core: 2. Of those that a mesh axis runs over, the one named last changes fastest.
Arguments:
- tokens: bfloat16 [32, 256, 2048], P(('dp', 'expert')), may hold values from -6 to 6
- w_qkv: bfloat16 [2048, 6144], P(('dp', 'expert')), may hold values from -0.125 to 0.125
- w_out: bfloat16 [2048, 2048], P(('dp', 'expert')), may hold values from -0.75 to 0.75
- w_router: bfloat16 [2048, 16], P(('dp', 'expert')), may hold values from -0.0625 to 0.0625
- gains: bfloat16 [4, 2048], P(None, ('dp', 'expert')), may hold values from 0.099609375 to 1.8984375
- w_gate: bfloat16 [16, 2048, 1024], P('expert', None, 'dp'), may hold values from -0.125 to 0.125
- w_up: bfloat16 [16, 2048, 1024], P('expert', None, 'dp'), may hold values from -0.125 to 0.125
- w_down: bfloat16 [16, 1024, 2048], P('expert', 'dp'), may hold values from -4 to 4
- lengths: int32 [32], P(('dp', 'expert')), may hold values from 64 to 256, as said below
- routes: int32 [32, 256, 8], P(('dp', 'expert')), may hold values from 0 to 15, as said below
- send_counts: int32 [32, 16], P(('dp', 'expert')), may hold values from 0 to 128, as said below
- cotangent: bfloat16 [32, 256, 2048], P(('dp', 'expert')), may hold values from -6 to 6
Outputs:
- result: bfloat16 [32, 256, 2048], P(('dp', 'expert'))
- grad_tokens: float32 [32, 256, 2048], P(('dp', 'expert'))
- grad_qkv: float32 [2048, 6144], P(('dp', 'expert'))
- grad_out: float32 [2048, 2048], P(('dp', 'expert'))
- grad_router: float32 [2048, 16], P(('dp', 'expert'))
- grad_gains: float32 [4, 2048], P(None, ('dp', 'expert'))
- grad_gate: float32 [16, 2048, 1024], P('expert', None, 'dp')
- grad_up: float32 [16, 2048, 1024], P('expert', None, 'dp')
- grad_down: float32 [16, 1024, 2048], P('expert', 'dp')
- balance: float32 [], replicated
Inputs may be any that keep to these rules, and one draw needn't show every extreme that they name: Row r holds one sequence in its first lengths[r] slots; the rest are padding; at least one row is full. Each slot names 8 different experts; the routes of padded slots are not used. send_counts[r, e] is the number of live slots of row r that name expert e; one expert is named by exactly min(128, lengths[r]) live slots of every row r.
All inputs are finite; a program needn't handle non-finite values.
Results may differ from a plain program's by a relative error of at most 0.02.
Values may be sent and summed in bfloat16 or wider, within the bound.
A program may use at most 384 MiB of HBM per device.

v0:
```python
import math

import jax
import jax.numpy as jnp
from jax import lax
from jax.sharding import PartitionSpec as P

D = 2048
HEADS = 16
HEAD = 128


NORM_EPS = 1e-05
BALANCE_WEIGHT = 0.01


def norm_scale(values, gain_row):
    return (
        values * lax.rsqrt(jnp.mean(values * values, axis=-1, keepdims=True) + NORM_EPS) * gain_row
    )


def rope_tables(positions_count, head_width):
    half_width = head_width // 2
    frequency = jnp.exp(
        jnp.arange(half_width, dtype=jnp.float32) * (-2.0 * math.log(10000.0) / head_width)
    )
    angles = jnp.arange(positions_count, dtype=jnp.float32)[:, None] * frequency[None, :]
    angles = jnp.concatenate([angles, angles], axis=1)
    return (jnp.cos(angles)[:, None, :], jnp.sin(angles)[:, None, :])


def rotate(values, cosine, sine_part):
    half_width = values.shape[-1] // 2
    turned = jnp.concatenate([-values[..., half_width:], values[..., :half_width]], axis=-1)
    return values * cosine + turned * sine_part


def query_key(query_part, key_part, query_gain, key_gain):
    positions_count = query_part.shape[0]
    cosine, sine_part = rope_tables(positions_count, HEAD)
    queries = norm_scale(query_part, query_gain).reshape(positions_count, HEADS, HEAD)
    key_heads = norm_scale(key_part, key_gain).reshape(positions_count, HEADS, HEAD)
    return (rotate(queries, cosine, sine_part), rotate(key_heads, cosine, sine_part))


def expert_forward(rows_in, gate_weight, up_weight, down_weight):
    gate_pre = jnp.einsum(
        "nkcd,kdf->nkcf", rows_in, gate_weight, preferred_element_type=jnp.float32
    )
    up_pre = jnp.einsum("nkcd,kdf->nkcf", rows_in, up_weight, preferred_element_type=jnp.float32)
    hidden_low = (jax.nn.silu(gate_pre) * up_pre).astype(jnp.bfloat16)
    output = jnp.einsum(
        "nkcf,kfd->nkcd", hidden_low, down_weight, preferred_element_type=jnp.float32
    )
    return (gate_pre, up_pre, hidden_low, output)


def body(
    tokens,
    w_qkv,
    w_out,
    w_router,
    gains,
    w_gate,
    w_up,
    w_down,
    lengths,
    routes,
    send_counts,
    cotangent,
):
    row_count = tokens.shape[1]
    top_count = routes.shape[2]
    expert_count = w_router.shape[1]
    owners = lax.axis_size("expert")
    local_experts = expert_count // owners
    capacity = row_count * top_count // expert_count
    slots_all = row_count * lax.axis_size("dp") * owners
    balance_factor = float(expert_count) / (float(top_count) * float(slots_all) * float(slots_all))
    score_scale = HEAD ** (-0.5)
    inputs = tokens[0].astype(jnp.float32)
    positions = jnp.arange(row_count, dtype=jnp.int32)
    live_slots = positions < lengths[0]
    live_float = live_slots.astype(jnp.float32)[:, None]
    mixer_parts = (
        lax.all_gather(w_qkv, ("dp", "expert"), axis=0, tiled=True),
        lax.all_gather(w_out, ("dp", "expert"), axis=0, tiled=True),
        lax.all_gather(w_router, ("dp", "expert"), axis=0, tiled=True),
        lax.all_gather(gains, ("dp", "expert"), axis=1, tiled=True),
    )
    qkv_weight, out_weight, router_weight, gain_rows = mixer_parts
    gain_float = gain_rows.astype(jnp.float32)
    attn_in, attn_norm_back = jax.vjp(norm_scale, inputs, gain_float[0])
    normed = attn_in.astype(jnp.bfloat16)
    projected = jnp.dot(normed, qkv_weight, preferred_element_type=jnp.float32)
    (rot_query, rot_keys), query_key_back = jax.vjp(
        query_key, projected[:, :D], projected[:, D : 2 * D], gain_float[1], gain_float[2]
    )
    queries = rot_query.astype(jnp.bfloat16)
    keys_low = rot_keys.astype(jnp.bfloat16)
    values_low = projected[:, 2 * D :].astype(jnp.bfloat16).reshape(row_count, HEADS, HEAD)
    allowed = (positions[None, :] <= positions[:, None]) & live_slots[None, :]
    scores = (
        jnp.einsum("qhd,khd->hqk", queries, keys_low, preferred_element_type=jnp.float32)
        * score_scale
    )
    scores = jnp.where(allowed[None], scores, -1e30)
    highest = jnp.max(scores, axis=-1, keepdims=True)
    expo_scores = jnp.exp(scores - highest)
    totals = jnp.sum(expo_scores, axis=-1, keepdims=True)
    attn_probs = expo_scores / totals
    log_total = highest + jnp.log(totals)
    mixed_heads = jnp.einsum(
        "hqk,khd->qhd",
        attn_probs.astype(jnp.bfloat16),
        values_low,
        preferred_element_type=jnp.float32,
    )
    mixed_low = mixed_heads.reshape(row_count, D).astype(jnp.bfloat16)
    hidden_state = inputs + jnp.dot(mixed_low, out_weight, preferred_element_type=jnp.float32)
    ffn_in, ffn_norm_back = jax.vjp(norm_scale, hidden_state, gain_float[3])
    ffn_low = ffn_in.astype(jnp.bfloat16)
    logits = jnp.dot(ffn_low, router_weight, preferred_element_type=jnp.float32)
    router_probs = jax.nn.softmax(logits, axis=-1)
    count_float = send_counts[0].astype(jnp.float32)
    prob_local = jnp.sum(router_probs * live_float, axis=0)
    count_total, prob_total = lax.psum((count_float, prob_local), ("dp", "expert"))
    balance = jnp.sum(count_total * prob_total) * balance_factor
    route_rows = routes[0]
    expert_ids = jnp.arange(expert_count, dtype=jnp.int32)
    route_hot = (route_rows[:, :, None] == expert_ids) & live_slots[:, None, None]
    route_int = route_hot.astype(jnp.int32)
    per_token = jnp.sum(route_int, axis=1)
    earlier = jnp.cumsum(per_token, axis=0) - per_token
    route_rank = jnp.sum(earlier[:, None, :] * route_int, axis=-1)
    limits = jnp.sum(jnp.minimum(send_counts[0], capacity)[None, None, :] * route_int, axis=-1)
    kept_route = route_rank < limits
    target_expert = jnp.where(kept_route, route_rows, expert_count)
    target_slot = jnp.where(kept_route, route_rank, 0)
    token_ids = jnp.broadcast_to(positions[:, None], route_rows.shape)
    source = (
        jnp.full((expert_count, capacity), row_count, jnp.int32)
        .at[target_expert, target_slot]
        .set(token_ids, mode="drop")
    )
    padded_in = jnp.concatenate([ffn_low, jnp.zeros((1, D), jnp.bfloat16)], axis=0)
    send_rows = padded_in[source].reshape(owners, local_experts, capacity, D)
    expert_weights = (w_gate, w_up, w_down)
    gathered = lax.all_gather(
        lax.all_to_all(send_rows, "expert", split_axis=0, concat_axis=0, tiled=True),
        "dp",
        axis=0,
        tiled=True,
    )
    gate_pre, up_pre, hidden_low, partial_out = expert_forward(gathered, w_gate, w_up, w_down)
    summed = lax.psum_scatter(
        partial_out.astype(jnp.bfloat16), "dp", scatter_dimension=0, tiled=True
    )
    expert_out, expert_rows, gate_pre, up_pre, hidden_low = (
        summed,
        gathered,
        gate_pre,
        up_pre,
        hidden_low,
    )
    returned = lax.all_to_all(
        expert_out, "expert", split_axis=0, concat_axis=0, tiled=True
    ).reshape(expert_count * capacity, D)
    flat_index = jnp.where(kept_route, route_rows * capacity + route_rank, 0)
    picked = returned[flat_index]
    route_prob = jnp.sum(router_probs[:, None, :] * route_hot.astype(jnp.float32), axis=-1)
    combine_weight = jnp.where(kept_route, route_prob, 0.0)
    mixture = jnp.sum(combine_weight[:, :, None] * picked, axis=1)
    layer = live_float * (hidden_state + mixture)
    result = layer.astype(jnp.bfloat16)[None]
    qkv_back, out_back, router_back = (
        lax.all_gather(w_qkv, ("dp", "expert"), axis=0, tiled=True),
        lax.all_gather(w_out, ("dp", "expert"), axis=0, tiled=True),
        lax.all_gather(w_router, ("dp", "expert"), axis=0, tiled=True),
    )
    grad_layer = cotangent[0].astype(jnp.float32) * live_float
    dot_route = jnp.sum(grad_layer[:, None, :] * picked, axis=-1)
    balance_coef = BALANCE_WEIGHT * balance_factor
    grad_probs = jnp.sum(
        jnp.where(kept_route, dot_route, 0.0)[:, :, None] * route_hot.astype(jnp.float32), axis=1
    )
    grad_probs = grad_probs + balance_coef * count_total[None, :] * live_float
    grad_logits = router_probs * (
        grad_probs - jnp.sum(router_probs * grad_probs, axis=-1, keepdims=True)
    )
    grad_logits_low = grad_logits.astype(jnp.bfloat16)
    route_scale = (
        jnp.zeros((expert_count, capacity), jnp.float32)
        .at[target_expert, target_slot]
        .set(combine_weight, mode="drop")
    )
    padded_grad = jnp.concatenate([grad_layer, jnp.zeros((1, D), jnp.float32)], axis=0)
    grad_send = (
        (padded_grad[source] * route_scale[:, :, None])
        .astype(jnp.bfloat16)
        .reshape(owners, local_experts, capacity, D)
    )
    arrived = lax.all_to_all(grad_send, "expert", split_axis=0, concat_axis=0, tiled=True)
    grad_rows_all = lax.all_gather(arrived, "dp", axis=0, tiled=True)
    gate_weight, up_weight, down_weight = expert_weights
    grad_down_w = jnp.einsum(
        "nkcf,nkcd->kfd", hidden_low, grad_rows_all, preferred_element_type=jnp.float32
    )
    grad_units = jnp.einsum(
        "nkcd,kfd->nkcf", grad_rows_all, down_weight, preferred_element_type=jnp.float32
    )
    gate_sigmoid = jax.nn.sigmoid(gate_pre)
    grad_gate_low = (
        grad_units * up_pre * gate_sigmoid * (1.0 + gate_pre * (1.0 - gate_sigmoid))
    ).astype(jnp.bfloat16)
    grad_up_low = (grad_units * gate_pre * gate_sigmoid).astype(jnp.bfloat16)
    grad_gate_w = jnp.einsum(
        "nkcd,nkcf->kdf", expert_rows, grad_gate_low, preferred_element_type=jnp.float32
    )
    grad_up_w = jnp.einsum(
        "nkcd,nkcf->kdf", expert_rows, grad_up_low, preferred_element_type=jnp.float32
    )
    back_part = jnp.einsum(
        "nkcf,kdf->nkcd", grad_gate_low, gate_weight, preferred_element_type=jnp.float32
    )
    back_part = back_part + jnp.einsum(
        "nkcf,kdf->nkcd", grad_up_low, up_weight, preferred_element_type=jnp.float32
    )
    back_rows = lax.psum_scatter(
        back_part.astype(jnp.bfloat16), "dp", scatter_dimension=0, tiled=True
    )
    expert_grads = (grad_gate_w, grad_up_w, grad_down_w)
    sent_back = lax.all_to_all(
        back_rows, "expert", split_axis=0, concat_axis=0, tiled=True
    ).reshape(expert_count * capacity, D)
    grad_ffn = jnp.einsum(
        "tj,tjd->td",
        kept_route.astype(jnp.bfloat16),
        sent_back[flat_index],
        preferred_element_type=jnp.float32,
    )
    grad_ffn = grad_ffn + jnp.einsum(
        "te,de->td", grad_logits_low, router_back, preferred_element_type=jnp.float32
    )
    grad_router_w = jnp.einsum(
        "td,te->de", ffn_low, grad_logits_low, preferred_element_type=jnp.float32
    )
    grad_hidden_part, grad_gain_ffn = ffn_norm_back(grad_ffn)
    grad_hidden_state = grad_layer + grad_hidden_part
    grad_attn_low = grad_hidden_state.astype(jnp.bfloat16)
    grad_out_w = jnp.einsum(
        "td,te->de", mixed_low, grad_attn_low, preferred_element_type=jnp.float32
    )
    grad_mixed = jnp.einsum(
        "te,de->td", grad_attn_low, out_back, preferred_element_type=jnp.float32
    )
    grad_mixed = grad_mixed.astype(jnp.bfloat16).reshape(row_count, HEADS, HEAD)
    scores_again = (
        jnp.einsum("qhd,khd->hqk", queries, keys_low, preferred_element_type=jnp.float32)
        * score_scale
    )
    probs_again = jnp.where(allowed[None], jnp.exp(scores_again - log_total), 0.0)
    grad_values = jnp.einsum(
        "hqk,qhd->khd",
        probs_again.astype(jnp.bfloat16),
        grad_mixed,
        preferred_element_type=jnp.float32,
    )
    grad_attn_probs = jnp.einsum(
        "qhd,khd->hqk", grad_mixed, values_low, preferred_element_type=jnp.float32
    )
    grad_scores = probs_again * (
        grad_attn_probs - jnp.sum(probs_again * grad_attn_probs, axis=-1, keepdims=True)
    )
    grad_scores_low = grad_scores.astype(jnp.bfloat16)
    grad_queries = (
        jnp.einsum("hqk,khd->qhd", grad_scores_low, keys_low, preferred_element_type=jnp.float32)
        * score_scale
    )
    grad_keys = (
        jnp.einsum("hqk,qhd->khd", grad_scores_low, queries, preferred_element_type=jnp.float32)
        * score_scale
    )
    grad_query_part, grad_key_part, grad_gain_query, grad_gain_key = query_key_back(
        (grad_queries, grad_keys)
    )
    grad_projected = jnp.concatenate(
        [grad_query_part, grad_key_part, grad_values.reshape(row_count, D)], axis=1
    ).astype(jnp.bfloat16)
    grad_qkv_w = jnp.einsum("td,te->de", normed, grad_projected, preferred_element_type=jnp.float32)
    grad_normed = jnp.einsum(
        "te,de->td", grad_projected, qkv_back, preferred_element_type=jnp.float32
    )
    grad_input_part, grad_gain_attn = attn_norm_back(grad_normed)
    grad_inputs = grad_hidden_state + grad_input_part
    grad_gain_rows = jnp.stack([grad_gain_attn, grad_gain_query, grad_gain_key, grad_gain_ffn])
    mixer_grads = (
        lax.psum_scatter(grad_qkv_w, ("dp", "expert"), scatter_dimension=0, tiled=True),
        lax.psum_scatter(grad_out_w, ("dp", "expert"), scatter_dimension=0, tiled=True),
        lax.psum_scatter(grad_router_w, ("dp", "expert"), scatter_dimension=0, tiled=True),
        lax.psum_scatter(grad_gain_rows, ("dp", "expert"), scatter_dimension=1, tiled=True),
    )
    return (
        result,
        grad_inputs[None],
        mixer_grads[0],
        mixer_grads[1],
        mixer_grads[2],
        mixer_grads[3],
        expert_grads[0],
        expert_grads[1],
        expert_grads[2],
        balance,
    )


def solution(mesh):
    placed = (
        P(("dp", "expert"), None, None),
        P(("dp", "expert"), None),
        P(("dp", "expert"), None),
        P(("dp", "expert"), None),
        P(None, ("dp", "expert")),
        P("expert", None, "dp"),
        P("expert", None, "dp"),
        P("expert", "dp", None),
        P(("dp", "expert")),
        P(("dp", "expert"), None, None),
        P(("dp", "expert"), None),
        P(("dp", "expert"), None, None),
    )
    return jax.shard_map(
        body,
        mesh=mesh,
        in_specs=placed,
        out_specs=(
            P(("dp", "expert"), None, None),
            P(("dp", "expert"), None, None),
            P(("dp", "expert"), None),
            P(("dp", "expert"), None),
            P(("dp", "expert"), None),
            P(None, ("dp", "expert")),
            P("expert", None, "dp"),
            P("expert", None, "dp"),
            P("expert", "dp", None),
            P(),
        ),
        check_vma=False,
    )
```

profile of v0, /device:TPU:8, one launch (start us, length us, event | category | flops | bytes accessed | tf_op | source)
XLA Modules:
  0.0 2461.3 jit_solution(9017728123629658557)
XLA Ops:
  10.9 64.6 %all-gather = bf16[32,64,4]{1,2,0:T(4,128)(2,1)S(1)} all-gather(bf16[1,64,4]{1,2,0:T(4,128)(2,1)} %bitcast.356), channel_id=1, replica_groups=mesh['dp'=2,'expert'=16] {'dp','expert'}, dimensions={0}, use_global_device_ids=true | all-gather | bytes 16896 | tf_op jit(solution)/shard_map/all_gather | solution.py:90
  92.0 73.2 %all-gather.7.cloned.1.call-done = bf16[2048,6144]{1,0:T(8,128)(2,1)} async-done(((bf16[64,6144]{1,0:T(8,128)(2,1)}), bf16[2048,6144]{1,0:T(8,128)(2,1)}) %all-gather.7.cloned.1.call-update) | async-done | bytes 25165840 | tf_op jit(solution)/shard_map/all_gather | solution.py:87
  165.2 11.7 fusion.101
  198.5 47.3 %all-gather.9.cloned.1.call-done = bf16[2048,2048]{1,0:T(8,128)(2,1)} async-done(((bf16[64,2048]{1,0:T(8,128)(2,1)}), bf16[2048,2048]{1,0:T(8,128)(2,1)}) %all-gather.9.cloned.1.call-update) | async-done | bytes 8388624 | tf_op jit(solution)/shard_map/all_gather | solution.py:88
  254.6 11.0 gather_fusion
  271.1 236.3 %all-gather.1 = bf16[32,64,16]{1,2,0:T(8,128)(2,1)S(1)} all-gather(bf16[1,64,16]{1,2,0:T(8,128)(2,1)S(1)} %bitcast.355), channel_id=1, replica_groups=mesh['dp'=2,'expert'=16] {'dp','expert'}, dimensions={0}, use_global_device_ids=true | all-gather | bytes 67584 | tf_op jit(solution)/shard_map/all_gather | solution.py:89
  511.3 18.2 gather_fusion.2
  546.8 188.5 %all_to_all.20 = bf16[16,1,128,2048]{3,2,1,0:T(8,128)(2,1)} all-to-all(bf16[16,1,128,2048]{3,2,1,0:T(8,128)(2,1)S(1)} %multiply_convert_fusion), channel_id=1, replica_groups=mesh['dp'=2,'expert'=16] {'expert'}, dimensions={0} | all-to-all | bytes 16777216 | tf_op jit(solution)/shard_map/all_to_all | solution.py:204
  735.4 15.5 fusion.10
  755.2 11.1 fusion.12
  766.3 24.1 fusion.21
  790.4 14.7 convert_bitcast_fusion
  806.6 24.6 %fusion.30 = f32[32,128,2048]{2,1,0:T(8,128)} fusion(bf16[32,1,128,512]{3,2,0,1:T(8,128)(2,1)} %get-tuple-element.33, bf16[1,2048,512]{2,1,0:T(8,128)(2,1)S(1)} %copy-done.87), kind=kOutput, calls=%fused_computation.47 | convolution fusion | flops 8589934592 | bytes 39845888 | tf_op jit(solution)/shard_map/nkcf,kdf->nkcd/dot_general | solution.py:224
  831.3 22.7 fusion.14
  860.1 20.7 reduce-scatter.13.cloned.1.call-done
  880.8 160.5 %all-to-all-done.1 = bf16[16,1,128,2048]{3,2,1,0:T(8,128)(2,1)} async-done(((bf16[16,1,128,2048]{3,2,1,0:T(8,128)(2,1)}), bf16[16,1,128,2048]{3,2,1,0:T(8,128)(2,1)}, u32[]{:S(2)}, u32[]{:S(2)}) %all-to-all-start.1) | async-done | bytes 8388640 | tf_op jit(solution)/shard_map/all_to_all | solution.py:167
  1041.3 16.0 all-to-all-start.3
  1057.3 206.6 %psum.14 = f32[16]{0:T(128)S(1)} all-reduce(f32[16]{0:T(128)S(1)} %copy-done.88), channel_id=1, replica_groups=mesh['dp'=2,'expert'=16] {'dp','expert'}, use_global_device_ids=true, to_apply=%region_21.22 | all-reduce | flops 16 | bytes 128 | tf_op jit(solution)/shard_map/psum | solution.py:128
  1264.6 20.9 gather_fusion.1
  1285.6 9.5 fusion.1
  1296.0 21.2 gather_fusion.3
  1363.7 14.4 fusion.56
  1382.7 9.4 fusion.97
  1393.6 20.8 fusion.88
  1414.5 15.1 fusion.44
  1429.6 14.0 fusion.39
  1443.7 10.6 fusion.34
  1454.4 42.2 %psum.15 = f32[16]{0:T(128)S(1)} all-reduce(f32[16]{0:T(128)S(1)} %copy-done.84), channel_id=1, replica_groups=mesh['dp'=2,'expert'=16] {'dp','expert'}, use_global_device_ids=true, to_apply=%region_37.38 | all-reduce | flops 16 | bytes 128 | tf_op jit(solution)/shard_map/psum | solution.py:128
  1502.1 13.2 reduce-scatter.21.cloned.1.call-done
  1516.7 135.8 %reduce-scatter.19.cloned.1.call-done = f32[64,16]{1,0:T(8,128)} async-done(((f32[2048,16]{1,0:T(8,128)}), f32[64,16]{1,0:T(8,128)}) %reduce-scatter.19.cloned.1.call-update) | async-done | bytes 4112
  1653.9 360.9 %reduce-scatter.17.cloned.1.call-done = f32[64,2048]{1,0:T(8,128)} async-done(((f32[2048,2048]{1,0:T(8,128)}), f32[64,2048]{1,0:T(8,128)}) %reduce-scatter.17.cloned.1.call-update) | async-done | bytes 524304 | tf_op jit(solution)/shard_map/reduce_scatter | solution.py:300
  2014.8 438.1 %reduce-scatter.15.cloned.1.call-done = f32[64,6144]{1,0:T(8,128)} async-done(((f32[2048,6144]{1,0:T(8,128)}), f32[64,6144]{1,0:T(8,128)}) %reduce-scatter.15.cloned.1.call-update) | async-done | bytes 1572880 | tf_op jit(solution)/shard_map/reduce_scatter | solution.py:299
  (326 shorter events, 149.4 us)
Async XLA Ops:
  7.2 759.1 %copy-start = (bf16[1,512,2048]{2,1,0:T(8,128)(2,1)S(1)}, bf16[1,512,2048]{2,1,0:T(8,128)(2,1)}, u32[]{:S(2)}) copy-start(bf16[1,512,2048]{2,1,0:T(8,128)(2,1)} %param.19) | copy-start | bytes 6291460
  7.2 83.7 %copy-start.14 = (bf16[1,256,2048]{2,1,0:T(8,128)(2,1)S(1)}, bf16[1,256,2048]{2,1,0:T(8,128)(2,1)}, u32[]{:S(2)}) copy-start(bf16[1,256,2048]{2,1,0:T(8,128)(2,1)} %param.12) | copy-start | bytes 3145732
  7.2 158.0 %all-gather.7.cloned.1.call-start = ((), (), s32[]{:S(2)}) async-start(), calls=%async_computation.10 | async-start | bytes 25952256 | tf_op jit(solution)/shard_map/all_gather | solution.py:87
  7.9 237.8 %all-gather.9.cloned.1.call-start = ((), (), s32[]{:S(2)}) async-start(), calls=%async_computation.11 | async-start | bytes 8650752 | tf_op jit(solution)/shard_map/all_gather | solution.py:88
  9.3 82.6 %copy-start.71 = (pred[256]{0:T(512)(128)(4,1)}, pred[256]{0:T(512)(128)(4,1)S(1)}, u32[]{:S(2)}) copy-start(pred[256]{0:T(512)(128)(4,1)S(1)} %iota_compare_fusion.2) | copy-start | bytes 772
  91.9 101.5 %copy-start.30 = (pred[256,256]{0,1:T(8,128)(4,1)}, pred[256,256]{0,1:T(8,128)(4,1)S(1)}, u32[]{:S(2)}) copy-start(pred[256,256]{0,1:T(8,128)(4,1)S(1)} %fusion.103) | copy-start | bytes 196612
  92.0 85.0 %copy-start.36 = (f32[1,2048]{1,0:T(1,128)}, f32[1,2048]{1,0:T(1,128)S(1)}, u32[]{:S(2)}) copy-start(f32[1,2048]{1,0:T(1,128)S(1)} %get-tuple-element.62) | copy-start | bytes 24580
  92.0 85.4 %copy-start.46 = (f32[1,2048]{1,0:T(1,128)}, f32[1,2048]{1,0:T(1,128)S(1)}, u32[]{:S(2)}) copy-start(f32[1,2048]{1,0:T(1,128)S(1)} %get-tuple-element.60) | copy-start | bytes 24580
  92.0 85.4 %copy-start.48 = (f32[1,2048]{1,0:T(1,128)}, f32[1,2048]{1,0:T(1,128)S(1)}, u32[]{:S(2)}) copy-start(f32[1,2048]{1,0:T(1,128)S(1)} %get-tuple-element.61) | copy-start | bytes 24580
  92.0 160.0 %copy-start.50 = (f32[1,2048]{1,0:T(1,128)}, f32[1,2048]{1,0:T(1,128)S(1)}, u32[]{:S(2)}) copy-start(f32[1,2048]{1,0:T(1,128)S(1)} %get-tuple-element.59) | copy-start | bytes 24580
  265.6 242.1 %copy-start.28 = (bf16[1,256,2048]{2,1,0:T(8,128)(2,1)S(1)}, bf16[1,256,2048]{2,1,0:T(8,128)(2,1)}, u32[]{:S(2)}) copy-start(bf16[1,256,2048]{2,1,0:T(8,128)(2,1)} %param.23) | copy-start | bytes 3145732
  265.6 274.5 %all-to-all-start = ((bf16[16,1,128,2048]{3,2,1,0:T(8,128)(2,1)}), bf16[16,1,128,2048]{3,2,1,0:T(8,128)(2,1)}, u32[]{:S(2)}, u32[]{:S(2)}) async-start(bf16[16,1,128,2048]{3,2,1,0:T(8,128)(2,1)} %bitcast.313), calls=%async_computation | async-start | bytes 16777216 | tf_op jit(solution)/shard_map/all_to_all | solution.py:151
  271.1 464.3 %all-gather.11.cloned.1.call-start = ((), (), s32[]{:S(2)}) async-start(), calls=%async_computation.12 | async-start | bytes 25165824 | tf_op jit(solution)/shard_map/all_gather | solution.py:150
  540.2 226.1 %all-gather.13.cloned.1.call-start = ((), (), s32[]{:S(2)}) async-start(), calls=%async_computation.14 | async-start | bytes 25165824 | tf_op jit(solution)/shard_map/all_gather | solution.py:205
  735.3 118.7 %reduce-scatter.11.cloned.1.call-start = ((), (), s32[]{:S(2)}) async-start(), calls=%async_computation.13 | async-start | bytes 25165824 | tf_op jit(solution)/shard_map/reduce_scatter | solution.py:157
  805.1 75.7 %reduce-scatter.13.cloned.1.call-start = ((), (), s32[]{:S(2)}) async-start(), calls=%async_computation.15 | async-start | bytes 25165824 | tf_op jit(solution)/shard_map/reduce_scatter | solution.py:230
  854.0 187.2 %all-to-all-start.1 = ((bf16[16,1,128,2048]{3,2,1,0:T(8,128)(2,1)}), bf16[16,1,128,2048]{3,2,1,0:T(8,128)(2,1)}, u32[]{:S(2)}, u32[]{:S(2)}) async-start(bf16[16,1,128,2048]{3,2,1,0:T(8,128)(2,1)} %bitcast.323), calls=%async_computation.2 | async-start | bytes 16777216 | tf_op jit(solution)/shard_map/all_to_all | solution.py:167
  1041.3 222.7 %copy-start.57 = (s32[256,8,1]{0,1,2:T(8,128)S(1)}, s32[256,8,1]{0,1,2:T(8,128)}, u32[]{:S(2)}) copy-start(s32[256,8,1]{0,1,2:T(8,128)} %get-tuple-element.30) | copy-start | bytes 24580
  1041.3 223.0 %copy-start.60 = (pred[256,8]{0,1:T(8,128)(4,1)S(1)}, pred[256,8]{0,1:T(8,128)(4,1)}, u32[]{:S(2)}) copy-start(pred[256,8]{0,1:T(8,128)(4,1)} %get-tuple-element.29) | copy-start | bytes 6148
  1041.3 223.3 %copy-start.45 = (f32[16,256]{1,0:T(8,128)S(1)}, f32[16,256]{1,0:T(8,128)}, u32[]{:S(2)}) copy-start(f32[16,256]{1,0:T(8,128)} %copy-done.44) | copy-start | bytes 49156
  1041.3 223.3 %copy-start.56 = (f32[16,256]{1,0:T(8,128)S(1)}, f32[16,256]{1,0:T(8,128)}, u32[]{:S(2)}) copy-start(f32[16,256]{1,0:T(8,128)} %copy-done.55) | copy-start | bytes 49156
  1041.3 254.7 %all-to-all-start.3 = ((bf16[16,1,128,2048]{3,2,1,0:T(8,128)(2,1)}), bf16[16,1,128,2048]{3,2,1,0:T(8,128)(2,1)}, u32[]{:S(2)}, u32[]{:S(2)}) async-start(bf16[16,1,128,2048]{3,2,1,0:T(8,128)(2,1)} %bitcast.322), calls=%async_computation.5 | async-start | bytes 16777216 | tf_op jit(solution)/shard_map/all_to_all | solution.py:234
  1057.3 458.0 %reduce-scatter.21.cloned.1.call-start = ((), (), s32[]{:S(2)}) async-start(), calls=%async_computation.19 | async-start | bytes 1081344
  1379.5 273.0 %reduce-scatter.19.cloned.1.call-start = ((), (), s32[]{:S(2)}) async-start(), calls=%async_computation.18 | async-start | bytes 1081344
  1382.4 632.3 %reduce-scatter.17.cloned.1.call-start = ((), (), s32[]{:S(2)}) async-start(), calls=%async_computation.17 | async-start | bytes 17301504 | tf_op jit(solution)/shard_map/reduce_scatter | solution.py:300
  1392.1 1060.7 %reduce-scatter.15.cloned.1.call-start = ((), (), s32[]{:S(2)}) async-start(), calls=%async_computation.16 | async-start | bytes 51904512 | tf_op jit(solution)/shard_map/reduce_scatter | solution.py:299
  1414.5 29.2 %slice-start.2 = ((s8[16777216]{0:T(1024)(128)(4,1)}), s8[4194304]{0:T(1024)(128)(4,1)S(1)}, s32[]{:S(2)}) async-start(s8[16777216]{0:T(1024)(128)(4,1)} %bitcast.357), calls=%async_computation.22 | async-start | bytes 8388608
  1414.5 29.2 %slice-start.3 = ((s8[16777216]{0:T(1024)(128)(4,1)}), s8[4194304]{0:T(1024)(128)(4,1)S(1)}, s32[]{:S(2)}) async-start(s8[16777216]{0:T(1024)(128)(4,1)} %bitcast.357), calls=%async_computation.23 | async-start | bytes 8388608
  1414.5 29.2 %slice-start.4 = ((s8[16777216]{0:T(1024)(128)(4,1)}), s8[4194304]{0:T(1024)(128)(4,1)S(1)}, s32[]{:S(2)}) async-start(s8[16777216]{0:T(1024)(128)(4,1)} %bitcast.357), calls=%async_computation.24 | async-start | bytes 8388608
  1443.7 52.8 %copy-start.90 = (f32[16]{0:T(128)S(1)}, f32[16]{0:T(128)}, u32[]{:S(2)}) copy-start(f32[16]{0:T(128)} %copy-done.89) | copy-start | bytes 196
  1443.7 54.1 %copy-start.75 = (f32[256]{0:T(256)S(1)}, f32[256]{0:T(256)}, u32[]{:S(2)}) copy-start(f32[256]{0:T(256)} %copy-done.74) | copy-start | bytes 3076
  1497.8 955.1 %copy-start.1 = (bf16[1,512,2048]{2,1,0:T(8,128)(2,1)S(1)}, bf16[1,512,2048]{2,1,0:T(8,128)(2,1)}, u32[]{:S(2)}) copy-start(bf16[1,512,2048]{2,1,0:T(8,128)(2,1)} %param.19) | copy-start | bytes 6291460
  (80 other events, 508.6 us)
Sparse Core Ops, SparseCore 0:
  10.9 154.2 all-gather.6
  168.1 77.5 all-gather.8
  540.3 31.9 all-gather.10
  735.4 29.2 all-gather.12
  805.2 25.8 reduce-scatter.10
  854.1 26.5 reduce-scatter.12
  1379.6 135.6 reduce-scatter.20
  1517.6 134.8 reduce-scatter.18
  1655.4 359.3 reduce-scatter.16
  2021.6 431.1 reduce-scatter.14
where the time goes:
time: 2480 us; the launch traced here: 2460 us
  waiting for transfers between devices  1250 us (50%)
  blocking collectives  738 us (30%)
  matrix products  242 us (10%)
  local copies, waits for them, and re-layouts  127 us (5%)
  other arithmetic  56.1 us (2%)
  starting transfers between devices  28.1 us (1%)
    reduce_scatter x1, waiting for transfers between devices, body(): lax.psum_scatter(grad_qkv_w, ('dp', 'expert'), scatter_dimension=0, tiled...  438 us
    reduce_scatter x1, waiting for transfers between devices, body(): lax.psum_scatter(grad_out_w, ('dp', 'expert'), scatter_dimension=0, tiled...  361 us
    psum x2, blocking collectives, body(): lax.psum((count_float, prob_local), ('dp', 'expert'))  249 us
    all_gather x1, blocking collectives, body(): lax.all_gather(w_router, ('dp', 'expert'), axis=0, tiled=True)  236 us
    all_to_all x1, blocking collectives, body(): lax.all_to_all(grad_send, 'expert', split_axis=0, concat_axis=0, tiled=True)  189 us
    all_to_all x1, waiting for transfers between devices, body(): lax.all_to_all(expert_out, 'expert', split_axis=0, concat_axis=0, tiled=T...  161 us
    unnamed x12, waiting for transfers between devices  151 us
    all_gather x1, waiting for transfers between devices, body(): lax.all_gather(w_qkv, ('dp', 'expert'), axis=0, tiled=True)  73.2 us
  transfers between devices with their start and end apart: 13, of which 8 were waited for; matrix products, arithmetic and copies ran while one was open for 11% of the time, Pallas kernels for 0%

commit v1 on v0

--- a/solution.py
+++ b/solution.py
@@ -1,8 +1,12 @@
+import functools
+import itertools
 import math
 
 import jax
 import jax.numpy as jnp
 from jax import lax
+from jax.experimental import pallas as pl
+from jax.experimental.pallas import tpu as pltpu
 from jax.sharding import PartitionSpec as P
 
 D = 2048
@@ -56,7 +60,7 @@
     return (gate_pre, up_pre, hidden_low, output)
 
 
-def body(
+def routed_body(
     tokens,
     w_qkv,
     w_out,
@@ -315,7 +319,615 @@
     )
 
 
+MESH = pl.DeviceIdType.MESH
+
+
+class Grid:
+    def __init__(self, dims, cores=False):
+        self.cores = cores
+        self.dims = ((2,) if cores else ()) + tuple(dims)
+        self.size = math.prod(self.dims)
+        self.strides = [math.prod(self.dims[d + 1 :]) for d in range(len(self.dims))]
+        self.lanes = {}
+        for d in range(len(self.dims)):
+            for side in self.sides(d):
+                self.lanes[(d, side)] = len(self.lanes)
+
+    def coords(self):
+        expert = lax.axis_index("expert")
+        c = [lax.axis_index("dp")] if self.cores else []
+        first = len(c)
+        for d in range(first, len(self.dims)):
+            c.append(lax.rem(expert // self.strides[d], self.dims[d]))
+        return c
+
+    def rels(self, d):
+        n = self.dims[d]
+        if n == 1:
+            return []
+        if n == 2:
+            return [(1, 0)]
+        return [(k, side) for k in range(1, n) for side in (-1, 1)]
+
+    def sides(self, d):
+        n = self.dims[d]
+        return [] if n == 1 else [0] if n == 2 else [-1, 1]
+
+    def at(self, c, d, rel):
+        k, side = rel
+        return 1 - c[d] if side == 0 else c[d] + side * k
+
+    def valid(self, c, d, rel):
+        k, side = rel
+        if side == 0:
+            return None
+        return c[d] - k >= 0 if side < 0 else c[d] + k < self.dims[d]
+
+    def index(self, coords):
+        return sum(x * s for x, s in zip(coords, self.strides))
+
+    def neighbor(self, c, d, side):
+        other = list(c)
+        other[d] = self.at(c, d, (1, side))
+        ok = self.valid(c, d, (1, side))
+        if self.cores and d == 0:
+            return {"dp": other[0]}, ok
+        first = 1 if self.cores else 0
+        expert = sum(x * s for x, s in zip(other[first:], self.strides[first:]))
+        return {"expert": expert}, ok
+
+    def events(self, order):
+        return [
+            dict(zip(order, combo))
+            for combo in itertools.product(*[[None] + self.rels(d) for d in order])
+        ]
+
+    def place(self, c, order, event):
+        pred, o, last = None, list(c), -1
+        for i, d in enumerate(order):
+            if event[d]:
+                pred = both(pred, self.valid(c, d, event[d]))
+                o[d] = self.at(c, d, event[d])
+                last = i
+        return o, pred, last
+
+
+def both(a, b):
+    if a is None:
+        return b
+    if b is None:
+        return a
+    return jnp.logical_and(a, b)
+
+
+def when(pred, f):
+    if pred is None:
+        f()
+    else:
+        pl.when(pred)(f)
+
+
+def greet(grid, c):
+    barrier = pltpu.get_barrier_semaphore()
+    total = jnp.int32(0)
+    for d, side in grid.lanes:
+        device, ok = grid.neighbor(c, d, side)
+        when(
+            ok,
+            lambda device=device: pl.semaphore_signal(
+                barrier, inc=1, device_id=device, device_id_type=MESH
+            ),
+        )
+        total = total + (1 if ok is None else ok.astype(jnp.int32))
+    pl.semaphore_wait(barrier, total)
+
+
+def hops(event):
+    return sum(r[0] for r in event.values() if r)
+
+
+def gather_kernel(grid, parts, count, *refs):
+    srcs, outs = refs[:count], refs[count : 2 * count]
+    send_sem, recv_sem, own_sem = refs[2 * count :]
+    c = grid.coords()
+    me = grid.index(c)
+    own = [pltpu.make_async_copy(s, o.at[me], own_sem.at[i]) for i, (s, o) in enumerate(zip(srcs, outs))]
+    for copy in own:
+        copy.start()
+    greet(grid, c)
+    sent = []
+
+    def piece(p, ref):
+        _, row0, rows, _ = parts[p]
+        return ref.at[pl.ds(row0, rows)]
+
+    def push(p, origin, source, d, side, pred):
+        device, ok = grid.neighbor(c, d, side)
+        pred = both(pred, ok)
+        copy = pltpu.make_async_remote_copy(
+            src_ref=source,
+            dst_ref=piece(p, outs[parts[p][0]].at[origin]),
+            send_sem=send_sem.at[p, origin, grid.lanes[(d, side)]],
+            recv_sem=recv_sem.at[p, origin],
+            device_id=device,
+            device_id_type=MESH,
+        )
+        when(pred, copy.start)
+        sent.append((pred, copy))
+
+    todo = []
+    for p, (_, _, _, order) in enumerate(parts):
+        for n, event in enumerate(grid.events(order)):
+            todo.append((hops(event), p if len(parts) > 8 else 0, n, p, event))
+    todo.sort(key=lambda t: t[:4])
+    for _, _, _, p, event in todo:
+        a, _, _, order = parts[p]
+        o, pred, last = grid.place(c, order, event)
+        origin = grid.index(o)
+        if last < 0:
+            source = piece(p, srcs[a])
+        else:
+            source = piece(p, outs[a].at[origin])
+            arrival = pltpu.make_async_remote_copy(
+                src_ref=source,
+                dst_ref=source,
+                send_sem=send_sem.at[p, origin, 0],
+                recv_sem=recv_sem.at[p, origin],
+                device_id={"expert": lax.axis_index("expert")},
+                device_id_type=MESH,
+            )
+            when(pred, arrival.wait_recv)
+            side = event[order[last]][1]
+            if side:
+                push(p, origin, source, order[last], -side, pred)
+        for d in order[last + 1 :]:
+            for side in grid.sides(d):
+                push(p, origin, source, d, side, pred)
+    for pred, copy in sent:
+        when(pred, copy.wait_send)
+    for copy in own:
+        copy.wait()
+
+
+def gather(arrays, grid, parts, cid):
+    n, count = grid.size, len(arrays)
+    return pl.pallas_call(
+        functools.partial(gather_kernel, grid, parts, count),
+        out_shape=[jax.ShapeDtypeStruct((n,) + x.shape, x.dtype) for x in arrays],
+        in_specs=[pl.BlockSpec(memory_space=pl.ANY)] * count,
+        out_specs=[pl.BlockSpec(memory_space=pl.ANY)] * count,
+        scratch_shapes=[
+            pltpu.SemaphoreType.DMA((len(parts), n, len(grid.lanes))),
+            pltpu.SemaphoreType.DMA((len(parts), n)),
+            pltpu.SemaphoreType.DMA((count,)),
+        ],
+        compiler_params=pltpu.CompilerParams(collective_id=cid, has_side_effects=True),
+    )(*arrays)
+
+
+def landing_slots(grid, order):
+    base, total, earlier = {}, 0, 1
+    for d in order:
+        base[d] = total
+        total += len(grid.rels(d)) * earlier
+        earlier *= grid.dims[d]
+    return base, total
+
+
+def scatter_kernel(grid, parts, count, *refs):
+    k = len(parts)
+    srcs, outs = refs[:count], refs[count : 2 * count]
+    held, mine, totals = refs[2 * count : 2 * count + k], refs[2 * count + k : 2 * count + 2 * k], refs[2 * count + 2 * k : 3 * count + 2 * k]
+    send_sem, recv_sem, mine_sem, out_sem = refs[3 * count + 2 * k :]
+    c = grid.coords()
+
+    def piece(p, ref):
+        _, row0, rows, _ = parts[p]
+        return ref.at[pl.ds(row0, rows)]
+
+    def own_slot(order, o):
+        slot = 0
+        for d in order[:-1]:
+            slot = slot * grid.dims[d] + o[d]
+        return slot
+
+    def landing(order, d, rel, o):
+        base, _ = landing_slots(grid, order)
+        slot = grid.rels(d).index(rel)
+        for q in order[: order.index(d)]:
+            slot = slot * grid.dims[q] + o[q]
+        return base[d] + slot
+
+    def own_copy(p, o):
+        a, _, _, order = parts[p]
+        slot = own_slot(order, o)
+        return pltpu.make_async_copy(
+            piece(p, srcs[a].at[grid.index(o)]), mine[p].at[slot], mine_sem.at[p, slot]
+        )
+
+    for p, (_, _, _, order) in enumerate(parts):
+        for position in itertools.product(*[range(grid.dims[d]) for d in order[:-1]]):
+            o = list(c)
+            for d, v in zip(order[:-1], position):
+                o[d] = v
+            own_copy(p, o).start()
+    greet(grid, c)
+    todo = []
+    for p, (_, _, _, order) in enumerate(parts):
+        for event in grid.events(order):
+            todo.append((tuple(-(event[d][0] if event[d] else 0) for d in reversed(order)), p, event))
+    todo.sort(key=lambda t: t[:2])
+    sent = []
+    for _, p, event in todo:
+        a, row0, rows, order = parts[p]
+        o, pred, last = grid.place(c, order, event)
+        always, sometimes = [], []
+        if last >= 0:
+            far, side = event[order[last]]
+            if side and far + 1 < grid.dims[order[last]]:
+                _, ok = grid.neighbor(c, order[last], -side)
+                sometimes.append((landing(order, order[last], (far + 1, side), o), ok))
+        for d in order[last + 1 :]:
+            for side in grid.sides(d):
+                _, ok = grid.neighbor(c, d, side)
+                slot = landing(order, d, (1, -side), o)
+                if ok is None:
+                    always.append(slot)
+                else:
+                    sometimes.append((slot, ok))
+        final = last < 0
+        if not always and not sometimes and not final:
+            source = piece(p, srcs[a].at[grid.index(o)])
+        else:
+            source = mine[p].at[own_slot(order, o)]
+            when(pred, own_copy(p, o).wait)
+            steps = [(slot, ok) for slot, ok in sometimes]
+            if always or final:
+                steps.insert(0, (always, None))
+
+            def add(slots, opening, final=final, source=source, p=p, row0=row0, rows=rows, a=a):
+                for slot in slots:
+                    landed = held[p].at[slot]
+                    pltpu.make_async_remote_copy(
+                        src_ref=landed,
+                        dst_ref=landed,
+                        send_sem=send_sem.at[p, 0],
+                        recv_sem=recv_sem.at[p, slot],
+                        device_id={"expert": lax.axis_index("expert")},
+                        device_id_type=MESH,
+                    ).wait_recv()
+                tile = min(16, rows)
+
+                @pl.loop(0, rows // tile)
+                def _(t):
+                    here = pl.ds(pl.multiple_of(t * tile, tile), tile)
+                    there = pl.ds(pl.multiple_of(row0 + t * tile, tile), tile)
+                    if final and not opening:
+                        value = totals[a][there, :]
+                    else:
+                        value = source[here, :].astype(jnp.float32)
+                    for slot in slots:
+                        value = value + held[p][slot, here, :].astype(jnp.float32)
+                    if final:
+                        totals[a][there, :] = value
+                    else:
+                        source[here, :] = value.astype(source.dtype)
+
+            for n, (slots, ok) in enumerate(steps):
+                slots = slots if isinstance(slots, list) else [slots]
+                when(both(pred, ok), functools.partial(add, slots, n == 0))
+        if last >= 0:
+            d = order[last]
+            device, _ = grid.neighbor(c, d, event[d][1])
+            slot = landing(order, d, event[d], o)
+            copy = pltpu.make_async_remote_copy(
+                src_ref=source,
+                dst_ref=held[p].at[slot],
+                send_sem=send_sem.at[p, slot],
+                recv_sem=recv_sem.at[p, slot],
+                device_id=device,
+                device_id_type=MESH,
+            )
+            when(pred, copy.start)
+            sent.append((pred, copy))
+    done = [pltpu.make_async_copy(t, o, out_sem.at[i]) for i, (t, o) in enumerate(zip(totals, outs))]
+    for copy in done:
+        copy.start()
+    for pred, copy in sent:
+        when(pred, copy.wait_send)
+    for copy in done:
+        copy.wait()
+
+
+def scatter(arrays, grid, parts, cid):
+    count = len(arrays)
+    slots = [landing_slots(grid, order)[1] for _, _, _, order in parts]
+    mine = [grid.size // grid.dims[order[-1]] for _, _, _, order in parts]
+    blocks = [((rows, arrays[a].shape[2]), arrays[a].dtype) for a, _, rows, _ in parts]
+    flat = [jax.ShapeDtypeStruct(x.shape[1:], jnp.float32) for x in arrays]
+    return pl.pallas_call(
+        functools.partial(scatter_kernel, grid, parts, count),
+        out_shape=flat,
+        in_specs=[pl.BlockSpec(memory_space=pl.ANY)] * count,
+        out_specs=[pl.BlockSpec(memory_space=pl.ANY)] * count,
+        scratch_shapes=[pltpu.VMEM((s,) + b, t) for s, (b, t) in zip(slots, blocks)]
+        + [pltpu.VMEM((s,) + b, t) for s, (b, t) in zip(mine, blocks)]
+        + [pltpu.VMEM(x.shape, x.dtype) for x in flat]
+        + [
+            pltpu.SemaphoreType.DMA((len(parts), max(slots))),
+            pltpu.SemaphoreType.DMA((len(parts), max(slots))),
+            pltpu.SemaphoreType.DMA((len(parts), max(mine))),
+            pltpu.SemaphoreType.DMA((count,)),
+        ],
+        compiler_params=pltpu.CompilerParams(
+            collective_id=cid, has_side_effects=True, vmem_limit_bytes=60 << 20
+        ),
+    )(*arrays)
+
+
+def cut(array, rows, orders):
+    share = rows // len(orders)
+    return tuple((array, i * share, share, order) for i, order in enumerate(orders))
+
+
+def gathered_body(
+    dims,
+    tokens,
+    w_qkv,
+    w_out,
+    w_router,
+    gains,
+    w_gate,
+    w_up,
+    w_down,
+    lengths,
+    routes,
+    send_counts,
+    cotangent,
+):
+    row_count = tokens.shape[1]
+    top_count = routes.shape[2]
+    expert_count = w_router.shape[1]
+    owners = math.prod(dims)
+    weight_rows = w_qkv.shape[0]
+    capacity = row_count * top_count // expert_count
+    slots_all = row_count * 2 * owners
+    balance_factor = float(expert_count) / (float(top_count) * float(slots_all) * float(slots_all))
+    score_scale = HEAD ** (-0.5)
+    low = jnp.bfloat16
+    full = jnp.float32
+    chips = Grid(dims)
+    devices = Grid(dims, cores=True)
+    z, y, x = 0, 1, 2
+    row_orders = [(x, z, y), (y, z, x), (z, x, y), (z, y, x)]
+    wide_orders = [tuple(d + 1 for d in order) + (0,) for order in row_orders]
+    expert = lax.axis_index("expert")
+    core = lax.axis_index("dp")
+    swap = [(0, 1), (1, 0)]
+
+    small = jnp.concatenate(
+        [w_router, gains.T, jnp.zeros((weight_rows, 128 - expert_count - 4), low)], axis=1
+    )
+    qkv_all, out_all, small_all = gather(
+        [w_qkv, w_out, small],
+        devices,
+        cut(0, weight_rows, wide_orders) + cut(1, weight_rows, wide_orders[:2]) + cut(2, weight_rows, wide_orders[2:3]),
+        1,
+    )
+    qkv_weight = qkv_all.reshape(D, 3 * D)
+    out_weight = out_all.reshape(D, D)
+    small_all = small_all.reshape(D, 128)
+    router_weight = small_all[:, :expert_count]
+    gain_float = small_all[:, expert_count : expert_count + 4].T.astype(full)
+    gate_own, up_own, down_own = w_gate[0], w_up[0], w_down[0]
+    gate_far, up_far, down_far = (lax.ppermute(w, "dp", swap) for w in (gate_own, up_own, down_own))
+
+    positions = jnp.arange(row_count, dtype=jnp.int32)
+    live_slots = positions < lengths[0]
+    live_float = live_slots.astype(full)[:, None]
+    expert_ids = jnp.arange(expert_count, dtype=jnp.int32)
+    named = jnp.any(routes[0][:, :, None] == expert_ids, axis=1) & live_slots[:, None]
+    before = (positions[None, :] < positions[:, None]).astype(low)
+    rank = jnp.dot(before, named.astype(low), preferred_element_type=full)
+    limit = jnp.minimum(send_counts[0], capacity).astype(full)
+    kept = named & (rank < limit[None, :])
+    kept_rank = jnp.where(kept, rank, -1.0)
+
+    inputs = tokens[0].astype(full)
+    attn_in, attn_norm_back = jax.vjp(norm_scale, inputs, gain_float[0])
+    normed = attn_in.astype(low)
+    projected = jnp.dot(normed, qkv_weight, preferred_element_type=full)
+    (rot_query, rot_keys), query_key_back = jax.vjp(
+        query_key, projected[:, :D], projected[:, D : 2 * D], gain_float[1], gain_float[2]
+    )
+    queries = rot_query.astype(low)
+    keys_low = rot_keys.astype(low)
+    values_low = projected[:, 2 * D :].astype(low).reshape(row_count, HEADS, HEAD)
+    allowed = (positions[None, :] <= positions[:, None]) & live_slots[None, :]
+    scores = jnp.einsum("qhd,khd->hqk", queries, keys_low, preferred_element_type=full) * score_scale
+    scores = jnp.where(allowed[None], scores, -1e30)
+    highest = jnp.max(scores, axis=-1, keepdims=True)
+    expo_scores = jnp.exp(scores - highest)
+    totals = jnp.sum(expo_scores, axis=-1, keepdims=True)
+    attn_probs = expo_scores / totals
+    log_total = highest + jnp.log(totals)
+    mixed_heads = jnp.einsum("hqk,khd->qhd", attn_probs.astype(low), values_low, preferred_element_type=full)
+    mixed_low = mixed_heads.reshape(row_count, D).astype(low)
+    hidden_state = inputs + jnp.dot(mixed_low, out_weight, preferred_element_type=full)
+    ffn_in, ffn_norm_back = jax.vjp(norm_scale, hidden_state, gain_float[3])
+    ffn_low = ffn_in.astype(low)
+    logits = jnp.dot(ffn_low, router_weight, preferred_element_type=full)
+    router_probs = jax.nn.softmax(logits, axis=-1)
+    prob_local = jnp.sum(router_probs * live_float, axis=0)
+    sums = jnp.concatenate([send_counts[0].astype(full), prob_local])
+    aside = jnp.concatenate(
+        [
+            jnp.where(kept, router_probs, 0.0).T,
+            kept_rank.T,
+            jnp.pad(sums[None, :], ((0, 7), (0, row_count - 2 * expert_count))),
+        ],
+        axis=0,
+    )
+
+    (cot_rows,) = gather([cotangent[0]], chips, cut(0, row_count, row_orders), 2)
+    ffn_rows, aside_rows = gather(
+        [ffn_low, aside],
+        chips,
+        cut(0, row_count, row_orders) + cut(1, aside.shape[0], row_orders[2:3]),
+        3,
+    )
+    sums_core = jnp.sum(aside_rows[:, 2 * expert_count, : 2 * expert_count], axis=0)
+    sums_all = sums_core + lax.ppermute(sums_core, "dp", swap)
+    count_total, prob_total = sums_all[:expert_count], sums_all[expert_count:]
+    balance = jnp.sum(count_total * prob_total) * balance_factor
+    weight_of = lax.dynamic_index_in_dim(aside_rows, expert, 1, keepdims=False)
+    rank_of = lax.dynamic_index_in_dim(aside_rows, expert_count + expert, 1, keepdims=False)
+    pick = rank_of[:, None, :] == jnp.arange(capacity, dtype=jnp.int32).astype(full)[None, :, None]
+    pick_low = pick.astype(low)
+    all_slots = owners * capacity
+    rows_in = jnp.einsum("rkt,rtd->rkd", pick_low, ffn_rows, preferred_element_type=full)
+    rows_in = rows_in.astype(low).reshape(all_slots, D)
+    cot_in = jnp.einsum("rkt,rtd->rkd", pick_low, cot_rows, preferred_element_type=full)
+    cot_in = cot_in.astype(low).reshape(all_slots, D)
+    slot_weight = jnp.sum(jnp.where(pick, weight_of[:, None, :], 0.0), axis=-1).reshape(all_slots, 1)
+    grad_rows = (cot_in.astype(full) * slot_weight).astype(low)
+
+    def forward(gate_weight, up_weight):
+        gate_pre = jnp.dot(rows_in, gate_weight, preferred_element_type=full)
+        up_pre = jnp.dot(rows_in, up_weight, preferred_element_type=full)
+        return gate_pre, up_pre, (jax.nn.silu(gate_pre) * up_pre).astype(low)
+
+    own, far = forward(gate_own, up_own), forward(gate_far, up_far)
+    expert_out = jnp.dot(own[2], down_own, preferred_element_type=full)
+    expert_out = (expert_out + jnp.dot(far[2], down_far, preferred_element_type=full)).astype(low)
+    dot_slot = jnp.sum(cot_in.astype(full) * expert_out.astype(full), axis=-1).reshape(owners, 1, capacity)
+    dot_route = jnp.sum(jnp.where(pick, dot_slot.reshape(owners, capacity, 1), 0.0), axis=1)
+    mixture_part = jnp.einsum(
+        "rkt,rkd->rtd", pick_low, expert_out.reshape(owners, capacity, D), preferred_element_type=full
+    )
+    mixture_part = (mixture_part * weight_of[:, :, None]).astype(low)
+
+    def backward(parts, down_weight):
+        gate_pre, up_pre, _ = parts
+        grad_units = jnp.einsum("sd,fd->sf", grad_rows, down_weight, preferred_element_type=full)
+        gate_sigmoid = jax.nn.sigmoid(gate_pre)
+        grad_gate = grad_units * up_pre * gate_sigmoid * (1.0 + gate_pre * (1.0 - gate_sigmoid))
+        return grad_gate.astype(low), (grad_units * gate_pre * gate_sigmoid).astype(low)
+
+    grad_own, grad_far = backward(own, down_own), backward(far, down_far)
+    back = jnp.einsum("sf,df->sd", grad_own[0], gate_own, preferred_element_type=full)
+    back = back + jnp.einsum("sf,df->sd", grad_own[1], up_own, preferred_element_type=full)
+    back = back + jnp.einsum("sf,df->sd", grad_far[0], gate_far, preferred_element_type=full)
+    back = back + jnp.einsum("sf,df->sd", grad_far[1], up_far, preferred_element_type=full)
+    back_part = jnp.einsum(
+        "rkt,rkd->rtd", pick_low, back.astype(low).reshape(owners, capacity, D), preferred_element_type=full
+    ).astype(low)
+    route_part = jnp.where(
+        (expert_ids == expert)[None, :, None], dot_route[:, None, :], 0.0
+    )
+
+    def outer(left, right):
+        return jnp.einsum("sa,sb->ab", left, right, preferred_element_type=full)
+
+    def weight_grads(units, grads):
+        return outer(rows_in, grads[0]), outer(rows_in, grads[1]), outer(units, grad_rows)
+
+    sent_grads = [
+        lax.ppermute(g.astype(low), "dp", swap) for g in weight_grads(far[2], grad_far)
+    ]
+    expert_grads = [
+        (a + b.astype(full))[None] for a, b in zip(weight_grads(own[2], grad_own), sent_grads)
+    ]
+    grad_ffn, grad_route = scatter(
+        [back_part, route_part],
+        chips,
+        cut(0, row_count, row_orders) + cut(1, expert_count, row_orders[2:3]),
+        4,
+    )
+    (mixture,) = scatter([mixture_part], chips, cut(0, row_count, row_orders), 5)
+    result = (live_float * (hidden_state + mixture)).astype(low)[None]
+
+    balance_coef = BALANCE_WEIGHT * balance_factor
+    grad_probs = grad_route.T + balance_coef * count_total[None, :] * live_float
+    grad_logits = router_probs * (
+        grad_probs - jnp.sum(router_probs * grad_probs, axis=-1, keepdims=True)
+    )
+    grad_logits_low = grad_logits.astype(low)
+    grad_ffn = grad_ffn + jnp.einsum("te,de->td", grad_logits_low, router_weight, preferred_element_type=full)
+    grad_router_w = jnp.einsum("td,te->de", ffn_low, grad_logits_low, preferred_element_type=full)
+
+    grad_layer = cotangent[0].astype(full) * live_float
+    grad_hidden_part, grad_gain_ffn = ffn_norm_back(grad_ffn)
+    grad_hidden_state = grad_layer + grad_hidden_part
+    grad_attn_low = grad_hidden_state.astype(low)
+    grad_mixed = jnp.einsum("te,de->td", grad_attn_low, out_weight, preferred_element_type=full)
+    grad_mixed = grad_mixed.astype(low).reshape(row_count, HEADS, HEAD)
+    scores_again = jnp.einsum("qhd,khd->hqk", queries, keys_low, preferred_element_type=full) * score_scale
+    probs_again = jnp.where(allowed[None], jnp.exp(scores_again - log_total), 0.0)
+    grad_values = jnp.einsum("hqk,qhd->khd", probs_again.astype(low), grad_mixed, preferred_element_type=full)
+    grad_attn_probs = jnp.einsum("qhd,khd->hqk", grad_mixed, values_low, preferred_element_type=full)
+    grad_scores = probs_again * (
+        grad_attn_probs - jnp.sum(probs_again * grad_attn_probs, axis=-1, keepdims=True)
+    )
+    grad_scores_low = grad_scores.astype(low)
+    grad_queries = jnp.einsum("hqk,khd->qhd", grad_scores_low, keys_low, preferred_element_type=full) * score_scale
+    grad_keys = jnp.einsum("hqk,qhd->khd", grad_scores_low, queries, preferred_element_type=full) * score_scale
+    grad_query_part, grad_key_part, grad_gain_query, grad_gain_key = query_key_back(
+        (grad_queries, grad_keys)
+    )
+    grad_projected = jnp.concatenate(
+        [grad_query_part, grad_key_part, grad_values.reshape(row_count, D)], axis=1
+    ).astype(low)
+    grad_normed = jnp.einsum("te,de->td", grad_projected, qkv_weight, preferred_element_type=full)
+    grad_input_part, grad_gain_attn = attn_norm_back(grad_normed)
+    grad_inputs = grad_hidden_state + grad_input_part
+    grad_gain_rows = jnp.stack([grad_gain_attn, grad_gain_query, grad_gain_key, grad_gain_ffn])
+
+    half = D // 2
+
+    def core_half(value, side):
+        return lax.dynamic_slice_in_dim(value, side * half, half, 1)
+
+    small_grads = jnp.concatenate(
+        [grad_router_w, grad_gain_rows.T, jnp.zeros((D, 128 - expert_count - 4), full)], axis=1
+    )
+
+    def mixer_grads(side):
+        return (
+            outer(core_half(normed, side), grad_projected),
+            outer(core_half(mixed_low, side), grad_attn_low),
+            lax.dynamic_slice_in_dim(small_grads, side * half, half, 0),
+        )
+
+    far_qkv, far_out, far_small = mixer_grads(1 - core)
+    far_parts = [
+        lax.ppermute(g, "dp", swap) for g in (far_qkv.astype(low), far_out.astype(low), far_small)
+    ]
+    shares = [
+        (a + b.astype(full)).astype(b.dtype).reshape(owners, weight_rows, a.shape[1])
+        for a, b in zip(mixer_grads(core), far_parts)
+    ]
+    grad_qkv, grad_out, grad_small = scatter(
+        shares,
+        chips,
+        cut(0, weight_rows, row_orders) + cut(1, weight_rows, row_orders) + cut(2, weight_rows, row_orders[2:3]),
+        6,
+    )
+    return (
+        result,
+        grad_inputs[None],
+        grad_qkv,
+        grad_out,
+        grad_small[:, :expert_count],
+        grad_small[:, expert_count : expert_count + 4].T,
+        *expert_grads,
+        balance,
+    )
+
+
 def solution(mesh):
+    dims = {4: (1, 2, 2), 8: (2, 2, 2), 16: (4, 2, 2)}.get(mesh.shape["expert"])
+    plan = routed_body if dims is None or mesh.shape["dp"] != 2 else functools.partial(gathered_body, dims)
     placed = (
         P(("dp", "expert"), None, None),
         P(("dp", "expert"), None),
@@ -331,7 +943,7 @@
         P(("dp", "expert"), None, None),
     )
     return jax.shard_map(
-        body,
+        plan,
         mesh=mesh,
         in_specs=placed,
         out_specs=(

time: 2480 us -> 1230 us (0.50)
  waiting for transfers between devices: 1250 us -> 0.03 us
  Pallas kernels: 0 us -> 826 us
  blocking collectives: 738 us -> 0 us
  local copies, waits for them, and re-layouts: 127 us -> 35 us
  matrix products: 242 us -> 293 us
  starting transfers between devices: 28.1 us -> 1.98 us
    pallas_call x0 -> x6, Pallas kernels: none -> 826 us  [the longest x3 420 us: gather(): pl.pallas_call(functools.partial(gather_kernel, grid, parts, count), out_...]
    reduce_scatter x4 -> x0, waiting for transfers between devices: 820 us -> none  [the longest x1 438 us: body(): lax.psum_scatter(grad_qkv_w, ('dp', 'expert'), scatter_dimension=0, tiled...]
    all_gather x2 -> x0, blocking collectives: 301 us -> none  [the longest x1 236 us: body(): lax.all_gather(w_router, ('dp', 'expert'), axis=0, tiled=True)]
    psum x2 -> x0, blocking collectives: 249 us -> none  [body(): lax.psum((count_float, prob_local), ('dp', 'expert'))]
    all_to_all x1 -> x0, blocking collectives: 189 us -> none  [body(): lax.all_to_all(grad_send, 'expert', split_axis=0, concat_axis=0, tiled=True)]
    all_to_all x3 -> x0, waiting for transfers between devices: 161 us -> none  [the longest x1 161 us: body(): lax.all_to_all(expert_out, 'expert', split_axis=0, concat_axis=0, tiled=T...]
    unnamed x12 -> x0, waiting for transfers between devices: 151 us -> none
    all_gather x4 -> x0, waiting for transfers between devices: 121 us -> none  [the longest x1 73.2 us: body(): lax.all_gather(w_qkv, ('dp', 'expert'), axis=0, tiled=True)]
  transfers between devices with their start and end apart: 13 -> 10, of which waited for: 8 -> 0; matrix products, arithmetic and copies ran while one was open for 11% -> 13% of each run, Pallas kernels for 0% -> 35%
where the time goes in v1:
time: 1230 us; the launch traced here: 1220 us
  Pallas kernels  826 us (67%)
  matrix products  293 us (24%)
  other arithmetic  56.9 us (5%)
  local copies, waits for them, and re-layouts  35 us (3%)
    pallas_call x3, Pallas kernels, gather(): pl.pallas_call(functools.partial(gather_kernel, grid, parts, count), out_...  420 us
    pallas_call x3, Pallas kernels, scatter(): pl.pallas_call(functools.partial(scatter_kernel, grid, parts, count), out...  406 us
    dot_general x10, matrix products, outer(): return jnp.einsum('sa,sb->ab', left, right, preferred_element_type=full)  69.4 us
    dot_general x2, matrix products, forward(): up_pre = jnp.dot(rows_in, up_weight, preferred_element_type=full)  25.7 us
  transfers between devices with their start and end apart: 10, of which 0 were waited for; matrix products, arithmetic and copies ran while one was open for 13% of the time, Pallas kernels for 35%

profile of v1, /device:TPU:8, one launch (start us, length us, event | category | flops | bytes accessed | tf_op | source)
XLA Modules:
  0.0 1218.0 jit_solution(2602108739303214896)
XLA Ops:
  8.7 137.1 %shard_map.195 = (bf16[32,64,6144]{2,1,0:T(8,128)(2,1)}, bf16[32,64,2048]{2,1,0:T(8,128)(2,1)}, bf16[32,64,128]{2,1,0:T(8,128)(2,1)}) custom-call(bf16[64,6144]{1,0:T(8,128)(2,1)} %refs_0_.1, bf16[64,2048]{1,0:T(8,128)(2,1)} %refs_1_.1, bf16[64,128]{1,0:T(8,128)(2,1)} %maximum_maximum_fusion.1.refs_2_), custom_call_target="tpu_custom_call" | custom-call | tf_op jit(solution)/shard_map/pallas_call | solution.py:494
  147.5 12.0 fusion.52
  185.4 144.3 %shard_map.196 = (bf16[16,256,2048]{2,1,0:T(8,128)(2,1)}, f32[16,40,256]{2,1,0:T(8,128)}) custom-call(bf16[256,2048]{1,0:T(8,128)(2,1)} %copy-done.10, f32[40,256]{1,0:T(8,128)} %select_maximum_fusion.refs_1_), custom_call_target="tpu_custom_call" | custom-call | tf_op jit(solution)/shard_map/pallas_call | solution.py:494
  331.8 139.1 %shard_map.198 = bf16[16,256,2048]{2,1,0:T(8,128)(2,1)} custom-call(bf16[256,2048]{1,0:T(8,128)(2,1)} %bitcast.259), custom_call_target="tpu_custom_call" | custom-call | tf_op jit(solution)/shard_map/pallas_call | solution.py:494
  471.9 12.0 convolution_convert_fusion.3
  483.9 9.6 fusion.109
  493.5 12.3 %multiply_convert_fusion.7 = (bf16[2048,512]{1,0:T(8,128)(2,1)S(1)}, f32[2048,512]{1,0:T(8,128)}) fusion(f32[2048,512]{1,0:T(8,128)} %fusion.109, bf16[2048,2048]{1,0:T(8,128)(2,1)} %bitcast.228, bf16[1,2048,512]{2,1,0:T(8,128)(2,1)} %param.18), kind=kOutput, calls=%fused_computation.33 | convolution fusion | flops 4301258752 | bytes 20971520 | tf_op jit(solution)/shard_map/dot_general | solution.py:797
  505.9 8.1 fusion.101
  516.4 7.8 fusion.124
  524.2 13.3 %multiply_convert_fusion.6 = (bf16[2048,512]{1,0:T(8,128)(2,1)}, f32[2048,512]{1,0:T(8,128)}) fusion(f32[2048,512]{1,0:T(8,128)S(1)} %fusion.124, bf16[2048,2048]{1,0:T(8,128)(2,1)} %bitcast.230, bf16[2048,512]{1,0:T(8,128)(2,1)} %collective-permute-done.1), kind=kOutput, calls=%fused_computation.31 | convolution fusion | flops 4301258752 | bytes 20971520 | tf_op jit(solution)/shard_map/dot_general | solution.py:797
  537.6 11.6 add_convert_fusion.2
  549.2 9.9 fusion.2
  560.9 8.8 multiply_convert_fusion.refs_0_
  569.7 141.9 %shard_map.197 = f32[256,2048]{1,0:T(8,128)} custom-call(bf16[16,256,2048]{2,1,0:T(8,128)(2,1)} %multiply_convert_fusion.refs_0_), custom_call_target="tpu_custom_call" | custom-call | tf_op jit(solution)/shard_map/pallas_call | solution.py:648
  711.6 8.1 fusion
  719.7 8.3 fusion.1
  728.0 11.1 multiply_convert_fusion.4
  739.2 8.8 fusion.107
  748.0 9.1 fusion.103
  757.2 7.6 multiply_convert_fusion.3
  764.8 11.3 fusion.125
  776.2 21.5 %add_convert_fusion.1 = bf16[2048,2048]{1,0:T(8,128)(2,1)} fusion(f32[2048,2048]{1,0:T(8,128)} %fusion.125, f32[2048,2048]{1,0:T(8,128)} %fusion.107, f32[2048,2048]{1,0:T(8,128)} %fusion.103, bf16[2048,512]{1,0:T(8,128)(2,1)S(1)} %get-tuple-element.77, bf16[2048,512]{1,0:T(8,128)(2,1)} %collective-permute-done.1), kind=kOutput, calls=%fused_computation.8 | convolution fusion | flops 4311744512 | bytes 62914560 | tf_op jit(solution)/shard_map/sf,df->sd/dot_general | solution.py:821
  797.7 11.5 convolution_convert_fusion.refs_0_
  810.1 123.6 %shard_map.199 = (f32[256,2048]{1,0:T(8,128)}, f32[16,256]{1,0:T(8,128)}) custom-call(bf16[16,256,2048]{2,1,0:T(8,128)(2,1)} %convolution_convert_fusion.refs_0_, f32[16,16,256]{2,1,0:T(8,128)} %broadcast_select_fusion.refs_1_), custom_call_target="tpu_custom_call" | custom-call | tf_op jit(solution)/shard_map/pallas_call | solution.py:648
  977.1 14.5 %fusion.19 = (f32[2048]{0:T(1024)S(1)}, f32[256]{0:T(256)S(1)}, bf16[256,2048]{1,0:T(8,128)(2,1)}, f32[256,2048]{1,0:T(8,128)}) fusion(bf16[1,256,2048]{2,1,0:T(8,128)(2,1)S(1)} %copy-done.13, f32[256]{0:T(256)S(1)} %copy-done.70, f32[2048]{0:T(1024)S(1)} %bitcast.285, bf16[2048,6144]{1,0:T(8,128)(2,1)} %bitcast.294, bf16[256,2048]{1,0:T(8,128)(2,1)} %copy.117, ...), kind=kOutput, calls=%fused_computation.62 | convolution fusion | flops 6456604672 | bytes 32524288 | tf_op jit(solution)/shard_map/te,de->td/dot_general | solution.py:881
  991.6 10.3 convolution_convert_fusion.1
  1001.9 9.6 convolution_convert_fusion.6
  1033.1 8.1 add_bitcast_fusion
  1041.2 7.4 add_bitcast_fusion.1
  1048.6 7.3 add_bitcast_fusion.2
  1059.3 10.3 add_convert_fusion
  1069.6 140.4 %shard_map.200 = (f32[64,6144]{1,0:T(8,128)}, f32[64,2048]{1,0:T(8,128)}, f32[64,128]{1,0:T(8,128)}) custom-call(bf16[16,64,6144]{2,1,0:T(8,128)(2,1)} %bitcast.217, bf16[16,64,2048]{2,1,0:T(8,128)(2,1)} %bitcast.243, f32[16,64,128]{2,1,0:T(8,128)} %bitcast.267), custom_call_target="tpu_custom_call" | custom-call | tf_op jit(solution)/shard_map/pallas_call | solution.py:648
  (325 shorter events, 116.5 us)
Async XLA Ops:
  0.6 536.9 %collective-permute-start.2 = (bf16[512,2048]{1,0:T(8,128)(2,1)}, bf16[512,2048]{1,0:T(8,128)(2,1)}, u32[]{:S(2)}, u32[]{:S(2)}) collective-permute-start(bf16[512,2048]{1,0:T(8,128)(2,1)} %bitcast.295), channel_id=1, source_target_pairs={{0,16},{16,0},{1,17},{17,1},{2,18},{18,2},{3,19},{19,3},{4,20},{20... | collective-permute-start | bytes 6291464 | tf_op jit(solution)/shard_map/ppermute | solution.py:723
  0.7 523.5 %collective-permute-start.1 = (bf16[2048,512]{1,0:T(8,128)(2,1)}, bf16[2048,512]{1,0:T(8,128)(2,1)}, u32[]{:S(2)}, u32[]{:S(2)}) collective-permute-start(bf16[2048,512]{1,0:T(8,128)(2,1)} %bitcast.297), channel_id=1, source_target_pairs={{0,16},{16,0},{1,17},{17,1},{2,18},{18,2},{3,19},{19,3},{4,20},{20... | collective-permute-start | bytes 6291464 | tf_op jit(solution)/shard_map/ppermute | solution.py:723
  1.2 515.2 %collective-permute-start = (bf16[2048,512]{1,0:T(8,128)(2,1)}, bf16[2048,512]{1,0:T(8,128)(2,1)}, u32[]{:S(2)}, u32[]{:S(2)}) collective-permute-start(bf16[2048,512]{1,0:T(8,128)(2,1)} %bitcast.296), channel_id=1, source_target_pairs={{0,16},{16,0},{1,17},{17,1},{2,18},{18,2},{3,19},{19,3},{4,20},{20... | collective-permute-start | bytes 6291464 | tf_op jit(solution)/shard_map/ppermute | solution.py:723
  3.5 144.0 %copy-start.69 = (f32[256]{0:T(256)}, f32[256]{0:T(256)S(1)}, u32[]{:S(2)}) copy-start(f32[256]{0:T(256)S(1)} %fusion.95) | copy-start | bytes 3076
  4.2 179.8 %copy-start.50 = (f32[256]{0:T(256)}, f32[256]{0:T(256)S(1)}, u32[]{:S(2)}) copy-start(f32[256]{0:T(256)S(1)} %get-tuple-element.133) | copy-start | bytes 3076
  6.7 168.0 %copy-start.32 = (pred[256,256]{0,1:T(8,128)(4,1)}, pred[256,256]{0,1:T(8,128)(4,1)S(1)}, u32[]{:S(2)}) copy-start(pred[256,256]{0,1:T(8,128)(4,1)S(1)} %fusion.82) | copy-start | bytes 196612
  6.8 140.8 %copy-start.12 = (bf16[1,256,2048]{2,1,0:T(8,128)(2,1)S(1)}, bf16[1,256,2048]{2,1,0:T(8,128)(2,1)}, u32[]{:S(2)}) copy-start(bf16[1,256,2048]{2,1,0:T(8,128)(2,1)} %param.12) | copy-start | bytes 3145732
  147.5 12.5 %copy-start.40 = (f32[1,2048]{1,0:T(1,128)}, f32[1,2048]{1,0:T(1,128)S(1)}, u32[]{:S(2)}) copy-start(f32[1,2048]{1,0:T(1,128)S(1)} %get-tuple-element.106) | copy-start | bytes 24580
  147.5 34.6 %copy-start.44 = (f32[1,2048]{1,0:T(1,128)}, f32[1,2048]{1,0:T(1,128)S(1)}, u32[]{:S(2)}) copy-start(f32[1,2048]{1,0:T(1,128)S(1)} %get-tuple-element.105) | copy-start | bytes 24580
  184.0 286.9 %copy-start.48 = (f32[256]{0:T(256)}, f32[256]{0:T(256)S(1)}, u32[]{:S(2)}) copy-start(f32[256]{0:T(256)S(1)} %get-tuple-element.119) | copy-start | bytes 3076
  184.1 286.8 %copy-start.52 = (f32[256]{0:T(256)}, f32[256]{0:T(256)S(1)}, u32[]{:S(2)}) copy-start(f32[256]{0:T(256)S(1)} %fusion.88) | copy-start | bytes 3076
  330.6 184.1 %collective-permute-start.3 = (f32[32]{0:T(128)S(1)}, f32[32]{0:T(128)S(1)}, u32[]{:S(2)}, u32[]{:S(2)}) collective-permute-start(f32[32]{0:T(128)S(1)} %slice_reduce_fusion), channel_id=1, source_target_pairs={{0,16},{16,0},{1,17},{17,1},{2,18},{18,2},{3,19},{19,3},{4,20},{20... | collective-permute-start | bytes 392 | tf_op jit(solution)/shard_map/ppermute | solution.py:780
  524.2 13.4 %copy-start.85 = (f32[2048,512]{1,0:T(8,128)}, f32[2048,512]{1,0:T(8,128)S(1)}, u32[]{:S(2)}) copy-start(f32[2048,512]{1,0:T(8,128)S(1)} %fusion.124) | copy-start | bytes 12582916
  739.2 18.0 %slice-start.2 = ((s8[8388608]{0:T(1024)(128)(4,1)}), s8[4194304]{0:T(1024)(128)(4,1)S(1)}, s32[]{:S(2)}) async-start(s8[8388608]{0:T(1024)(128)(4,1)} %bitcast.221), calls=%async_computation.2 | async-start | bytes 8388608
  810.0 123.7 %copy-start.38 = (f32[256,16]{0,1:T(8,128)S(1)}, f32[256,16]{0,1:T(8,128)}, u32[]{:S(2)}) copy-start(f32[256,16]{0,1:T(8,128)} %copy-done.37) | copy-start | bytes 49156
  810.0 123.7 %copy-start.49 = (f32[256]{0:T(256)S(1)}, f32[256]{0:T(256)}, u32[]{:S(2)}) copy-start(f32[256]{0:T(256)} %copy-done.48) | copy-start | bytes 3076
  810.0 123.7 %copy-start.51 = (f32[256]{0:T(256)S(1)}, f32[256]{0:T(256)}, u32[]{:S(2)}) copy-start(f32[256]{0:T(256)} %copy-done.50) | copy-start | bytes 3076
  810.0 123.7 %copy-start.53 = (f32[256]{0:T(256)S(1)}, f32[256]{0:T(256)}, u32[]{:S(2)}) copy-start(f32[256]{0:T(256)} %copy-done.52) | copy-start | bytes 3076
  810.0 123.7 %copy-start.68 = (f32[16]{0:T(128)S(1)}, f32[16]{0:T(128)}, u32[]{:S(2)}) copy-start(f32[16]{0:T(128)} %get-tuple-element.112) | copy-start | bytes 196
  810.0 125.3 %copy-start.4 = (f32[256,2048]{1,0:T(8,128)S(1)}, f32[256,2048]{1,0:T(8,128)}, u32[]{:S(2)}) copy-start(f32[256,2048]{1,0:T(8,128)} %copy-done.3) | copy-start | bytes 6291460
  810.0 125.3 %copy-start.24 = (bf16[32,64,128]{2,1,0:T(8,128)(2,1)S(1)}, bf16[32,64,128]{2,1,0:T(8,128)(2,1)}, u32[]{:S(2)}) copy-start(bf16[32,64,128]{2,1,0:T(8,128)(2,1)} %get-tuple-element.20) | copy-start | bytes 1572868
  810.0 125.3 %copy-start.45 = (f32[1,2048]{1,0:T(1,128)S(1)}, f32[1,2048]{1,0:T(1,128)}, u32[]{:S(2)}) copy-start(f32[1,2048]{1,0:T(1,128)} %copy-done.44) | copy-start | bytes 24580
  810.1 125.3 %copy-start.55 = (f32[256]{0:T(256)S(1)}, f32[256]{0:T(256)}, u32[]{:S(2)}) copy-start(f32[256]{0:T(256)} %copy-done.54) | copy-start | bytes 3076
  810.1 127.9 %copy-start.28 = (bf16[1,256,2048]{2,1,0:T(8,128)(2,1)S(1)}, bf16[1,256,2048]{2,1,0:T(8,128)(2,1)}, u32[]{:S(2)}) copy-start(bf16[1,256,2048]{2,1,0:T(8,128)(2,1)} %param.23) | copy-start | bytes 3145732
  991.6 20.4 %slice-start.8 = ((s8[8388608]{0:T(1024)(128)(4,1)}), s8[4194304]{0:T(1024)(128)(4,1)S(1)}, s32[]{:S(2)}) async-start(s8[8388608]{0:T(1024)(128)(4,1)} %bitcast.232), calls=%async_computation.8 | async-start | bytes 8388608
  1001.9 57.4 %collective-permute-start.4 = (bf16[1024,6144]{1,0:T(8,128)(2,1)}, bf16[1024,6144]{1,0:T(8,128)(2,1)}, u32[]{:S(2)}, u32[]{:S(2)}) collective-permute-start(bf16[1024,6144]{1,0:T(8,128)(2,1)} %convolution_convert_fusion.1), channel_id=1, source_target_pairs={{0,16},{16,0},{1,17},{17,1},{2,18},{18,2},{3,19},{19,3},{4,20},{20... | collective-permute-start | bytes 37748744 | tf_op jit(solution)/shard_map/ppermute | solution.py:904
  1001.9 15.9 %slice-start.4 = ((s8[8388608]{0:T(1024)(128)(4,1)}), s8[4194304]{0:T(1024)(128)(4,1)S(1)}, s32[]{:S(2)}) async-start(s8[8388608]{0:T(1024)(128)(4,1)} %bitcast.223), calls=%async_computation.4 | async-start | bytes 8388608
  1011.5 29.6 %collective-permute-start.8 = (bf16[2048,512]{1,0:T(8,128)(2,1)}, bf16[2048,512]{1,0:T(8,128)(2,1)}, u32[]{:S(2)}, u32[]{:S(2)}) collective-permute-start(bf16[2048,512]{1,0:T(8,128)(2,1)} %convolution_convert_fusion.6), channel_id=1, source_target_pairs={{0,16},{16,0},{1,17},{17,1},{2,18},{18,2},{3,19},{19,3},{4,20},{20... | collective-permute-start | bytes 6291464 | tf_op jit(solution)/shard_map/ppermute | solution.py:836
  1017.8 30.9 %collective-permute-start.7 = (bf16[2048,512]{1,0:T(8,128)(2,1)}, bf16[2048,512]{1,0:T(8,128)(2,1)}, u32[]{:S(2)}, u32[]{:S(2)}) collective-permute-start(bf16[2048,512]{1,0:T(8,128)(2,1)} %convolution_convert_fusion.7), channel_id=1, source_target_pairs={{0,16},{16,0},{1,17},{17,1},{2,18},{18,2},{3,19},{19,3},{4,20},{20... | collective-permute-start | bytes 6291464 | tf_op jit(solution)/shard_map/ppermute | solution.py:836
  1023.9 7.8 collective-permute-start.9
  1025.8 5.0 collective-permute-start.6
  1030.8 25.2 %collective-permute-start.5 = (bf16[1024,2048]{1,0:T(8,128)(2,1)S(1)}, bf16[1024,2048]{1,0:T(8,128)(2,1)S(1)}, u32[]{:S(2)}, u32[]{:S(2)}) collective-permute-start(bf16[1024,2048]{1,0:T(8,128)(2,1)S(1)} %convolution_convert_fusion.4), channel_id=1, source_target_pairs={{0,16},{16,0},{1,17},{17,1},{2,18},{18,2},{3,19},{19,3},{4,20},{20... | collective-permute-start | bytes 12582920 | tf_op jit(solution)/shard_map/ppermute | solution.py:904
  (82 other events, 412.9 us)

commit v2 on v1

--- a/solution.py
+++ b/solution.py
@@ -422,13 +422,45 @@
     pl.semaphore_wait(barrier, total)
 
 
-def hops(event):
-    return sum(r[0] for r in event.values() if r)
-
-
-def gather_kernel(grid, parts, count, *refs):
-    srcs, outs = refs[:count], refs[count : 2 * count]
-    send_sem, recv_sem, own_sem = refs[2 * count :]
+def farthest(order, event):
+    return tuple(event[d][0] if event[d] else 0 for d in reversed(order))
+
+
+class Beside:
+    def __init__(self, ins=(), in_specs=(), outs=(), scratch=(), steps=None, lead=0.0, span=1.0):
+        self.lead, self.span = lead, span
+        self.ins, self.in_specs, self.outs, self.scratch = ins, in_specs, outs, scratch
+        self.steps = steps
+
+    def share(self, refs, count, own_scratch):
+        cuts = [count, len(self.ins), count, len(self.outs), own_scratch, len(self.scratch)]
+        groups, at = [], 0
+        for n in cuts:
+            groups.append(refs[at : at + n])
+            at += n
+        steps = self.steps(groups[1], groups[3], groups[5]) if self.steps else []
+        return groups[0], groups[2], groups[4], steps
+
+
+def mingle(events, steps, free, lead, span):
+    for event in events[:free]:
+        event()
+    first = round(lead * len(steps))
+    for step in steps[:first]:
+        step()
+    rest, left = events[free:], steps[first:]
+    done = 0
+    for n, event in enumerate(rest):
+        event()
+        while done < len(left) and done * len(rest) * span < (n + 1) * len(left):
+            left[done]()
+            done += 1
+    for step in left[done:]:
+        step()
+
+
+def gather_kernel(grid, parts, count, beside, *refs):
+    srcs, outs, (send_sem, recv_sem, own_sem), steps = beside.share(refs, count, 3)
     c = grid.coords()
     me = grid.index(c)
     own = [pltpu.make_async_copy(s, o.at[me], own_sem.at[i]) for i, (s, o) in enumerate(zip(srcs, outs))]
@@ -457,10 +489,11 @@
 
     todo = []
     for p, (_, _, _, order) in enumerate(parts):
-        for n, event in enumerate(grid.events(order)):
-            todo.append((hops(event), p if len(parts) > 8 else 0, n, p, event))
-    todo.sort(key=lambda t: t[:4])
-    for _, _, _, p, event in todo:
+        for event in grid.events(order):
+            todo.append((farthest(order, event), p, event))
+    todo.sort(key=lambda t: t[:2])
+
+    def handle(p, event):
         a, _, _, order = parts[p]
         o, pred, last = grid.place(c, order, event)
         origin = grid.index(o)
@@ -483,26 +516,37 @@
         for d in order[last + 1 :]:
             for side in grid.sides(d):
                 push(p, origin, source, d, side, pred)
+
+    mingle(
+        [functools.partial(handle, p, event) for _, p, event in todo],
+        steps,
+        sum(not any(event.values()) for _, _, event in todo),
+        beside.lead,
+        beside.span,
+    )
     for pred, copy in sent:
         when(pred, copy.wait_send)
     for copy in own:
         copy.wait()
 
 
-def gather(arrays, grid, parts, cid):
+def gather(arrays, grid, parts, cid, beside=Beside(), vmem=16 << 20):
     n, count = grid.size, len(arrays)
     return pl.pallas_call(
-        functools.partial(gather_kernel, grid, parts, count),
-        out_shape=[jax.ShapeDtypeStruct((n,) + x.shape, x.dtype) for x in arrays],
-        in_specs=[pl.BlockSpec(memory_space=pl.ANY)] * count,
-        out_specs=[pl.BlockSpec(memory_space=pl.ANY)] * count,
+        functools.partial(gather_kernel, grid, parts, count, beside),
+        out_shape=[jax.ShapeDtypeStruct((n,) + x.shape, x.dtype) for x in arrays] + list(beside.outs),
+        in_specs=[pl.BlockSpec(memory_space=pl.ANY)] * count + list(beside.in_specs),
+        out_specs=[pl.BlockSpec(memory_space=pl.ANY)] * (count + len(beside.outs)),
         scratch_shapes=[
             pltpu.SemaphoreType.DMA((len(parts), n, len(grid.lanes))),
             pltpu.SemaphoreType.DMA((len(parts), n)),
             pltpu.SemaphoreType.DMA((count,)),
-        ],
-        compiler_params=pltpu.CompilerParams(collective_id=cid, has_side_effects=True),
-    )(*arrays)
+        ]
+        + list(beside.scratch),
+        compiler_params=pltpu.CompilerParams(
+            collective_id=cid, has_side_effects=True, vmem_limit_bytes=vmem
+        ),
+    )(*arrays, *beside.ins)
 
 
 def landing_slots(grid, order):
@@ -514,11 +558,11 @@
     return base, total
 
 
-def scatter_kernel(grid, parts, count, *refs):
+def scatter_kernel(grid, parts, count, beside, *refs):
     k = len(parts)
-    srcs, outs = refs[:count], refs[count : 2 * count]
-    held, mine, totals = refs[2 * count : 2 * count + k], refs[2 * count + k : 2 * count + 2 * k], refs[2 * count + 2 * k : 3 * count + 2 * k]
-    send_sem, recv_sem, mine_sem, out_sem = refs[3 * count + 2 * k :]
+    srcs, outs, scratch, steps = beside.share(refs, count, 2 * k + count + 4)
+    held, mine, totals = scratch[:k], scratch[k : 2 * k], scratch[2 * k : 2 * k + count]
+    send_sem, recv_sem, mine_sem, out_sem = scratch[2 * k + count :]
     c = grid.coords()
 
     def piece(p, ref):
@@ -555,10 +599,11 @@
     todo = []
     for p, (_, _, _, order) in enumerate(parts):
         for event in grid.events(order):
-            todo.append((tuple(-(event[d][0] if event[d] else 0) for d in reversed(order)), p, event))
+            todo.append((tuple(-far for far in farthest(order, event)), p, event))
     todo.sort(key=lambda t: t[:2])
     sent = []
-    for _, p, event in todo:
+
+    def handle(p, event):
         a, row0, rows, order = parts[p]
         o, pred, last = grid.place(c, order, event)
         always, sometimes = [], []
@@ -630,6 +675,14 @@
             )
             when(pred, copy.start)
             sent.append((pred, copy))
+
+    mingle(
+        [functools.partial(handle, p, event) for _, p, event in todo],
+        steps,
+        sum(event[parts[p][3][-1]] is not None for _, p, event in todo),
+        beside.lead,
+        beside.span,
+    )
     done = [pltpu.make_async_copy(t, o, out_sem.at[i]) for i, (t, o) in enumerate(zip(totals, outs))]
     for copy in done:
         copy.start()
@@ -639,17 +692,17 @@
         copy.wait()
 
 
-def scatter(arrays, grid, parts, cid):
+def scatter(arrays, grid, parts, cid, beside=Beside()):
     count = len(arrays)
     slots = [landing_slots(grid, order)[1] for _, _, _, order in parts]
     mine = [grid.size // grid.dims[order[-1]] for _, _, _, order in parts]
     blocks = [((rows, arrays[a].shape[2]), arrays[a].dtype) for a, _, rows, _ in parts]
     flat = [jax.ShapeDtypeStruct(x.shape[1:], jnp.float32) for x in arrays]
     return pl.pallas_call(
-        functools.partial(scatter_kernel, grid, parts, count),
-        out_shape=flat,
-        in_specs=[pl.BlockSpec(memory_space=pl.ANY)] * count,
-        out_specs=[pl.BlockSpec(memory_space=pl.ANY)] * count,
+        functools.partial(scatter_kernel, grid, parts, count, beside),
+        out_shape=flat + list(beside.outs),
+        in_specs=[pl.BlockSpec(memory_space=pl.ANY)] * count + list(beside.in_specs),
+        out_specs=[pl.BlockSpec(memory_space=pl.ANY)] * (count + len(beside.outs)),
         scratch_shapes=[pltpu.VMEM((s,) + b, t) for s, (b, t) in zip(slots, blocks)]
         + [pltpu.VMEM((s,) + b, t) for s, (b, t) in zip(mine, blocks)]
         + [pltpu.VMEM(x.shape, x.dtype) for x in flat]
@@ -658,16 +711,492 @@
             pltpu.SemaphoreType.DMA((len(parts), max(slots))),
             pltpu.SemaphoreType.DMA((len(parts), max(mine))),
             pltpu.SemaphoreType.DMA((count,)),
-        ],
+        ]
+        + list(beside.scratch),
         compiler_params=pltpu.CompilerParams(
             collective_id=cid, has_side_effects=True, vmem_limit_bytes=60 << 20
         ),
-    )(*arrays)
-
-
-def cut(array, rows, orders):
-    share = rows // len(orders)
-    return tuple((array, i * share, share, order) for i, order in enumerate(orders))
+    )(*arrays, *beside.ins)
+
+
+def cut(array, shares, orders):
+    starts = [sum(shares[:i]) for i in range(len(shares))]
+    return tuple((array, start, share, order) for start, share, order in zip(starts, shares, orders))
+
+
+def each_tile(total, width, f):
+    @pl.loop(0, total // width)
+    def _(t):
+        f(pl.ds(pl.multiple_of(t * width, width), width))
+
+
+def dot(left, right):
+    return jnp.dot(left, right, preferred_element_type=jnp.float32)
+
+
+def dot_across(left, right):
+    return lax.dot_general(left, right, (((1,), (1,)), ((), ())), preferred_element_type=jnp.float32)
+
+
+class Move:
+    def __init__(self, *refs):
+        self.refs = refs
+
+    def start(self):
+        pltpu.make_async_copy(*self.refs).start()
+
+    def wait(self):
+        pltpu.make_async_copy(*self.refs).wait()
+
+
+ANYWHERE = pl.BlockSpec(memory_space=pl.ANY)
+ON_CORE = pl.BlockSpec(memory_space=pltpu.VMEM)
+
+
+def weight_copies(halves, held, sem):
+    gate_own, gate_far, up_own, up_far, down_own, down_far = halves
+    gate, up, down = held
+    half = gate.shape[1] // 2
+    own, far = pl.ds(0, half), pl.ds(half, half)
+    pairs = [
+        (gate_own, gate.at[:, own]),
+        (gate_far, gate.at[:, far]),
+        (up_own, up.at[:, own]),
+        (up_far, up.at[:, far]),
+        (down_own, down.at[own, :]),
+        (down_far, down.at[far, :]),
+    ]
+    return [Move(a, b, sem.at[i]) for i, (a, b) in enumerate(pairs)]
+
+
+def pick_of(ranks, row, capacity):
+    line = ranks[row : row + 1, :]
+    slot = lax.broadcasted_iota(jnp.int32, (capacity, line.shape[1]), 0).astype(jnp.float32)
+    return line == slot
+
+
+def put_of(ranks, row, capacity):
+    line = ranks[:, row : row + 1]
+    slot = lax.broadcasted_iota(jnp.int32, (line.shape[0], capacity), 1).astype(jnp.float32)
+    return (line == slot).astype(jnp.float32).astype(jnp.bfloat16)
+
+
+def forward_beside(ffn_rows, rank_rows, rank_cols, weight_cols, halves, capacity):
+    row_count, tokens, width = ffn_rows.shape
+    hidden = 2 * halves[0].shape[1]
+    pairs, pair = row_count // 2, 2 * capacity
+    slots = row_count * capacity
+    low, full = jnp.bfloat16, jnp.float32
+
+    def steps(ins, outs, scratch):
+        ffn_in, ranks, ranks_t, weights_t = ins[:4]
+        weights, (ffn, xs, pre, units, out, mix), sems = scratch[:3], scratch[3:9], scratch[9:]
+        load_sem, row_sem, out_sem = sems
+        heavy = weight_copies(ins[4:], weights, load_sem)
+        gate_w, up_w, down_w = weights
+
+        def load(q):
+            return Move(ffn_in.at[pl.ds(2 * q, 2)], ffn.at[q % 2], row_sem.at[q % 2])
+
+        def leave(q):
+            here = pl.ds(q * pair, pair)
+            moves = [
+                (xs, outs[0].at[here]),
+                (pre.at[0], outs[1].at[here]),
+                (pre.at[1], outs[2].at[here]),
+                (units, outs[3].at[here]),
+                (out, outs[4].at[here]),
+                (mix, outs[5].at[pl.ds(2 * q, 2)]),
+            ]
+            return [Move(a, b, out_sem.at[i]) for i, (a, b) in enumerate(moves)]
+
+        def opening():
+            for copy in heavy:
+                copy.start()
+            load(0).start()
+
+        def choose(q):
+            load(q).wait()
+            if q + 1 < pairs:
+                load(q + 1).start()
+            if q:
+                leave(q - 1)[0].wait()
+            for i in range(2):
+                pick = pick_of(ranks, 2 * q + i, capacity).astype(full).astype(low)
+                rows = pl.ds(i * capacity, capacity)
+
+                def tile(cols, i=i, pick=pick, rows=rows):
+                    xs[rows, cols] = dot(pick, ffn[q % 2, i, :, cols]).astype(low)
+
+                each_tile(width, 512, tile)
+            leave(q)[0].start()
+
+        def widen(q):
+            if q == 0:
+                for copy in heavy[:4]:
+                    copy.wait()
+            else:
+                for copy in leave(q - 1)[1:4]:
+                    copy.wait()
+
+            def tile(cols):
+                gate = dot(xs[...], gate_w[:, cols])
+                up = dot(xs[...], up_w[:, cols])
+                pre[0, :, cols] = gate
+                pre[1, :, cols] = up
+                units[:, cols] = (gate * jax.nn.sigmoid(gate) * up).astype(low)
+
+            each_tile(hidden, 256, tile)
+            for copy in leave(q)[1:4]:
+                copy.start()
+
+        def narrow(q):
+            if q == 0:
+                for copy in heavy[4:]:
+                    copy.wait()
+            else:
+                for copy in leave(q - 1)[4:]:
+                    copy.wait()
+            puts = [put_of(ranks_t, 2 * q + i, capacity) for i in range(2)]
+            scales = [weights_t[:, 2 * q + i : 2 * q + i + 1] for i in range(2)]
+
+            def tile(cols):
+                value = dot(units[...], down_w[:, cols]).astype(low)
+                out[:, cols] = value
+                for i in range(2):
+                    part = dot(puts[i], value[i * capacity : (i + 1) * capacity]) * scales[i]
+                    mix[i, :, cols] = part.astype(low)
+
+            each_tile(width, 256, tile)
+            for copy in leave(q)[4:]:
+                copy.start()
+
+        def closing():
+            for copy in leave(pairs - 1):
+                copy.wait()
+
+        listed = [opening]
+        for q in range(pairs):
+            listed += [functools.partial(f, q) for f in (choose, widen, narrow)]
+        return listed + [closing]
+
+    return Beside(
+        ins=(ffn_rows, rank_rows, rank_cols, weight_cols) + tuple(halves),
+        in_specs=(ANYWHERE, ON_CORE, ON_CORE, ON_CORE) + (ANYWHERE,) * 6,
+        outs=[
+            jax.ShapeDtypeStruct((slots, width), low),
+            jax.ShapeDtypeStruct((slots, hidden), full),
+            jax.ShapeDtypeStruct((slots, hidden), full),
+            jax.ShapeDtypeStruct((slots, hidden), low),
+            jax.ShapeDtypeStruct((slots, width), low),
+            jax.ShapeDtypeStruct((row_count, tokens, width), low),
+        ],
+        scratch=[
+            pltpu.VMEM((width, hidden), low),
+            pltpu.VMEM((width, hidden), low),
+            pltpu.VMEM((hidden, width), low),
+            pltpu.VMEM((2, 2, tokens, width), low),
+            pltpu.VMEM((pair, width), low),
+            pltpu.VMEM((2, pair, hidden), full),
+            pltpu.VMEM((pair, hidden), low),
+            pltpu.VMEM((pair, width), low),
+            pltpu.VMEM((2, tokens, width), low),
+            pltpu.SemaphoreType.DMA((6,)),
+            pltpu.SemaphoreType.DMA((2,)),
+            pltpu.SemaphoreType.DMA((6,)),
+        ],
+        steps=steps,
+        lead=0.2,
+        span=0.5,
+    )
+
+
+def backward_beside(cot_rows, rank_rows, rank_cols, weight_rows, gate_pre, up_pre, expert_out, halves, capacity):
+    row_count, tokens, width = cot_rows.shape
+    hidden = 2 * halves[0].shape[1]
+    pairs, pair = row_count // 2, 2 * capacity
+    slots = row_count * capacity
+    low, full = jnp.bfloat16, jnp.float32
+
+    def steps(ins, outs, scratch):
+        cot_in, ranks, ranks_t, weights, gate_in, up_in, out_in = ins[:7]
+        heavy_refs, (cot, ge, pre, out, gg, gu, gx, dots, sums), sems = scratch[:3], scratch[3:12], scratch[12:]
+        load_sem, row_sem, out_sem = sems
+        heavy = weight_copies(ins[7:], heavy_refs, load_sem)
+        gate_w, up_w, down_w = heavy_refs
+
+        def load(q):
+            return Move(cot_in.at[pl.ds(2 * q, 2)], cot.at[q % 2], row_sem.at[q % 2])
+
+        def fetch(q):
+            here = pl.ds(q * pair, pair)
+            moves = [(out_in, out), (gate_in, pre.at[0]), (up_in, pre.at[1])]
+            return [Move(a.at[here], b, row_sem.at[2 + i]) for i, (a, b) in enumerate(moves)]
+
+        def leave(q):
+            here = pl.ds(q * pair, pair)
+            moves = [(ge, outs[0].at[here]), (gg, outs[1].at[here]), (gu, outs[2].at[here])]
+            moves.append((gx, outs[3].at[pl.ds(2 * q, 2)]))
+            return [Move(a, b, out_sem.at[i]) for i, (a, b) in enumerate(moves)]
+
+        last = Move(dots, outs[4], out_sem.at[4])
+
+        def opening():
+            load(0).start()
+            for copy in fetch(0):
+                copy.start()
+            for copy in heavy:
+                copy.start()
+
+        def choose(q):
+            load(q).wait()
+            fetch(q)[0].wait()
+            if q + 1 < pairs:
+                load(q + 1).start()
+            if q:
+                leave(q - 1)[0].wait()
+            for i in range(2):
+                row = 2 * q + i
+                pick = pick_of(ranks, row, capacity)
+                pick_low = pick.astype(full).astype(low)
+                scale = jnp.sum(jnp.where(pick, weights[row : row + 1, :], 0.0), axis=1, keepdims=True)
+                rows = pl.ds(i * capacity, capacity)
+                sums[...] = jnp.zeros_like(sums)
+
+                def tile(cols, i=i, pick_low=pick_low, scale=scale, rows=rows):
+                    value = dot(pick_low, cot[q % 2, i, :, cols])
+                    ge[rows, cols] = (value * scale).astype(low)
+                    product = value * out[rows, cols].astype(full)
+                    total = product[:, :128]
+                    for lane in range(128, product.shape[1], 128):
+                        total = total + product[:, lane : lane + 128]
+                    sums[...] += total
+
+                each_tile(width, 512, tile)
+                slot_dot = jnp.sum(sums[...], axis=1, keepdims=True)
+                dots[row : row + 1, :] = jnp.sum(jnp.where(pick, slot_dot, 0.0), axis=0, keepdims=True)
+            leave(q)[0].start()
+            if q + 1 < pairs:
+                fetch(q + 1)[0].start()
+
+        def narrow(q):
+            for copy in fetch(q)[1:]:
+                copy.wait()
+            if q == 0:
+                for copy in heavy:
+                    copy.wait()
+            else:
+                for copy in leave(q - 1)[1:3]:
+                    copy.wait()
+
+            def tile(cols):
+                grad = dot_across(ge[...], down_w[cols, :])
+                gate, up = pre[0, :, cols], pre[1, :, cols]
+                sigmoid = jax.nn.sigmoid(gate)
+                gg[:, cols] = (grad * up * sigmoid * (1.0 + gate * (1.0 - sigmoid))).astype(low)
+                gu[:, cols] = (grad * gate * sigmoid).astype(low)
+
+            each_tile(hidden, 256, tile)
+            for copy in leave(q)[1:3]:
+                copy.start()
+            if q + 1 < pairs:
+                for copy in fetch(q + 1)[1:]:
+                    copy.start()
+
+        def widen(q):
+            if q:
+                leave(q - 1)[3].wait()
+            puts = [put_of(ranks_t, 2 * q + i, capacity) for i in range(2)]
+
+            def tile(cols):
+                value = dot_across(gg[...], gate_w[cols, :]) + dot_across(gu[...], up_w[cols, :])
+                value = value.astype(low)
+                for i in range(2):
+                    part = dot(puts[i], value[i * capacity : (i + 1) * capacity])
+                    gx[i, :, cols] = part.astype(low)
+
+            each_tile(width, 256, tile)
+            leave(q)[3].start()
+
+        def closing():
+            last.start()
+            for copy in leave(pairs - 1):
+                copy.wait()
+            last.wait()
+
+        listed = [opening]
+        for q in range(pairs):
+            listed += [functools.partial(f, q) for f in (choose, narrow, widen)]
+        return listed + [closing]
+
+    return Beside(
+        ins=(cot_rows, rank_rows, rank_cols, weight_rows, gate_pre, up_pre, expert_out) + tuple(halves),
+        in_specs=(ANYWHERE, ON_CORE, ON_CORE, ON_CORE) + (ANYWHERE,) * 9,
+        outs=[
+            jax.ShapeDtypeStruct((slots, width), low),
+            jax.ShapeDtypeStruct((slots, hidden), low),
+            jax.ShapeDtypeStruct((slots, hidden), low),
+            jax.ShapeDtypeStruct((row_count, tokens, width), low),
+            jax.ShapeDtypeStruct((row_count, tokens), full),
+        ],
+        scratch=[
+            pltpu.VMEM((width, hidden), low),
+            pltpu.VMEM((width, hidden), low),
+            pltpu.VMEM((hidden, width), low),
+            pltpu.VMEM((2, 2, tokens, width), low),
+            pltpu.VMEM((pair, width), low),
+            pltpu.VMEM((2, pair, hidden), full),
+            pltpu.VMEM((pair, width), low),
+            pltpu.VMEM((pair, hidden), low),
+            pltpu.VMEM((pair, hidden), low),
+            pltpu.VMEM((2, tokens, width), low),
+            pltpu.VMEM((row_count, tokens), full),
+            pltpu.VMEM((capacity, 128), full),
+            pltpu.SemaphoreType.DMA((6,)),
+            pltpu.SemaphoreType.DMA((5,)),
+            pltpu.SemaphoreType.DMA((5,)),
+        ],
+        steps=steps,
+        span=0.8,
+    )
+
+
+def outer_beside(rows_in, grad_rows, grad_gate, grad_up, units):
+    slots, width = rows_in.shape
+    hidden = units.shape[1]
+    half = hidden // 2
+    block = 256
+    low, full = jnp.bfloat16, jnp.float32
+
+    def steps(ins, outs, scratch):
+        rows_ref, grads_ref, gate_ref, up_ref, units_ref = ins
+        left, turned, gate, up, grads, wide_own, wide_far, tall_own, tall_far, load_sem, left_sem, out_sem = scratch
+        heavy = [
+            Move(a, b, load_sem.at[i])
+            for i, (a, b) in enumerate([(gate_ref, gate), (up_ref, up), (grads_ref, grads)])
+        ]
+        jobs = [(rows_ref, t) for t in range(width // block)] + [
+            (units_ref, t) for t in range(hidden // block)
+        ]
+
+        def load(n):
+            ref, t = jobs[n]
+            return Move(
+                ref.at[:, pl.ds(t * block, block)], left.at[n % 2], left_sem.at[n % 2]
+            )
+
+        def turn(n):
+            load(n).wait()
+            if n + 1 < len(jobs):
+                load(n + 1).start()
+
+            @pl.loop(0, slots // block)
+            def _(k):
+                here = pl.ds(pl.multiple_of(k * block, block), block)
+                turned[:, here] = left[n % 2, here, :].astype(full).T.astype(low)
+
+        def leave_wide(which, t):
+            here = pl.ds(t * block, block)
+            return [
+                Move(wide_own.at[which], outs[2 * which].at[here], out_sem.at[2 * which]),
+                Move(wide_far.at[which], outs[2 * which + 1].at[here], out_sem.at[2 * which + 1]),
+            ]
+
+        def leave_tall(t):
+            far = t * block >= half
+            here = pl.ds(t * block - (half if far else 0), block)
+            return Move(
+                tall_far if far else tall_own, outs[5 if far else 4].at[here], out_sem.at[5 if far else 4]
+            )
+
+        def wide(which, t):
+            right = (gate, up)[which]
+            if t == 0:
+                heavy[which].wait()
+            else:
+                for copy in leave_wide(which, t - 1):
+                    copy.wait()
+
+            def own(cols):
+                wide_own[which, :, cols] = dot(turned[...], right[:, cols])
+
+            each_tile(half, 256, own)
+
+            @pl.loop(0, half // 256)
+            def _(k):
+                cols = pl.ds(pl.multiple_of(k * 256, 256), 256)
+                there = pl.ds(pl.multiple_of(half + k * 256, 256), 256)
+                wide_far[which, :, cols] = dot(turned[...], right[:, there]).astype(low)
+
+            for copy in leave_wide(which, t):
+                copy.start()
+
+        def tall(t):
+            far = t * block >= half
+            if t == 0:
+                heavy[2].wait()
+            if t * block not in (0, half):
+                leave_tall(t - 1).wait()
+
+            def tile(cols):
+                value = dot(turned[...], grads[:, cols])
+                if far:
+                    tall_far[:, cols] = value.astype(low)
+                else:
+                    tall_own[:, cols] = value
+
+            each_tile(width, 256, tile)
+            leave_tall(t).start()
+
+        def opening():
+            load(0).start()
+            for copy in heavy:
+                copy.start()
+
+        def closing():
+            for which in range(2):
+                for copy in leave_wide(which, width // block - 1):
+                    copy.wait()
+            leave_tall(half // block - 1).wait()
+            leave_tall(hidden // block - 1).wait()
+
+        listed = [opening]
+        for n, (ref, t) in enumerate(jobs):
+            listed.append(functools.partial(turn, n))
+            if n < width // block:
+                listed += [functools.partial(wide, which, t) for which in range(2)]
+            else:
+                listed.append(functools.partial(tall, t))
+        return listed + [closing]
+
+    return Beside(
+        ins=(rows_in, grad_rows, grad_gate, grad_up, units),
+        in_specs=(ANYWHERE,) * 5,
+        outs=[
+            jax.ShapeDtypeStruct((width, half), full),
+            jax.ShapeDtypeStruct((width, half), low),
+            jax.ShapeDtypeStruct((width, half), full),
+            jax.ShapeDtypeStruct((width, half), low),
+            jax.ShapeDtypeStruct((half, width), full),
+            jax.ShapeDtypeStruct((half, width), low),
+        ],
+        scratch=[
+            pltpu.VMEM((2, slots, block), low),
+            pltpu.VMEM((block, slots), low),
+            pltpu.VMEM((slots, hidden), low),
+            pltpu.VMEM((slots, hidden), low),
+            pltpu.VMEM((slots, width), low),
+            pltpu.VMEM((2, block, half), full),
+            pltpu.VMEM((2, block, half), low),
+            pltpu.VMEM((block, width), full),
+            pltpu.VMEM((block, width), low),
+            pltpu.SemaphoreType.DMA((3,)),
+            pltpu.SemaphoreType.DMA((2,)),
+            pltpu.SemaphoreType.DMA((6,)),
+        ],
+        steps=steps,
+        span=0.6,
+    )
 
 
 def gathered_body(
@@ -700,6 +1229,8 @@
     devices = Grid(dims, cores=True)
     z, y, x = 0, 1, 2
     row_orders = [(x, z, y), (y, z, x), (z, x, y), (z, y, x)]
+    row_shares = [5 * row_count // 16, 5 * row_count // 16, 3 * row_count // 16, 3 * row_count // 16]
+    quarter = [weight_rows // 4] * 4
     wide_orders = [tuple(d + 1 for d in order) + (0,) for order in row_orders]
     expert = lax.axis_index("expert")
     core = lax.axis_index("dp")
@@ -711,7 +1242,9 @@
     qkv_all, out_all, small_all = gather(
         [w_qkv, w_out, small],
         devices,
-        cut(0, weight_rows, wide_orders) + cut(1, weight_rows, wide_orders[:2]) + cut(2, weight_rows, wide_orders[2:3]),
+        cut(0, quarter, wide_orders)
+        + cut(1, quarter, wide_orders[:2] * 2)
+        + cut(2, [weight_rows], wide_orders[2:3]),
         1,
     )
     qkv_weight = qkv_all.reshape(D, 3 * D)
@@ -769,11 +1302,10 @@
         axis=0,
     )
 
-    (cot_rows,) = gather([cotangent[0]], chips, cut(0, row_count, row_orders), 2)
     ffn_rows, aside_rows = gather(
         [ffn_low, aside],
         chips,
-        cut(0, row_count, row_orders) + cut(1, aside.shape[0], row_orders[2:3]),
+        cut(0, row_shares, row_orders) + cut(1, [aside.shape[0]], row_orders[2:3]),
         3,
     )
     sums_core = jnp.sum(aside_rows[:, 2 * expert_count, : 2 * expert_count], axis=0)
@@ -782,69 +1314,36 @@
     balance = jnp.sum(count_total * prob_total) * balance_factor
     weight_of = lax.dynamic_index_in_dim(aside_rows, expert, 1, keepdims=False)
     rank_of = lax.dynamic_index_in_dim(aside_rows, expert_count + expert, 1, keepdims=False)
-    pick = rank_of[:, None, :] == jnp.arange(capacity, dtype=jnp.int32).astype(full)[None, :, None]
-    pick_low = pick.astype(low)
-    all_slots = owners * capacity
-    rows_in = jnp.einsum("rkt,rtd->rkd", pick_low, ffn_rows, preferred_element_type=full)
-    rows_in = rows_in.astype(low).reshape(all_slots, D)
-    cot_in = jnp.einsum("rkt,rtd->rkd", pick_low, cot_rows, preferred_element_type=full)
-    cot_in = cot_in.astype(low).reshape(all_slots, D)
-    slot_weight = jnp.sum(jnp.where(pick, weight_of[:, None, :], 0.0), axis=-1).reshape(all_slots, 1)
-    grad_rows = (cot_in.astype(full) * slot_weight).astype(low)
-
-    def forward(gate_weight, up_weight):
-        gate_pre = jnp.dot(rows_in, gate_weight, preferred_element_type=full)
-        up_pre = jnp.dot(rows_in, up_weight, preferred_element_type=full)
-        return gate_pre, up_pre, (jax.nn.silu(gate_pre) * up_pre).astype(low)
-
-    own, far = forward(gate_own, up_own), forward(gate_far, up_far)
-    expert_out = jnp.dot(own[2], down_own, preferred_element_type=full)
-    expert_out = (expert_out + jnp.dot(far[2], down_far, preferred_element_type=full)).astype(low)
-    dot_slot = jnp.sum(cot_in.astype(full) * expert_out.astype(full), axis=-1).reshape(owners, 1, capacity)
-    dot_route = jnp.sum(jnp.where(pick, dot_slot.reshape(owners, capacity, 1), 0.0), axis=1)
-    mixture_part = jnp.einsum(
-        "rkt,rkd->rtd", pick_low, expert_out.reshape(owners, capacity, D), preferred_element_type=full
-    )
-    mixture_part = (mixture_part * weight_of[:, :, None]).astype(low)
-
-    def backward(parts, down_weight):
-        gate_pre, up_pre, _ = parts
-        grad_units = jnp.einsum("sd,fd->sf", grad_rows, down_weight, preferred_element_type=full)
-        gate_sigmoid = jax.nn.sigmoid(gate_pre)
-        grad_gate = grad_units * up_pre * gate_sigmoid * (1.0 + gate_pre * (1.0 - gate_sigmoid))
-        return grad_gate.astype(low), (grad_units * gate_pre * gate_sigmoid).astype(low)
-
-    grad_own, grad_far = backward(own, down_own), backward(far, down_far)
-    back = jnp.einsum("sf,df->sd", grad_own[0], gate_own, preferred_element_type=full)
-    back = back + jnp.einsum("sf,df->sd", grad_own[1], up_own, preferred_element_type=full)
-    back = back + jnp.einsum("sf,df->sd", grad_far[0], gate_far, preferred_element_type=full)
-    back = back + jnp.einsum("sf,df->sd", grad_far[1], up_far, preferred_element_type=full)
-    back_part = jnp.einsum(
-        "rkt,rkd->rtd", pick_low, back.astype(low).reshape(owners, capacity, D), preferred_element_type=full
-    ).astype(low)
-    route_part = jnp.where(
-        (expert_ids == expert)[None, :, None], dot_route[:, None, :], 0.0
-    )
-
-    def outer(left, right):
-        return jnp.einsum("sa,sb->ab", left, right, preferred_element_type=full)
-
-    def weight_grads(units, grads):
-        return outer(rows_in, grads[0]), outer(rows_in, grads[1]), outer(units, grad_rows)
-
-    sent_grads = [
-        lax.ppermute(g.astype(low), "dp", swap) for g in weight_grads(far[2], grad_far)
-    ]
-    expert_grads = [
-        (a + b.astype(full))[None] for a, b in zip(weight_grads(own[2], grad_own), sent_grads)
-    ]
-    grad_ffn, grad_route = scatter(
+    halves = (gate_own, gate_far, up_own, up_far, down_own, down_far)
+    cot_rows, rows_in, gate_pre, up_pre, units, expert_out, mixture_part = gather(
+        [cotangent[0]],
+        chips,
+        cut(0, row_shares, row_orders),
+        2,
+        forward_beside(ffn_rows, rank_of, rank_of.T, weight_of.T, halves, capacity),
+        vmem=60 << 20,
+    )
+    mixture, grad_rows, grad_gate, grad_up, back_part, dot_route = scatter(
+        [mixture_part],
+        chips,
+        cut(0, row_shares, row_orders),
+        5,
+        backward_beside(
+            cot_rows, rank_of, rank_of.T, weight_of, gate_pre, up_pre, expert_out, halves, capacity
+        ),
+    )
+    route_part = jnp.where((expert_ids == expert)[None, :, None], dot_route[:, None, :], 0.0)
+    grad_ffn, grad_route, *halves_grads = scatter(
         [back_part, route_part],
         chips,
-        cut(0, row_count, row_orders) + cut(1, expert_count, row_orders[2:3]),
+        cut(0, row_shares, row_orders) + cut(1, [expert_count], row_orders[2:3]),
         4,
-    )
-    (mixture,) = scatter([mixture_part], chips, cut(0, row_count, row_orders), 5)
+        outer_beside(rows_in, grad_rows, grad_gate, grad_up, units),
+    )
+    expert_grads = [
+        (own + lax.ppermute(far, "dp", swap).astype(full))[None]
+        for own, far in zip(halves_grads[::2], halves_grads[1::2])
+    ]
     result = (live_float * (hidden_state + mixture)).astype(low)[None]
 
     balance_coef = BALANCE_WEIGHT * balance_factor
@@ -885,6 +1384,9 @@
 
     half = D // 2
 
+    def outer(left, right):
+        return jnp.einsum("sa,sb->ab", left, right, preferred_element_type=full)
+
     def core_half(value, side):
         return lax.dynamic_slice_in_dim(value, side * half, half, 1)
 
@@ -910,7 +1412,9 @@
     grad_qkv, grad_out, grad_small = scatter(
         shares,
         chips,
-        cut(0, weight_rows, row_orders) + cut(1, weight_rows, row_orders) + cut(2, weight_rows, row_orders[2:3]),
+        cut(0, quarter, row_orders)
+        + cut(1, quarter, row_orders[:2] * 2)
+        + cut(2, [weight_rows], row_orders[2:3]),
         6,
     )
     return (

time: 1230 us -> 1020 us (0.83)
  matrix products: 293 us -> 95.3 us
  Pallas kernels: 826 us -> 783 us
  local copies, waits for them, and re-layouts: 35 us -> 54.8 us
  waiting for transfers between devices: 0.03 us -> 17.6 us
    dot_general x16 -> x0, matrix products: 174 us -> none  [the longest x2 25.7 us: forward(): up_pre = jnp.dot(rows_in, up_weight, preferred_element_type=full)]
    pallas_call x6, Pallas kernels: 826 us -> 783 us  [the longest x3 399 us: gather(): pl.pallas_call(functools.partial(gather_kernel, grid, parts, count, besid...]
    dot_general x10 -> x4, matrix products: 69.4 us -> 31.8 us  [outer(): return jnp.einsum('sa,sb->ab', left, right, preferred_element_type=full)]
    ppermute x3, waiting for transfers between devices: 0.01 us -> 17.6 us  [gathered_body(): lax.ppermute(g, 'dp', swap)]
    convert_element_type x3 -> x0, other arithmetic: 16.4 us -> none  [the longest x2 16.4 us: gathered_body(): grad_rows = (cot_in.astype(full) * slot_weight).astype(low)]
    unnamed x217 -> x112, local copies, waits for them, and re-layouts: 19.9 us -> 33.2 us
  transfers between devices with their start and end apart: 10 -> 10, of which waited for: 0 -> 1; matrix products, arithmetic and copies ran while one was open for 13% -> 8% of each run, Pallas kernels for 35% -> 27%
where the time goes in v2:
time: 1020 us; the launch traced here: 1010 us
  Pallas kernels  783 us (77%)
  matrix products  95.3 us (9%)
  local copies, waits for them, and re-layouts  54.8 us (5%)
  other arithmetic  53.6 us (5%)
  waiting for transfers between devices  17.6 us (2%)
    pallas_call x3, Pallas kernels, gather(): pl.pallas_call(functools.partial(gather_kernel, grid, parts, count, besid...  399 us
    pallas_call x3, Pallas kernels, scatter(): pl.pallas_call(functools.partial(scatter_kernel, grid, parts, count, besi...  384 us
    unnamed x112, local copies, waits for them, and re-layouts  33.2 us
    dot_general x4, matrix products, outer(): return jnp.einsum('sa,sb->ab', left, right, preferred_element_type=full)  31.8 us
    dot_general x1, matrix products, gathered_body(): projected = jnp.dot(normed, qkv_weight, preferred_element_type=full)  21.4 us
  transfers between devices with their start and end apart: 10, of which 1 were waited for; matrix products, arithmetic and copies ran while one was open for 8% of the time, Pallas kernels for 27%

profile of v2, /device:TPU:8, one launch (start us, length us, event | category | flops | bytes accessed | tf_op | source)
XLA Modules:
  0.0 1010.7 jit_solution(12903702853146288448)
XLA Ops:
  7.4 137.4 %shard_map.195 = (bf16[32,64,6144]{2,1,0:T(8,128)(2,1)S(1)}, bf16[32,64,2048]{2,1,0:T(8,128)(2,1)S(1)}, bf16[32,64,128]{2,1,0:T(8,128)(2,1)S(1)}) custom-call(bf16[64,6144]{1,0:T(8,128)(2,1)S(1)} %copy-done.2, bf16[64,2048]{1,0:T(8,128)(2,1)S(1)} %copy-done.3, bf16[64,128]{1,0:T(8,128)(2,1)S(1)} %maximum_maximum_fusion.1.refs_2_), custom_call_target="tpu_custom_call" | custom-call | tf_op jit(solution)/shard_map/pallas_call | solution.py:535
  144.9 3.3 copy-done.1
  148.2 8.3 copy-done.4
  157.1 21.4 %fusion.43 = f32[256,6144]{1,0:T(8,128)S(1)} fusion(bf16[2048,6144]{1,0:T(8,128)(2,1)} %bitcast.169, bf16[1,256,2048]{2,1,0:T(8,128)(2,1)S(1)} %copy-done.14, f32[2048]{0:T(1024)S(1)} %bitcast.214, f32[256]{0:T(256)S(1)} %fusion.79), kind=kOutput, calls=%fused_computation.81 | convolution fusion | flops 6444548096 | bytes 32515072 | tf_op jit(solution)/shard_map/dot_general | solution.py:1272
  182.5 2.9 copy.125
  185.3 2.9 copy.124
  196.5 3.5 fusion.36
  204.4 134.2 %shard_map.196 = (bf16[16,256,2048]{2,1,0:T(8,128)(2,1)S(1)}, f32[16,40,256]{2,1,0:T(8,128)S(1)}) custom-call(bf16[256,2048]{1,0:T(8,128)(2,1)S(1)} %multiply_convert_fusion.2.refs_0_, f32[40,256]{1,0:T(8,128)S(1)} %select_maximum_fusion.refs_1_), custom_call_target="tpu_custom_call" | custom-call | tf_op jit(solution)/shard_map/pallas_call | solution.py:535
  338.6 5.7 copy-done
  348.0 127.7 %shard_map.197 = (bf16[16,256,2048]{2,1,0:T(8,128)(2,1)}, bf16[2048,2048]{1,0:T(8,128)(2,1)}, f32[2048,1024]{1,0:T(8,128)}, f32[2048,1024]{1,0:T(8,128)}, bf16[2...) custom-call(bf16[256,2048]{1,0:T(8,128)(2,1)} %bitcast.191, ...), custom_call_target="tpu_custom_call" | custom-call | tf_op jit(solution)/shard_map/pallas_call | solution.py:535
  475.7 130.9 %shard_map.198 = (f32[256,2048]{1,0:T(8,128)}, bf16[2048,2048]{1,0:T(8,128)(2,1)}, bf16[2048,1024]{1,0:T(8,128)(2,1)}, bf16[2048,1024]{1,0:T(8,128)(2,1)}, bf16[...) custom-call(bf16[16,256,2048]{2,1,0:T(8,128)(2,1)} %get-tuple-element.44.refs_0_, ...), custom_call_target="tpu_custom_call" | custom-call | tf_op jit(solution)/shard_map/pallas_call | solution.py:701
  608.1 119.6 %shard_map.199 = (f32[256,2048]{1,0:T(8,128)}, f32[16,256]{1,0:T(8,128)}, f32[2048,512]{1,0:T(8,128)}, bf16[2048,512]{1,0:T(8,128)(2,1)}, f32[2048,512]{1,0:T(8,...) custom-call(bf16[16,256,2048]{2,1,0:T(8,128)(2,1)} %get-tuple-element.50.refs_0_, ...), custom_call_target="tpu_custom_call" | custom-call | tf_op jit(solution)/shard_map/pallas_call | solution.py:701
  729.3 3.2 multiply_reduce_fusion.1
  732.6 4.7 fusion.17
  737.3 3.3 convolution_convert_fusion.2
  743.1 4.6 fusion.37
  747.7 4.8 multiply_reduce_fusion
  754.8 4.6 multiply_convert_fusion
  764.6 2.9 copy.121
  767.4 2.9 copy.122
  770.4 4.7 multiply_reduce_fusion.3
  775.2 3.2 fusion.18
  778.4 15.5 %fusion.12 = (f32[2048]{0:T(1024)S(1)}, f32[256]{0:T(256)S(1)}, bf16[256,2048]{1,0:T(8,128)(2,1)}, f32[256,2048]{1,0:T(8,128)}) fusion(bf16[1,256,2048]{2,1,0:T(8,128)(2,1)S(1)} %copy-done.15, f32[256]{0:T(256)S(1)} %copy-done.46, f32[2048]{0:T(1024)S(1)} %bitcast.215, bf16[2048,6144]{1,0:T(8,128)(2,1)} %bitcast.170, bf16[256,2048]{1,0:T(8,128)(2,1)} %copy.123, ...), kind=kOutput, calls=%fused_computation.32 | convolution fusion | flops 6456604672 | bytes 32524288 | tf_op jit(solution)/shard_map/te,de->td/dot_general | solution.py:1380
  794.0 9.5 convolution_convert_fusion
  804.1 3.2 convolution_convert_fusion.1
  815.1 17.6 %collective-permute-done.6 = f32[1024,128]{1,0:T(8,128)} collective-permute-done((f32[1024,128]{1,0:T(8,128)}, f32[1024,128]{1,0:T(8,128)}, u32[]{:S(2)}, u32[]{:S(2)}) %collective-permute-start.6) | collective-permute-done | bytes 524320 | tf_op jit(solution)/shard_map/ppermute | solution.py:1406
  832.9 3.6 fusion.21
  838.4 4.6 add_bitcast_fusion.2
  842.9 4.6 add_bitcast_fusion.1
  850.2 5.5 add_convert_fusion.1
  855.7 13.6 %add_convert_fusion = bf16[1024,6144]{1,0:T(8,128)(2,1)} fusion(bf16[1024,6144]{1,0:T(8,128)(2,1)} %collective-permute-done.4, bf16[256,2048]{1,0:T(8,128)(2,1)} %get-tuple-element.124, s32[]{:T(128)S(6)} %select_n.44, bf16[256,2048]{1,0:T(8,128)(2,1)} %copy.123, bf16[256,2048]{1,0:T(8,128)(2,1)} %copy-done.26, bf16[256,2048]{1,0:T(8,128)(2,1)S(1)} %copy-done.25), kind=kOutput, calls=%fused_computation | convolution fusion | flops 3249537024 | bytes 28835844 | tf_op jit(solution)/shard_map/sa,sb->ab/dot_general | solution.py:1388
  869.3 133.7 %shard_map.200 = (f32[64,6144]{1,0:T(8,128)}, f32[64,2048]{1,0:T(8,128)}, f32[64,128]{1,0:T(8,128)}) custom-call(bf16[16,64,6144]{2,1,0:T(8,128)(2,1)} %bitcast.171, bf16[16,64,2048]{2,1,0:T(8,128)(2,1)} %bitcast.176, f32[16,64,128]{2,1,0:T(8,128)} %bitcast.194), custom_call_target="tpu_custom_call" | custom-call | tf_op jit(solution)/shard_map/pallas_call | solution.py:701
  (194 shorter events, 58.5 us)
Async XLA Ops:
  0.6 5.8 copy-start.2
  0.7 347.3 %collective-permute-start = (bf16[2048,512]{1,0:T(8,128)(2,1)}, bf16[2048,512]{1,0:T(8,128)(2,1)}, u32[]{:S(2)}, u32[]{:S(2)}) collective-permute-start(bf16[2048,512]{1,0:T(8,128)(2,1)} %bitcast.177), channel_id=1, source_target_pairs={{0,16},{16,0},{1,17},{17,1},{2,18},{18,2},{3,19},{19,3},{4,20},{20... | collective-permute-start | bytes 6291464 | tf_op jit(solution)/shard_map/ppermute | solution.py:1256
  0.7 347.2 %collective-permute-start.1 = (bf16[2048,512]{1,0:T(8,128)(2,1)}, bf16[2048,512]{1,0:T(8,128)(2,1)}, u32[]{:S(2)}, u32[]{:S(2)}) collective-permute-start(bf16[2048,512]{1,0:T(8,128)(2,1)} %bitcast.180), channel_id=1, source_target_pairs={{0,16},{16,0},{1,17},{17,1},{2,18},{18,2},{3,19},{19,3},{4,20},{20... | collective-permute-start | bytes 6291464 | tf_op jit(solution)/shard_map/ppermute | solution.py:1256
  1.2 346.7 %collective-permute-start.2 = (bf16[512,2048]{1,0:T(8,128)(2,1)}, bf16[512,2048]{1,0:T(8,128)(2,1)}, u32[]{:S(2)}, u32[]{:S(2)}) collective-permute-start(bf16[512,2048]{1,0:T(8,128)(2,1)} %bitcast.183), channel_id=1, source_target_pairs={{0,16},{16,0},{1,17},{17,1},{2,18},{18,2},{3,19},{19,3},{4,20},{20... | collective-permute-start | bytes 6291464 | tf_op jit(solution)/shard_map/ppermute | solution.py:1256
  3.5 153.6 %copy-start.45 = (f32[256]{0:T(256)}, f32[256]{0:T(256)S(1)}, u32[]{:S(2)}) copy-start(f32[256]{0:T(256)S(1)} %fusion.79) | copy-start | bytes 3076
  7.4 149.6 %copy-start.14 = (bf16[1,256,2048]{2,1,0:T(8,128)(2,1)S(1)}, bf16[1,256,2048]{2,1,0:T(8,128)(2,1)}, u32[]{:S(2)}) copy-start(bf16[1,256,2048]{2,1,0:T(8,128)(2,1)} %param.12) | copy-start | bytes 3145732
  148.2 8.3 copy-start.4
  194.4 5.7 slice-start
  338.6 5.7 copy-start
  344.4 2.9 collective-permute-start.3
  729.3 8.0 slice-start.2
  732.6 4.7 slice-start.3
  743.1 4.6 copy-start.32
  754.8 4.6 copy-start.20
  770.3 4.7 copy-start.43
  770.3 4.8 copy-start.41
  770.3 4.8 copy-start.10
  770.4 4.8 copy-start.11
  778.4 15.6 %copy-start.24 = (bf16[256,2048]{1,0:T(8,128)(2,1)}, bf16[256,2048]{1,0:T(8,128)(2,1)S(1)}, u32[]{:S(2)}) copy-start(bf16[256,2048]{1,0:T(8,128)(2,1)S(1)} %get-tuple-element.110) | copy-start | bytes 3145732
  778.4 15.6 %copy-start.26 = (bf16[256,2048]{1,0:T(8,128)(2,1)}, bf16[256,2048]{1,0:T(8,128)(2,1)S(1)}, u32[]{:S(2)}) copy-start(bf16[256,2048]{1,0:T(8,128)(2,1)S(1)} %get-tuple-element.111) | copy-start | bytes 3145732
  794.0 10.1 copy-start.22
  803.5 52.2 %collective-permute-start.4 = (bf16[1024,6144]{1,0:T(8,128)(2,1)}, bf16[1024,6144]{1,0:T(8,128)(2,1)}, u32[]{:S(2)}, u32[]{:S(2)}) collective-permute-start(bf16[1024,6144]{1,0:T(8,128)(2,1)} %convolution_convert_fusion), channel_id=1, source_target_pairs={{0,16},{16,0},{1,17},{17,1},{2,18},{18,2},{3,19},{19,3},{4,20},{20... | collective-permute-start | bytes 37748744 | tf_op jit(solution)/shard_map/ppermute | solution.py:1406
  803.6 34.8 %collective-permute-start.7 = (bf16[2048,512]{1,0:T(8,128)(2,1)}, bf16[2048,512]{1,0:T(8,128)(2,1)}, u32[]{:S(2)}, u32[]{:S(2)}) collective-permute-start(bf16[2048,512]{1,0:T(8,128)(2,1)} %get-tuple-element.63), channel_id=1, source_target_pairs={{0,16},{16,0},{1,17},{17,1},{2,18},{18,2},{3,19},{19,3},{4,20},{20... | collective-permute-start | bytes 6291464 | tf_op jit(solution)/shard_map/ppermute | solution.py:1344
  807.3 42.9 %collective-permute-start.5 = (bf16[1024,2048]{1,0:T(8,128)(2,1)}, bf16[1024,2048]{1,0:T(8,128)(2,1)}, u32[]{:S(2)}, u32[]{:S(2)}) collective-permute-start(bf16[1024,2048]{1,0:T(8,128)(2,1)} %convolution_convert_fusion.1), channel_id=1, source_target_pairs={{0,16},{16,0},{1,17},{17,1},{2,18},{18,2},{3,19},{19,3},{4,20},{20... | collective-permute-start | bytes 12582920 | tf_op jit(solution)/shard_map/ppermute | solution.py:1406
  810.2 4.9 copy-start.39
  810.2 22.7 %copy-start.16 = (bf16[1,256,2048]{2,1,0:T(8,128)(2,1)S(1)}, bf16[1,256,2048]{2,1,0:T(8,128)(2,1)}, u32[]{:S(2)}) copy-start(bf16[1,256,2048]{2,1,0:T(8,128)(2,1)} %param.12) | copy-start | bytes 3145732
  813.9 18.8 %collective-permute-start.6 = (f32[1024,128]{1,0:T(8,128)}, f32[1024,128]{1,0:T(8,128)}, u32[]{:S(2)}, u32[]{:S(2)}) collective-permute-start(f32[1024,128]{1,0:T(8,128)} %constant_dynamic-slice_fusion), channel_id=1, source_target_pairs={{0,16},{16,0},{1,17},{17,1},{2,18},{18,2},{3,19},{19,3},{4,20},{20... | collective-permute-start | bytes 1572872 | tf_op jit(solution)/shard_map/ppermute | solution.py:1406
  814.4 28.5 %collective-permute-start.8 = (bf16[2048,512]{1,0:T(8,128)(2,1)}, bf16[2048,512]{1,0:T(8,128)(2,1)}, u32[]{:S(2)}, u32[]{:S(2)}) collective-permute-start(bf16[2048,512]{1,0:T(8,128)(2,1)} %get-tuple-element.65), channel_id=1, source_target_pairs={{0,16},{16,0},{1,17},{17,1},{2,18},{18,2},{3,19},{19,3},{4,20},{20... | collective-permute-start | bytes 6291464 | tf_op jit(solution)/shard_map/ppermute | solution.py:1344
  832.7 14.8 %collective-permute-start.9 = (bf16[512,2048]{1,0:T(8,128)(2,1)}, bf16[512,2048]{1,0:T(8,128)(2,1)S(1)}, u32[]{:S(2)}, u32[]{:S(2)}) collective-permute-start(bf16[512,2048]{1,0:T(8,128)(2,1)} %get-tuple-element.67), channel_id=1, source_target_pairs={{0,16},{16,0},{1,17},{17,1},{2,18},{18,2},{3,19},{19,3},{4,20},{20... | collective-permute-start | bytes 6291464 | tf_op jit(solution)/shard_map/ppermute | solution.py:1344
  832.9 5.5 copy-start.29
  850.2 5.5 copy-start.25
  1003.0 5.6 copy-start.33
  (30 other events, 79.5 us)

commit v3 on v2

--- a/solution.py
+++ b/solution.py
@@ -530,7 +530,7 @@
         copy.wait()
 
 
-def gather(arrays, grid, parts, cid, beside=Beside(), vmem=16 << 20):
+def gather(arrays, grid, parts, cid, beside=Beside()):
     n, count = grid.size, len(arrays)
     return pl.pallas_call(
         functools.partial(gather_kernel, grid, parts, count, beside),
@@ -544,7 +544,7 @@
         ]
         + list(beside.scratch),
         compiler_params=pltpu.CompilerParams(
-            collective_id=cid, has_side_effects=True, vmem_limit_bytes=vmem
+            collective_id=cid, has_side_effects=True, vmem_limit_bytes=60 << 20
         ),
     )(*arrays, *beside.ins)
 
@@ -725,7 +725,7 @@
 
 
 def each_tile(total, width, f):
-    @pl.loop(0, total // width)
+    @pl.loop(0, total // width, unroll=4)
     def _(t):
         f(pl.ds(pl.multiple_of(t * width, width), width))
 
@@ -906,27 +906,35 @@
             pltpu.SemaphoreType.DMA((6,)),
         ],
         steps=steps,
-        lead=0.2,
-        span=0.5,
-    )
-
-
-def backward_beside(cot_rows, rank_rows, rank_cols, weight_rows, gate_pre, up_pre, expert_out, halves, capacity):
-    row_count, tokens, width = cot_rows.shape
+        lead=0.3,
+        span=0.6,
+    )
+
+
+def backward_beside(cot_early, cot_late, rank_rows, rank_cols, weight_rows, gate_pre, up_pre, expert_out, halves, capacity):
+    row_count, late, width = cot_late.shape
+    early = cot_early.shape[1]
+    tokens = early + late
     hidden = 2 * halves[0].shape[1]
     pairs, pair = row_count // 2, 2 * capacity
     slots = row_count * capacity
     low, full = jnp.bfloat16, jnp.float32
 
     def steps(ins, outs, scratch):
-        cot_in, ranks, ranks_t, weights, gate_in, up_in, out_in = ins[:7]
+        early_in, late_in, ranks, ranks_t, weights, gate_in, up_in, out_in = ins[:8]
         heavy_refs, (cot, ge, pre, out, gg, gu, gx, dots, sums), sems = scratch[:3], scratch[3:12], scratch[12:]
         load_sem, row_sem, out_sem = sems
-        heavy = weight_copies(ins[7:], heavy_refs, load_sem)
+        heavy = weight_copies(ins[8:], heavy_refs, load_sem)
         gate_w, up_w, down_w = heavy_refs
 
+        first = lax.axis_index("dp") * row_count
+
         def load(q):
-            return Move(cot_in.at[pl.ds(2 * q, 2)], cot.at[q % 2], row_sem.at[q % 2])
+            held = cot.at[q % 2]
+            return [
+                Move(early_in.at[pl.ds(first + 2 * q, 2)], held.at[:, pl.ds(0, early)], row_sem.at[q % 2]),
+                Move(late_in.at[pl.ds(2 * q, 2)], held.at[:, pl.ds(early, late)], row_sem.at[5 + q % 2]),
+            ]
 
         def fetch(q):
             here = pl.ds(q * pair, pair)
@@ -942,17 +950,20 @@
         last = Move(dots, outs[4], out_sem.at[4])
 
         def opening():
-            load(0).start()
+            for copy in load(0):
+                copy.start()
             for copy in fetch(0):
                 copy.start()
             for copy in heavy:
                 copy.start()
 
         def choose(q):
-            load(q).wait()
+            for copy in load(q):
+                copy.wait()
             fetch(q)[0].wait()
             if q + 1 < pairs:
-                load(q + 1).start()
+                for copy in load(q + 1):
+                    copy.start()
             if q:
                 leave(q - 1)[0].wait()
             for i in range(2):
@@ -1030,8 +1041,8 @@
         return listed + [closing]
 
     return Beside(
-        ins=(cot_rows, rank_rows, rank_cols, weight_rows, gate_pre, up_pre, expert_out) + tuple(halves),
-        in_specs=(ANYWHERE, ON_CORE, ON_CORE, ON_CORE) + (ANYWHERE,) * 9,
+        ins=(cot_early, cot_late, rank_rows, rank_cols, weight_rows, gate_pre, up_pre, expert_out) + tuple(halves),
+        in_specs=(ANYWHERE, ANYWHERE, ON_CORE, ON_CORE, ON_CORE) + (ANYWHERE,) * 9,
         outs=[
             jax.ShapeDtypeStruct((slots, width), low),
             jax.ShapeDtypeStruct((slots, hidden), low),
@@ -1053,7 +1064,7 @@
             pltpu.VMEM((row_count, tokens), full),
             pltpu.VMEM((capacity, 128), full),
             pltpu.SemaphoreType.DMA((6,)),
-            pltpu.SemaphoreType.DMA((5,)),
+            pltpu.SemaphoreType.DMA((7,)),
             pltpu.SemaphoreType.DMA((5,)),
         ],
         steps=steps,
@@ -1199,6 +1210,254 @@
     )
 
 
+def turn_half(values):
+    return pltpu.roll(values, values.shape[1] // 2, 1)
+
+
+def attend_beside(tokens, gain_rows, qkv_weight, live_row, cosine, sine):
+    row_count, width = tokens.shape
+    low, full = jnp.bfloat16, jnp.float32
+    block, group, strip = 256, 2, 32
+    tiles, per_part = 3 * width // block, width // block
+    score_scale = HEAD ** (-0.5)
+
+    def steps(ins, outs, scratch):
+        tokens_ref, gains, weight, live, cos, sin = ins
+        normed, proj, panel, queries, keys, values, mixed, probs, scale, panel_sem, out_sem, probs_sem = scratch
+
+        def load(t):
+            return Move(weight.at[:, pl.ds(t * block, block)], panel.at[t % 3], panel_sem.at[t % 3])
+
+        leaves = [
+            Move(ref, outs[i], out_sem.at[i])
+            for i, ref in enumerate((normed, proj.at[:, pl.ds(0, 2 * width)], queries, keys, values, mixed))
+        ]
+
+        def leave_probs(n):
+            return Move(probs.at[n % 2], outs[6].at[pl.ds(n * group, group)], probs_sem.at[n % 2])
+
+        def opening():
+            load(0).start()
+            load(1).start()
+
+            @pl.loop(0, row_count // strip)
+            def _(k):
+                here = pl.ds(pl.multiple_of(k * strip, strip), strip)
+                value = tokens_ref[here, :].astype(full)
+                value = value * lax.rsqrt(jnp.mean(value * value, axis=1, keepdims=True) + NORM_EPS)
+                normed[here, :] = (value * gains[0:1, :]).astype(low)
+
+            leaves[0].start()
+
+        def project(t):
+            load(t).wait()
+            if t + 2 < tiles:
+                load(t + 2).start()
+            proj[:, t * block : (t + 1) * block] = dot(normed[...], panel[t % 3])
+
+        def measure(part):
+            @pl.loop(0, row_count // strip)
+            def _(k):
+                here = pl.ds(pl.multiple_of(k * strip, strip), strip)
+                value = proj[here, part * width : (part + 1) * width]
+                inverse = lax.rsqrt(jnp.mean(value * value, axis=1, keepdims=True) + NORM_EPS)
+                scale[part, here, :] = jnp.broadcast_to(inverse, (strip, HEAD))
+
+        def attend(n):
+            if n == 0:
+                leaves[1].start()
+            if n >= 2:
+                leave_probs(n - 2).wait()
+            query_slot = lax.broadcasted_iota(jnp.int32, (row_count, row_count), 0)
+            key_slot = lax.broadcasted_iota(jnp.int32, (row_count, row_count), 1)
+            allowed = (key_slot <= query_slot) & (live[...] > 0.5)
+
+            @pl.loop(0, group)
+            def _(i):
+                head = n * group + i
+                cols = pl.ds(pl.multiple_of(head * HEAD, HEAD), HEAD)
+
+                def place(part, gain):
+                    there = pl.ds(pl.multiple_of(part * width + head * HEAD, HEAD), HEAD)
+                    value = proj[:, there] * scale[part] * gains[gain : gain + 1, cols]
+                    return (value * cos[...] + turn_half(value) * sin[...]).astype(low)
+
+                query, key = place(0, 1), place(1, 2)
+                value = proj[:, pl.ds(pl.multiple_of(2 * width + head * HEAD, HEAD), HEAD)].astype(low)
+                queries[:, cols], keys[:, cols], values[:, cols] = query, key, value
+                score = jnp.where(allowed, dot_across(query, key) * score_scale, -1e30)
+                expo = jnp.exp(score - jnp.max(score, axis=1, keepdims=True))
+                prob = expo / jnp.sum(expo, axis=1, keepdims=True)
+                probs[n % 2, i] = prob
+                mixed[:, cols] = dot(prob.astype(low), value).astype(low)
+
+            leave_probs(n).start()
+
+        def closing():
+            for move in leaves[2:]:
+                move.start()
+            for move in leaves:
+                move.wait()
+            for n in range(HEADS // group - 2, HEADS // group):
+                leave_probs(n).wait()
+
+        listed = [opening] + [functools.partial(project, t) for t in range(tiles)]
+        listed += [functools.partial(measure, 0), functools.partial(measure, 1)]
+        return listed + [functools.partial(attend, n) for n in range(HEADS // group)] + [closing]
+
+    shape = (row_count, width)
+    return Beside(
+        ins=(tokens, gain_rows, qkv_weight, live_row, cosine, sine),
+        in_specs=(ON_CORE, ON_CORE, ANYWHERE, ON_CORE, ON_CORE, ON_CORE),
+        outs=[
+            jax.ShapeDtypeStruct(shape, low),
+            jax.ShapeDtypeStruct((row_count, 2 * width), full),
+            jax.ShapeDtypeStruct(shape, low),
+            jax.ShapeDtypeStruct(shape, low),
+            jax.ShapeDtypeStruct(shape, low),
+            jax.ShapeDtypeStruct(shape, low),
+            jax.ShapeDtypeStruct((HEADS, row_count, row_count), full),
+        ],
+        scratch=[
+            pltpu.VMEM(shape, low),
+            pltpu.VMEM((row_count, 3 * width), full),
+            pltpu.VMEM((3, width, block), low),
+            pltpu.VMEM(shape, low),
+            pltpu.VMEM(shape, low),
+            pltpu.VMEM(shape, low),
+            pltpu.VMEM(shape, low),
+            pltpu.VMEM((2, group, row_count, row_count), full),
+            pltpu.VMEM((2, row_count, HEAD), full),
+            pltpu.SemaphoreType.DMA((3,)),
+            pltpu.SemaphoreType.DMA((6,)),
+            pltpu.SemaphoreType.DMA((2,)),
+        ],
+        steps=steps,
+        lead=0.2,
+        span=0.6,
+    )
+
+
+def attend_back_beside(grad_attn, out_weight, queries, keys, values, probs, parts, gain_rows, cosine, sine):
+    row_count, width = grad_attn.shape
+    low, full = jnp.bfloat16, jnp.float32
+    block, group, strip = 256, 2, 32
+    score_scale = HEAD ** (-0.5)
+    across_rows = (((0,), (0,)), ((), ()))
+
+    def steps(ins, outs, scratch):
+        grad_ref, weight, query_ref, key_ref, value_ref, probs_in, parts_ref, gains, cos, sin = ins
+        grad_mixed, grads, panel, prob_ref, projected, sums, panel_sem, probs_sem, out_sem = scratch
+        tiles = width // block
+
+        def load(t):
+            return Move(weight.at[pl.ds(t * block, block)], panel.at[t % 3], panel_sem.at[t % 3])
+
+        def load_probs(n):
+            return Move(probs_in.at[pl.ds(n * group, group)], prob_ref.at[n % 2], probs_sem.at[n % 2])
+
+        leaves = [Move(projected, outs[0], out_sem.at[0]), Move(sums, outs[1], out_sem.at[1])]
+
+        def opening():
+            load(0).start()
+            load(1).start()
+            load_probs(0).start()
+
+        def unmix(t):
+            load(t).wait()
+            if t + 2 < tiles:
+                load(t + 2).start()
+            grad_mixed[:, t * block : (t + 1) * block] = dot_across(grad_ref[...], panel[t % 3]).astype(low)
+
+        def attend(n):
+            load_probs(n).wait()
+            if n + 1 < HEADS // group:
+                load_probs(n + 1).start()
+
+            @pl.loop(0, group)
+            def _(i):
+                head = n * group + i
+                cols = pl.ds(pl.multiple_of(head * HEAD, HEAD), HEAD)
+                prob, grad = prob_ref[n % 2, i], grad_mixed[:, cols]
+                grad_value = lax.dot_general(prob.astype(low), grad, across_rows, preferred_element_type=full)
+                there = pl.ds(pl.multiple_of(2 * width + head * HEAD, HEAD), HEAD)
+                projected[:, there] = grad_value.astype(low)
+                grad_prob = dot_across(grad, value_ref[:, cols])
+                centre = jnp.sum(prob * grad_prob, axis=1, keepdims=True)
+                grad_score = (prob * (grad_prob - centre)).astype(low)
+                grad_query = dot(grad_score, key_ref[:, cols]) * score_scale
+                grad_key = lax.dot_general(grad_score, query_ref[:, cols], across_rows, preferred_element_type=full)
+                for part, value in enumerate((grad_query, grad_key * score_scale)):
+                    grads[part, :, cols] = value * cos[...] - turn_half(value) * sin[...]
+
+        def settle(part):
+            sums[part] = jnp.zeros((8, width), full)
+
+            @pl.loop(0, row_count // strip)
+            def _(k):
+                here = pl.ds(pl.multiple_of(k * strip, strip), strip)
+                value = parts_ref[here, part * width : (part + 1) * width]
+                inverse = lax.rsqrt(jnp.mean(value * value, axis=1, keepdims=True) + NORM_EPS)
+                unit = value * inverse
+                grad = grads[part, here, :]
+                product = grad * unit
+                total = product[0:8]
+                for first in range(8, strip, 8):
+                    total = total + product[first : first + 8]
+                sums[part] += total
+                grad = grad * gains[part + 1 : part + 2, :]
+                grad = inverse * (grad - unit * jnp.mean(grad * unit, axis=1, keepdims=True))
+                projected[here, part * width : (part + 1) * width] = grad.astype(low)
+
+        def closing():
+            for move in leaves:
+                move.start()
+            for move in leaves:
+                move.wait()
+
+        listed = [opening] + [functools.partial(unmix, t) for t in range(tiles)]
+        listed += [functools.partial(attend, n) for n in range(HEADS // group)]
+        return listed + [functools.partial(settle, part) for part in range(2)] + [closing]
+
+    shape = (row_count, width)
+    return Beside(
+        ins=(grad_attn, out_weight, queries, keys, values, probs, parts, gain_rows, cosine, sine),
+        in_specs=(ON_CORE, ANYWHERE, ON_CORE, ON_CORE, ON_CORE, ANYWHERE, ON_CORE, ON_CORE, ON_CORE, ON_CORE),
+        outs=[
+            jax.ShapeDtypeStruct((row_count, 3 * width), low),
+            jax.ShapeDtypeStruct((2, 8, width), full),
+        ],
+        scratch=[
+            pltpu.VMEM(shape, low),
+            pltpu.VMEM((2,) + shape, full),
+            pltpu.VMEM((3, block, width), low),
+            pltpu.VMEM((2, group, row_count, row_count), full),
+            pltpu.VMEM((row_count, 3 * width), low),
+            pltpu.VMEM((2, 8, width), full),
+            pltpu.SemaphoreType.DMA((3,)),
+            pltpu.SemaphoreType.DMA((2,)),
+            pltpu.SemaphoreType.DMA((2,)),
+        ],
+        steps=steps,
+    )
+
+
+def alone(beside):
+    def kernel(*refs):
+        a, b = len(beside.ins), len(beside.ins) + len(beside.outs)
+        for step in beside.steps(refs[:a], refs[a:b], refs[b:]):
+            step()
+
+    return pl.pallas_call(
+        kernel,
+        out_shape=beside.outs,
+        in_specs=list(beside.in_specs),
+        out_specs=[ANYWHERE] * len(beside.outs),
+        scratch_shapes=list(beside.scratch),
+        compiler_params=pltpu.CompilerParams(vmem_limit_bytes=40 << 20),
+    )(*beside.ins)
+
+
 def gathered_body(
     dims,
     tokens,
@@ -1222,7 +1481,6 @@
     capacity = row_count * top_count // expert_count
     slots_all = row_count * 2 * owners
     balance_factor = float(expert_count) / (float(top_count) * float(slots_all) * float(slots_all))
-    score_scale = HEAD ** (-0.5)
     low = jnp.bfloat16
     full = jnp.float32
     chips = Grid(dims)
@@ -1232,6 +1490,8 @@
     row_shares = [5 * row_count // 16, 5 * row_count // 16, 3 * row_count // 16, 3 * row_count // 16]
     quarter = [weight_rows // 4] * 4
     wide_orders = [tuple(d + 1 for d in order) + (0,) for order in row_orders]
+    late_shares = [row_count // 4, row_count // 4, row_count // 8, row_count // 8]
+    narrow_orders = [order[:-1] for order in wide_orders]
     expert = lax.axis_index("expert")
     core = lax.axis_index("dp")
     swap = [(0, 1), (1, 0)]
@@ -1239,19 +1499,13 @@
     small = jnp.concatenate(
         [w_router, gains.T, jnp.zeros((weight_rows, 128 - expert_count - 4), low)], axis=1
     )
-    qkv_all, out_all, small_all = gather(
-        [w_qkv, w_out, small],
-        devices,
-        cut(0, quarter, wide_orders)
-        + cut(1, quarter, wide_orders[:2] * 2)
-        + cut(2, [weight_rows], wide_orders[2:3]),
-        1,
-    )
-    qkv_weight = qkv_all.reshape(D, 3 * D)
-    out_weight = out_all.reshape(D, D)
+    qkv_all, small_all = gather(
+        [w_qkv, small], devices, cut(0, quarter, wide_orders) + cut(1, [weight_rows], wide_orders[2:3]), 1
+    )
     small_all = small_all.reshape(D, 128)
     router_weight = small_all[:, :expert_count]
     gain_float = small_all[:, expert_count : expert_count + 4].T.astype(full)
+    qkv_weight = qkv_all.reshape(D, 3 * D)
     gate_own, up_own, down_own = w_gate[0], w_up[0], w_down[0]
     gate_far, up_far, down_far = (lax.ppermute(w, "dp", swap) for w in (gate_own, up_own, down_own))
 
@@ -1266,26 +1520,19 @@
     kept = named & (rank < limit[None, :])
     kept_rank = jnp.where(kept, rank, -1.0)
 
+    cosine, sine = (table[:, 0] for table in rope_tables(row_count, HEAD))
+    sine = jnp.concatenate([-sine[:, : HEAD // 2], sine[:, HEAD // 2 :]], axis=1)
+    early = row_count // 4
+    out_all, cot_early, normed, qk_parts, queries, keys_low, values_low, mixed_low, probs = gather(
+        [w_out, cotangent[0, :early]],
+        devices,
+        cut(0, quarter, wide_orders) + cut(1, [early // 4] * 4, narrow_orders),
+        7,
+        attend_beside(tokens[0], gain_float, qkv_weight, live_slots[None, :].astype(full), cosine, sine),
+    )
+    out_weight = out_all.reshape(D, D)
     inputs = tokens[0].astype(full)
-    attn_in, attn_norm_back = jax.vjp(norm_scale, inputs, gain_float[0])
-    normed = attn_in.astype(low)
-    projected = jnp.dot(normed, qkv_weight, preferred_element_type=full)
-    (rot_query, rot_keys), query_key_back = jax.vjp(
-        query_key, projected[:, :D], projected[:, D : 2 * D], gain_float[1], gain_float[2]
-    )
-    queries = rot_query.astype(low)
-    keys_low = rot_keys.astype(low)
-    values_low = projected[:, 2 * D :].astype(low).reshape(row_count, HEADS, HEAD)
-    allowed = (positions[None, :] <= positions[:, None]) & live_slots[None, :]
-    scores = jnp.einsum("qhd,khd->hqk", queries, keys_low, preferred_element_type=full) * score_scale
-    scores = jnp.where(allowed[None], scores, -1e30)
-    highest = jnp.max(scores, axis=-1, keepdims=True)
-    expo_scores = jnp.exp(scores - highest)
-    totals = jnp.sum(expo_scores, axis=-1, keepdims=True)
-    attn_probs = expo_scores / totals
-    log_total = highest + jnp.log(totals)
-    mixed_heads = jnp.einsum("hqk,khd->qhd", attn_probs.astype(low), values_low, preferred_element_type=full)
-    mixed_low = mixed_heads.reshape(row_count, D).astype(low)
+    _, attn_norm_back = jax.vjp(norm_scale, inputs, gain_float[0])
     hidden_state = inputs + jnp.dot(mixed_low, out_weight, preferred_element_type=full)
     ffn_in, ffn_norm_back = jax.vjp(norm_scale, hidden_state, gain_float[3])
     ffn_low = ffn_in.astype(low)
@@ -1315,13 +1562,12 @@
     weight_of = lax.dynamic_index_in_dim(aside_rows, expert, 1, keepdims=False)
     rank_of = lax.dynamic_index_in_dim(aside_rows, expert_count + expert, 1, keepdims=False)
     halves = (gate_own, gate_far, up_own, up_far, down_own, down_far)
-    cot_rows, rows_in, gate_pre, up_pre, units, expert_out, mixture_part = gather(
-        [cotangent[0]],
+    cot_late, rows_in, gate_pre, up_pre, units, expert_out, mixture_part = gather(
+        [cotangent[0, early:]],
         chips,
-        cut(0, row_shares, row_orders),
+        cut(0, late_shares, row_orders),
         2,
         forward_beside(ffn_rows, rank_of, rank_of.T, weight_of.T, halves, capacity),
-        vmem=60 << 20,
     )
     mixture, grad_rows, grad_gate, grad_up, back_part, dot_route = scatter(
         [mixture_part],
@@ -1329,7 +1575,7 @@
         cut(0, row_shares, row_orders),
         5,
         backward_beside(
-            cot_rows, rank_of, rank_of.T, weight_of, gate_pre, up_pre, expert_out, halves, capacity
+            cot_early, cot_late, rank_of, rank_of.T, weight_of, gate_pre, up_pre, expert_out, halves, capacity
         ),
     )
     route_part = jnp.where((expert_ids == expert)[None, :, None], dot_route[:, None, :], 0.0)
@@ -1359,62 +1605,33 @@
     grad_hidden_part, grad_gain_ffn = ffn_norm_back(grad_ffn)
     grad_hidden_state = grad_layer + grad_hidden_part
     grad_attn_low = grad_hidden_state.astype(low)
-    grad_mixed = jnp.einsum("te,de->td", grad_attn_low, out_weight, preferred_element_type=full)
-    grad_mixed = grad_mixed.astype(low).reshape(row_count, HEADS, HEAD)
-    scores_again = jnp.einsum("qhd,khd->hqk", queries, keys_low, preferred_element_type=full) * score_scale
-    probs_again = jnp.where(allowed[None], jnp.exp(scores_again - log_total), 0.0)
-    grad_values = jnp.einsum("hqk,qhd->khd", probs_again.astype(low), grad_mixed, preferred_element_type=full)
-    grad_attn_probs = jnp.einsum("qhd,khd->hqk", grad_mixed, values_low, preferred_element_type=full)
-    grad_scores = probs_again * (
-        grad_attn_probs - jnp.sum(probs_again * grad_attn_probs, axis=-1, keepdims=True)
-    )
-    grad_scores_low = grad_scores.astype(low)
-    grad_queries = jnp.einsum("hqk,khd->qhd", grad_scores_low, keys_low, preferred_element_type=full) * score_scale
-    grad_keys = jnp.einsum("hqk,qhd->khd", grad_scores_low, queries, preferred_element_type=full) * score_scale
-    grad_query_part, grad_key_part, grad_gain_query, grad_gain_key = query_key_back(
-        (grad_queries, grad_keys)
-    )
-    grad_projected = jnp.concatenate(
-        [grad_query_part, grad_key_part, grad_values.reshape(row_count, D)], axis=1
-    ).astype(low)
+    grad_projected, head_sums = alone(
+        attend_back_beside(
+            grad_attn_low, out_weight, queries, keys_low, values_low, probs, qk_parts, gain_float, cosine, sine
+        )
+    )
+    grad_gain_query, grad_gain_key = jnp.sum(head_sums, axis=1)
     grad_normed = jnp.einsum("te,de->td", grad_projected, qkv_weight, preferred_element_type=full)
     grad_input_part, grad_gain_attn = attn_norm_back(grad_normed)
     grad_inputs = grad_hidden_state + grad_input_part
     grad_gain_rows = jnp.stack([grad_gain_attn, grad_gain_query, grad_gain_key, grad_gain_ffn])
 
-    half = D // 2
-
     def outer(left, right):
         return jnp.einsum("sa,sb->ab", left, right, preferred_element_type=full)
 
-    def core_half(value, side):
-        return lax.dynamic_slice_in_dim(value, side * half, half, 1)
-
     small_grads = jnp.concatenate(
         [grad_router_w, grad_gain_rows.T, jnp.zeros((D, 128 - expert_count - 4), full)], axis=1
     )
-
-    def mixer_grads(side):
-        return (
-            outer(core_half(normed, side), grad_projected),
-            outer(core_half(mixed_low, side), grad_attn_low),
-            lax.dynamic_slice_in_dim(small_grads, side * half, half, 0),
-        )
-
-    far_qkv, far_out, far_small = mixer_grads(1 - core)
-    far_parts = [
-        lax.ppermute(g, "dp", swap) for g in (far_qkv.astype(low), far_out.astype(low), far_small)
-    ]
     shares = [
-        (a + b.astype(full)).astype(b.dtype).reshape(owners, weight_rows, a.shape[1])
-        for a, b in zip(mixer_grads(core), far_parts)
+        g.reshape(devices.size, weight_rows, g.shape[1])
+        for g in (outer(normed, grad_projected).astype(low), outer(mixed_low, grad_attn_low).astype(low), small_grads)
     ]
     grad_qkv, grad_out, grad_small = scatter(
         shares,
-        chips,
-        cut(0, quarter, row_orders)
-        + cut(1, quarter, row_orders[:2] * 2)
-        + cut(2, [weight_rows], row_orders[2:3]),
+        devices,
+        cut(0, quarter, wide_orders)
+        + cut(1, quarter, wide_orders[:2] * 2)
+        + cut(2, [weight_rows], wide_orders[2:3]),
         6,
     )
     return (

time: 1020 us -> 946 us (0.927)
  Pallas kernels: 783 us -> 836 us
  matrix products: 95.3 us -> 43.7 us
  local copies, waits for them, and re-layouts: 54.8 us -> 21 us
  other arithmetic: 53.6 us -> 34.1 us
  waiting for transfers between devices: 17.6 us -> 0.02 us
    dot_general x8 -> x0, matrix products: 40.2 us -> none  [the longest x1 21.4 us: gathered_body(): projected = jnp.dot(normed, qkv_weight, preferred_element_type=full)]
    pallas_call x0 -> x1, Pallas kernels: none -> 23.5 us  [alone(): pl.pallas_call(kernel, out_shape=beside.outs, in_specs=list(beside.in_spe...]
    unnamed x112 -> x64, local copies, waits for them, and re-layouts: 33.2 us -> 11.8 us
    pallas_call x3 -> x4, Pallas kernels: 399 us -> 419 us  [gather(): pl.pallas_call(functools.partial(gather_kernel, grid, parts, count, besid...]
    ppermute x3 -> x0, waiting for transfers between devices: 17.6 us -> none  [gathered_body(): lax.ppermute(g, 'dp', swap)]
    reshape x6 -> x0, local copies, waits for them, and re-layouts: 16.2 us -> none  [the longest x2 5.78 us: query_key(): norm_scale(key_part, key_gain).reshape(positions_count, HEADS, HEAD)]
    dot_general x4 -> x2, matrix products: 31.8 us -> 20.7 us  [outer(): return jnp.einsum('sa,sb->ab', left, right, preferred_element_type=full)]
  transfers between devices with their start and end apart: 10 -> 7, of which waited for: 1 -> 0; matrix products, arithmetic and copies ran while one was open for 8% -> 8% of each run, Pallas kernels for 27% -> 48%
where the time goes in v3:
time: 946 us; the launch traced here: 939 us
  Pallas kernels  836 us (88%)
  matrix products  43.7 us (5%)
  other arithmetic  34.1 us (4%)
  local copies, waits for them, and re-layouts  21 us (2%)
    pallas_call x4, Pallas kernels, gather(): pl.pallas_call(functools.partial(gather_kernel, grid, parts, count, besid...  419 us
    pallas_call x3, Pallas kernels, scatter(): pl.pallas_call(functools.partial(scatter_kernel, grid, parts, count, besi...  393 us
    pallas_call x1, Pallas kernels, alone(): pl.pallas_call(kernel, out_shape=beside.outs, in_specs=list(beside.in_spe...  23.5 us
    dot_general x2, matrix products, outer(): return jnp.einsum('sa,sb->ab', left, right, preferred_element_type=full)  20.7 us
  transfers between devices with their start and end apart: 7, of which 0 were waited for; matrix products, arithmetic and copies ran while one was open for 8% of the time, Pallas kernels for 48%

profile of v3, /device:TPU:8, one launch (start us, length us, event | category | flops | bytes accessed | tf_op | source)
XLA Modules:
  0.0 939.4 jit_solution(14970405672038706609)
XLA Ops:
  4.9 1.2 fusion.14
  6.2 1.7 slice_bitcast_fusion.1.refs_1_
  8.6 106.1 %shard_map.195 = (bf16[32,64,6144]{2,1,0:T(8,128)(2,1)}, bf16[32,64,128]{2,1,0:T(8,128)(2,1)}) custom-call(bf16[64,6144]{1,0:T(8,128)(2,1)} %refs_0_.2, bf16[64,128]{1,0:T(8,128)(2,1)} %maximum_maximum_fusion.1.refs_1_), custom_call_target="tpu_custom_call" | custom-call | tf_op jit(solution)/shard_map/pallas_call | solution.py:535
  114.8 1.2 slice_convert_fusion
  117.1 80.5 %shard_map.196 = (bf16[32,64,2048]{2,1,0:T(8,128)(2,1)}, bf16[32,64,2048]{2,1,0:T(8,128)(2,1)}, bf16[256,2048]{1,0:T(8,128)(2,1)}, f32[256,4096]{1,0:T(8,128)}, ...) custom-call(bf16[64,2048]{1,0:T(8,128)(2,1)} %refs_0_.3, ...), custom_call_target="tpu_custom_call" | custom-call | tf_op jit(solution)/shard_map/pallas_call | solution.py:535
  197.6 6.2 multiply_reduce_fusion.2
  206.4 130.2 %shard_map.197 = (bf16[16,256,2048]{2,1,0:T(8,128)(2,1)}, f32[16,40,256]{2,1,0:T(8,128)}) custom-call(bf16[256,2048]{1,0:T(8,128)(2,1)} %copy-done.9, f32[40,256]{1,0:T(8,128)} %select_maximum_fusion.refs_1_), custom_call_target="tpu_custom_call" | custom-call | tf_op jit(solution)/shard_map/pallas_call | solution.py:535
  337.6 1.0 constant_dynamic-slice_fusion
  341.3 1.5 fusion.3
  342.8 2.1 slice_bitcast_fusion.refs_0_
  346.4 102.5 %shard_map.198 = (bf16[16,192,2048]{2,1,0:T(8,128)(2,1)}, bf16[2048,2048]{1,0:T(8,128)(2,1)}, f32[2048,1024]{1,0:T(8,128)}, f32[2048,1024]{1,0:T(8,128)}, bf16[2...) custom-call(bf16[192,2048]{1,0:T(8,128)(2,1)} %slice_bitcast_fusion.refs_0_, ...), custom_call_target="tpu_custom_call" | custom-call | tf_op jit(solution)/shard_map/pallas_call | solution.py:535
  448.9 133.3 %shard_map.199 = (f32[256,2048]{1,0:T(8,128)}, bf16[2048,2048]{1,0:T(8,128)(2,1)}, bf16[2048,1024]{1,0:T(8,128)(2,1)}, bf16[2048,1024]{1,0:T(8,128)(2,1)}, bf16[...) custom-call(bf16[16,256,2048]{2,1,0:T(8,128)(2,1)} %get-tuple-element.55.refs_0_, ...), custom_call_target="tpu_custom_call" | custom-call | tf_op jit(solution)/shard_map/pallas_call | solution.py:701
  582.2 1.5 broadcast_select_fusion.refs_1_
  583.7 121.5 %shard_map.200 = (f32[256,2048]{1,0:T(8,128)}, f32[16,256]{1,0:T(8,128)}, f32[2048,512]{1,0:T(8,128)}, bf16[2048,512]{1,0:T(8,128)(2,1)}, f32[2048,512]{1,0:T(8,...) custom-call(bf16[16,256,2048]{2,1,0:T(8,128)(2,1)} %get-tuple-element.62.refs_0_, ...), custom_call_target="tpu_custom_call" | custom-call | tf_op jit(solution)/shard_map/pallas_call | solution.py:701
  705.2 1.0 multiply_reduce_fusion.3
  707.0 1.5 fusion.27
  710.4 2.7 fusion.23
  713.1 0.9 copy-done.4
  714.7 23.5 %shard_map.201 = (bf16[256,6144]{1,0:T(8,128)(2,1)S(1)}, f32[2,8,2048]{2,1,0:T(8,128)S(1)}) custom-call(bf16[256,2048]{1,0:T(8,128)(2,1)S(1)} %get-tuple-element.132.refs_0_, bf16[2048,2048]{1,0:T(8,128)(2,1)} %bitcast.111, bf16[256,2048]{1,0:T(8,128)(2,1)S(1)} %copy-done.4, bf16[256,2048]{1,0:T(8,128)(2,1)S(1)} %copy-done.5, ...), custom_call_target="tpu_custom_call" | custom-call | tf_op jit(solution)/shard_map/pallas_call | solution.py:1451
  738.2 1.7 copy-done.1
  740.6 13.7 %convolution_convert_fusion = bf16[2048,6144]{1,0:T(8,128)(2,1)} fusion(bf16[256,2048]{1,0:T(8,128)(2,1)S(1)} %copy-done.24, bf16[256,6144]{1,0:T(8,128)(2,1)} %copy-done.1), kind=kOutput, calls=%fused_computation | convolution fusion | flops 6455033856 | bytes 29360128 | tf_op jit(solution)/shard_map/sa,sb->ab/dot_general | solution.py:1620
  754.3 13.9 %fusion.6 = (f32[2048]{0:T(1024)S(1)}, f32[256]{0:T(256)S(1)}, f32[256,2048]{1,0:T(8,128)}) fusion(f32[256]{0:T(256)S(1)} %fusion.21, bf16[1,256,2048]{2,1,0:T(8,128)(2,1)S(1)} %copy-done.12, f32[2048]{0:T(1024)S(1)} %bitcast.127, bf16[256,6144]{1,0:T(8,128)(2,1)} %copy-done.1, bf16[2048,6144]{1,0:T(8,128)(2,1)} %bitcast.99), kind=kOutput, calls=%fused_computation.18 | convolution fusion | flops 6446118912 | bytes 31475712 | tf_op jit(solution)/shard_map/te,de->td/dot_general | solution.py:1614
  768.2 1.3 copy.66
  769.6 7.0 convolution_convert_fusion.1
  776.5 1.3 maximum_maximum_fusion
  777.9 137.9 %shard_map.202 = (f32[64,6144]{1,0:T(8,128)}, f32[64,2048]{1,0:T(8,128)}, f32[64,128]{1,0:T(8,128)}) custom-call(bf16[32,64,6144]{2,1,0:T(8,128)(2,1)} %bitcast.96, bf16[32,64,2048]{2,1,0:T(8,128)(2,1)} %bitcast.97, f32[32,64,128]{2,1,0:T(8,128)} %bitcast.115), custom_call_target="tpu_custom_call" | custom-call | tf_op jit(solution)/shard_map/pallas_call | solution.py:701
  916.6 1.4 copy.67
  918.7 3.6 fusion.2
  922.3 4.6 add_bitcast_fusion.2
  926.9 4.6 add_bitcast_fusion.1
  931.5 4.4 add_bitcast_fusion
  935.9 1.1 copy.83
  (111 shorter events, 19.1 us)
Async XLA Ops:
  0.6 345.7 %collective-permute-start = (bf16[2048,512]{1,0:T(8,128)(2,1)}, bf16[2048,512]{1,0:T(8,128)(2,1)}, u32[]{:S(2)}, u32[]{:S(2)}) collective-permute-start(bf16[2048,512]{1,0:T(8,128)(2,1)} %bitcast.101), channel_id=1, source_target_pairs={{0,16},{16,0},{1,17},{17,1},{2,18},{18,2},{3,19},{19,3},{4,20},{20... | collective-permute-start | bytes 6291464 | tf_op jit(solution)/shard_map/ppermute | solution.py:1510
  0.7 345.6 %collective-permute-start.1 = (bf16[2048,512]{1,0:T(8,128)(2,1)}, bf16[2048,512]{1,0:T(8,128)(2,1)}, u32[]{:S(2)}, u32[]{:S(2)}) collective-permute-start(bf16[2048,512]{1,0:T(8,128)(2,1)} %bitcast.104), channel_id=1, source_target_pairs={{0,16},{16,0},{1,17},{17,1},{2,18},{18,2},{3,19},{19,3},{4,20},{20... | collective-permute-start | bytes 6291464 | tf_op jit(solution)/shard_map/ppermute | solution.py:1510
  1.2 345.2 %collective-permute-start.2 = (bf16[512,2048]{1,0:T(8,128)(2,1)}, bf16[512,2048]{1,0:T(8,128)(2,1)}, u32[]{:S(2)}, u32[]{:S(2)}) collective-permute-start(bf16[512,2048]{1,0:T(8,128)(2,1)} %bitcast.107), channel_id=1, source_target_pairs={{0,16},{16,0},{1,17},{17,1},{2,18},{18,2},{3,19},{19,3},{4,20},{20... | collective-permute-start | bytes 6291464 | tf_op jit(solution)/shard_map/ppermute | solution.py:1510
  117.1 80.5 %copy-start.11 = (bf16[1,256,2048]{2,1,0:T(8,128)(2,1)S(1)}, bf16[1,256,2048]{2,1,0:T(8,128)(2,1)}, u32[]{:S(2)}) copy-start(bf16[1,256,2048]{2,1,0:T(8,128)(2,1)} %param.12) | copy-start | bytes 3145732
  203.9 1.7 copy-start.27
  204.9 1.5 copy-start.9
  337.5 7.5 collective-permute-start.3
  583.7 123.3 %copy-start.10 = (bf16[256,2048]{1,0:T(8,128)(2,1)S(1)}, bf16[256,2048]{1,0:T(8,128)(2,1)}, u32[]{:S(2)}) copy-start(bf16[256,2048]{1,0:T(8,128)(2,1)} %copy-done.9) | copy-start | bytes 3145732
  583.7 124.8 %copy-start.16 = (bf16[32,64,128]{2,1,0:T(8,128)(2,1)S(1)}, bf16[32,64,128]{2,1,0:T(8,128)(2,1)}, u32[]{:S(2)}) copy-start(bf16[32,64,128]{2,1,0:T(8,128)(2,1)} %get-tuple-element.49) | copy-start | bytes 1572868
  705.2 3.2 copy-start.14
  708.5 1.9 copy-start.23
  710.4 2.8 copy-start
  710.4 2.8 copy-start.2
  710.4 2.8 copy-start.3
  710.4 3.7 copy-start.4
  710.4 4.0 copy-start.5
  710.4 4.3 copy-start.6
  710.4 4.3 copy-start.8
  714.7 25.9 %copy-start.24 = (bf16[256,2048]{1,0:T(8,128)(2,1)S(1)}, bf16[256,2048]{1,0:T(8,128)(2,1)}, u32[]{:S(2)}) copy-start(bf16[256,2048]{1,0:T(8,128)(2,1)} %get-tuple-element.77) | copy-start | bytes 3145732
  738.2 1.7 copy-start.1
  739.9 182.4 %collective-permute-start.4 = (bf16[2048,512]{1,0:T(8,128)(2,1)}, bf16[2048,512]{1,0:T(8,128)(2,1)}, u32[]{:S(2)}, u32[]{:S(2)}) collective-permute-start(bf16[2048,512]{1,0:T(8,128)(2,1)} %get-tuple-element.83), channel_id=1, source_target_pairs={{0,16},{16,0},{1,17},{17,1},{2,18},{18,2},{3,19},{19,3},{4,20},{20... | collective-permute-start | bytes 6291464 | tf_op jit(solution)/shard_map/ppermute | solution.py:1590
  740.0 186.9 %collective-permute-start.5 = (bf16[2048,512]{1,0:T(8,128)(2,1)}, bf16[2048,512]{1,0:T(8,128)(2,1)}, u32[]{:S(2)}, u32[]{:S(2)}) collective-permute-start(bf16[2048,512]{1,0:T(8,128)(2,1)} %get-tuple-element.85), channel_id=1, source_target_pairs={{0,16},{16,0},{1,17},{17,1},{2,18},{18,2},{3,19},{19,3},{4,20},{20... | collective-permute-start | bytes 6291464 | tf_op jit(solution)/shard_map/ppermute | solution.py:1590
  740.5 190.9 %collective-permute-start.6 = (bf16[512,2048]{1,0:T(8,128)(2,1)}, bf16[512,2048]{1,0:T(8,128)(2,1)}, u32[]{:S(2)}, u32[]{:S(2)}) collective-permute-start(bf16[512,2048]{1,0:T(8,128)(2,1)} %get-tuple-element.87), channel_id=1, source_target_pairs={{0,16},{16,0},{1,17},{17,1},{2,18},{18,2},{3,19},{19,3},{4,20},{20... | collective-permute-start | bytes 6291464 | tf_op jit(solution)/shard_map/ppermute | solution.py:1590
  740.6 13.7 %copy-start.12 = (bf16[1,256,2048]{2,1,0:T(8,128)(2,1)S(1)}, bf16[1,256,2048]{2,1,0:T(8,128)(2,1)}, u32[]{:S(2)}) copy-start(bf16[1,256,2048]{2,1,0:T(8,128)(2,1)} %param.12) | copy-start | bytes 3145732
  769.6 7.0 copy-start.20
  769.6 7.0 copy-start.21
  777.9 140.9 %copy-start.13 = (f32[256,2048]{1,0:T(8,128)S(1)}, f32[256,2048]{1,0:T(8,128)}, u32[]{:S(2)}) copy-start(f32[256,2048]{1,0:T(8,128)} %get-tuple-element.133) | copy-start | bytes 6291460
  918.7 3.6 copy-start.19
  922.3 4.6 copy-start.18
  926.9 4.6 copy-start.17
  931.5 4.4 copy-start.25
  935.9 1.4 copy-start.26
  (3 other events, 3.1 us)

commit v4 on v3

--- a/solution.py
+++ b/solution.py
@@ -438,13 +438,14 @@
         for n in cuts:
             groups.append(refs[at : at + n])
             at += n
-        steps = self.steps(groups[1], groups[3], groups[5]) if self.steps else []
+        steps = self.steps(groups[1], groups[3], groups[5], groups[2]) if self.steps else []
         return groups[0], groups[2], groups[4], steps
 
 
-def mingle(events, steps, free, lead, span):
+def mingle(events, gate, steps, free, lead, span):
     for event in events[:free]:
         event()
+    gate()
     first = round(lead * len(steps))
     for step in steps[:first]:
         step()
@@ -459,7 +460,7 @@
         step()
 
 
-def gather_kernel(grid, parts, count, beside, *refs):
+def gather_kernel(grid, parts, lags, count, beside, *refs):
     srcs, outs, (send_sem, recv_sem, own_sem), steps = beside.share(refs, count, 3)
     c = grid.coords()
     me = grid.index(c)
@@ -488,10 +489,21 @@
         sent.append((pred, copy))
 
     todo = []
-    for p, (_, _, _, order) in enumerate(parts):
-        for event in grid.events(order):
-            todo.append((farthest(order, event), p, event))
-    todo.sort(key=lambda t: t[:2])
+    for lag in sorted(set(lags)):
+        group = []
+        for p, (_, _, _, order) in enumerate(parts):
+            if lags[p] == lag:
+                group += [(farthest(order, event), p, event) for event in grid.events(order)]
+        group.sort(key=lambda t: t[:2])
+        todo += [(lag + n / len(group), p, event) for n, (_, p, event) in enumerate(group)]
+    todo.sort(key=lambda t: t[0])
+    free = 1 + max(n for n, (_, p, _) in enumerate(todo) if lags[p] == 0)
+    if len(set(lags)) == 1:
+        free = len(parts)
+
+    def gate():
+        for copy in own:
+            copy.wait()
 
     def handle(p, event):
         a, _, _, order = parts[p]
@@ -517,23 +529,17 @@
             for side in grid.sides(d):
                 push(p, origin, source, d, side, pred)
 
-    mingle(
-        [functools.partial(handle, p, event) for _, p, event in todo],
-        steps,
-        sum(not any(event.values()) for _, _, event in todo),
-        beside.lead,
-        beside.span,
-    )
+    events = [functools.partial(handle, p, event) for _, p, event in todo]
+    mingle(events, gate, steps, free, beside.lead, beside.span)
     for pred, copy in sent:
         when(pred, copy.wait_send)
-    for copy in own:
-        copy.wait()
-
-
-def gather(arrays, grid, parts, cid, beside=Beside()):
+
+
+def gather(arrays, grid, parts, cid, beside=Beside(), lags=None):
+    lags = lags or (0,) * len(parts)
     n, count = grid.size, len(arrays)
     return pl.pallas_call(
-        functools.partial(gather_kernel, grid, parts, count, beside),
+        functools.partial(gather_kernel, grid, parts, lags, count, beside),
         out_shape=[jax.ShapeDtypeStruct((n,) + x.shape, x.dtype) for x in arrays] + list(beside.outs),
         in_specs=[pl.BlockSpec(memory_space=pl.ANY)] * count + list(beside.in_specs),
         out_specs=[pl.BlockSpec(memory_space=pl.ANY)] * (count + len(beside.outs)),
@@ -678,6 +684,7 @@
 
     mingle(
         [functools.partial(handle, p, event) for _, p, event in todo],
+        lambda: None,
         steps,
         sum(event[parts[p][3][-1]] is not None for _, p, event in todo),
         beside.lead,
@@ -781,18 +788,21 @@
     return (line == slot).astype(jnp.float32).astype(jnp.bfloat16)
 
 
-def forward_beside(ffn_rows, rank_rows, rank_cols, weight_cols, halves, capacity):
-    row_count, tokens, width = ffn_rows.shape
+def forward_beside(shape, aside_shape, halves, capacity):
+    row_count, tokens, width = shape
+    expert_count = (aside_shape[1] - 8) // 2
     hidden = 2 * halves[0].shape[1]
     pairs, pair = row_count // 2, 2 * capacity
     slots = row_count * capacity
     low, full = jnp.bfloat16, jnp.float32
 
-    def steps(ins, outs, scratch):
-        ffn_in, ranks, ranks_t, weights_t = ins[:4]
-        weights, (ffn, xs, pre, units, out, mix), sems = scratch[:3], scratch[3:9], scratch[9:]
+    def steps(ins, outs, scratch, arrivals):
+        ffn_in = arrivals[0]
+        weights, (ffn, xs, pre, units, out, mix), sems = scratch[:3], scratch[3:9], scratch[9:12]
+        notes, ranks, ranks_t, weights_t, notes_sem = scratch[12:]
         load_sem, row_sem, out_sem = sems
-        heavy = weight_copies(ins[4:], weights, load_sem)
+        heavy = weight_copies(ins, weights, load_sem)
+        notes_copy = Move(arrivals[1], notes, notes_sem)
         gate_w, up_w, down_w = weights
 
         def load(q):
@@ -811,9 +821,18 @@
             return [Move(a, b, out_sem.at[i]) for i, (a, b) in enumerate(moves)]
 
         def opening():
+            notes_copy.start()
+            load(0).start()
             for copy in heavy:
                 copy.start()
-            load(0).start()
+            notes_copy.wait()
+            expert = lax.axis_index("expert")
+            for first, kept in ((expert_count, ranks_t), (0, weights_t)):
+                for row in range(row_count):
+                    ranks[row : row + 1, :] = notes[row, pl.ds(first + expert, 1), :]
+                kept[...] = ranks[...].T
+            for row in range(row_count):
+                ranks[row : row + 1, :] = notes[row, pl.ds(expert_count + expert, 1), :]
 
         def choose(q):
             load(q).wait()
@@ -881,8 +900,8 @@
         return listed + [closing]
 
     return Beside(
-        ins=(ffn_rows, rank_rows, rank_cols, weight_cols) + tuple(halves),
-        in_specs=(ANYWHERE, ON_CORE, ON_CORE, ON_CORE) + (ANYWHERE,) * 6,
+        ins=tuple(halves),
+        in_specs=(ANYWHERE,) * 6,
         outs=[
             jax.ShapeDtypeStruct((slots, width), low),
             jax.ShapeDtypeStruct((slots, hidden), full),
@@ -904,10 +923,14 @@
             pltpu.SemaphoreType.DMA((6,)),
             pltpu.SemaphoreType.DMA((2,)),
             pltpu.SemaphoreType.DMA((6,)),
+            pltpu.VMEM(aside_shape, full),
+            pltpu.VMEM((row_count, tokens), full),
+            pltpu.VMEM((tokens, row_count), full),
+            pltpu.VMEM((tokens, row_count), full),
+            pltpu.SemaphoreType.DMA,
         ],
         steps=steps,
-        lead=0.3,
-        span=0.6,
+        span=0.7,
     )
 
 
@@ -920,7 +943,7 @@
     slots = row_count * capacity
     low, full = jnp.bfloat16, jnp.float32
 
-    def steps(ins, outs, scratch):
+    def steps(ins, outs, scratch, arrivals):
         early_in, late_in, ranks, ranks_t, weights, gate_in, up_in, out_in = ins[:8]
         heavy_refs, (cot, ge, pre, out, gg, gu, gx, dots, sums), sems = scratch[:3], scratch[3:12], scratch[12:]
         load_sem, row_sem, out_sem = sems
@@ -1079,7 +1102,7 @@
     block = 256
     low, full = jnp.bfloat16, jnp.float32
 
-    def steps(ins, outs, scratch):
+    def steps(ins, outs, scratch, arrivals):
         rows_ref, grads_ref, gate_ref, up_ref, units_ref = ins
         left, turned, gate, up, grads, wide_own, wide_far, tall_own, tall_far, load_sem, left_sem, out_sem = scratch
         heavy = [
@@ -1214,19 +1237,22 @@
     return pltpu.roll(values, values.shape[1] // 2, 1)
 
 
-def attend_beside(tokens, gain_rows, qkv_weight, live_row, cosine, sine):
+def attend_beside(tokens, weight_rows, gain_column, live_row, cosine, sine):
     row_count, width = tokens.shape
     low, full = jnp.bfloat16, jnp.float32
     block, group, strip = 256, 2, 32
     tiles, per_part = 3 * width // block, width // block
     score_scale = HEAD ** (-0.5)
 
-    def steps(ins, outs, scratch):
-        tokens_ref, gains, weight, live, cos, sin = ins
-        normed, proj, panel, queries, keys, values, mixed, probs, scale, panel_sem, out_sem, probs_sem = scratch
+    def steps(ins, outs, scratch, arrivals):
+        tokens_ref, live, cos, sin = ins
+        normed, proj, panel, queries, keys, values, mixed, probs, scale, panel_sem, out_sem, probs_sem = scratch[:12]
+        small, gains, small_sem = scratch[12:]
+        weight = arrivals[0]
+        small_copy = Move(arrivals[1], small, small_sem)
 
         def load(t):
-            return Move(weight.at[:, pl.ds(t * block, block)], panel.at[t % 3], panel_sem.at[t % 3])
+            return Move(weight.at[:, :, pl.ds(t * block, block)], panel.at[t % 3], panel_sem.at[t % 3])
 
         leaves = [
             Move(ref, outs[i], out_sem.at[i])
@@ -1237,8 +1263,14 @@
             return Move(probs.at[n % 2], outs[6].at[pl.ds(n * group, group)], probs_sem.at[n % 2])
 
         def opening():
+            small_copy.start()
             load(0).start()
             load(1).start()
+            small_copy.wait()
+            blocks = 128 // small.shape[1]
+            for k in range(width // 128):
+                columns = small[k * blocks : (k + 1) * blocks].astype(full).reshape(128, 128)
+                gains[:, k * 128 : (k + 1) * 128] = columns.T[gain_column : gain_column + 8]
 
             @pl.loop(0, row_count // strip)
             def _(k):
@@ -1253,7 +1285,7 @@
             load(t).wait()
             if t + 2 < tiles:
                 load(t + 2).start()
-            proj[:, t * block : (t + 1) * block] = dot(normed[...], panel[t % 3])
+            proj[:, t * block : (t + 1) * block] = dot(normed[...], panel[t % 3].reshape(width, block))
 
         def measure(part):
             @pl.loop(0, row_count // strip)
@@ -1307,8 +1339,8 @@
 
     shape = (row_count, width)
     return Beside(
-        ins=(tokens, gain_rows, qkv_weight, live_row, cosine, sine),
-        in_specs=(ON_CORE, ON_CORE, ANYWHERE, ON_CORE, ON_CORE, ON_CORE),
+        ins=(tokens, live_row, cosine, sine),
+        in_specs=(ON_CORE,) * 4,
         outs=[
             jax.ShapeDtypeStruct(shape, low),
             jax.ShapeDtypeStruct((row_count, 2 * width), full),
@@ -1321,7 +1353,7 @@
         scratch=[
             pltpu.VMEM(shape, low),
             pltpu.VMEM((row_count, 3 * width), full),
-            pltpu.VMEM((3, width, block), low),
+            pltpu.VMEM((3, width // weight_rows, weight_rows, block), low),
             pltpu.VMEM(shape, low),
             pltpu.VMEM(shape, low),
             pltpu.VMEM(shape, low),
@@ -1331,9 +1363,11 @@
             pltpu.SemaphoreType.DMA((3,)),
             pltpu.SemaphoreType.DMA((6,)),
             pltpu.SemaphoreType.DMA((2,)),
+            pltpu.VMEM((width // weight_rows, weight_rows, 128), low),
+            pltpu.VMEM((8, width), full),
+            pltpu.SemaphoreType.DMA,
         ],
         steps=steps,
-        lead=0.2,
         span=0.6,
     )
 
@@ -1345,7 +1379,7 @@
     score_scale = HEAD ** (-0.5)
     across_rows = (((0,), (0,)), ((), ()))
 
-    def steps(ins, outs, scratch):
+    def steps(ins, outs, scratch, arrivals):
         grad_ref, weight, query_ref, key_ref, value_ref, probs_in, parts_ref, gains, cos, sin = ins
         grad_mixed, grads, panel, prob_ref, projected, sums, panel_sem, probs_sem, out_sem = scratch
         tiles = width // block
@@ -1445,7 +1479,7 @@
 def alone(beside):
     def kernel(*refs):
         a, b = len(beside.ins), len(beside.ins) + len(beside.outs)
-        for step in beside.steps(refs[:a], refs[a:b], refs[b:]):
+        for step in beside.steps(refs[:a], refs[a:b], refs[b:], ()):
             step()
 
     return pl.pallas_call(
@@ -1454,8 +1488,102 @@
         in_specs=list(beside.in_specs),
         out_specs=[ANYWHERE] * len(beside.outs),
         scratch_shapes=list(beside.scratch),
-        compiler_params=pltpu.CompilerParams(vmem_limit_bytes=40 << 20),
+        compiler_params=pltpu.CompilerParams(vmem_limit_bytes=48 << 20),
     )(*beside.ins)
+
+
+DEEP = 4
+
+
+def total_beside(pairs):
+    low, full = jnp.bfloat16, jnp.float32
+    jobs, shapes = [], []
+    for n, (own, _) in enumerate(pairs):
+        rows = own.shape[0] // 8
+        shape = (rows, own.shape[1])
+        if shape not in shapes:
+            shapes.append(shape)
+        jobs += [(n, k, shapes.index(shape)) for k in range(8)]
+
+    def steps(ins, outs, scratch, arrivals):
+        count = len(shapes)
+        owns, fars, sums = scratch[:count], scratch[count : 2 * count], scratch[2 * count : 3 * count]
+        in_sem, out_sem = scratch[3 * count :]
+
+        def load(m):
+            n, k, s = jobs[m]
+            here = pl.ds(k * shapes[s][0], shapes[s][0])
+            return [
+                Move(ins[2 * n].at[here], owns[s].at[m % DEEP], in_sem.at[m % DEEP, 0]),
+                Move(ins[2 * n + 1].at[here], fars[s].at[m % DEEP], in_sem.at[m % DEEP, 1]),
+            ]
+
+        def leave(m):
+            n, k, s = jobs[m]
+            here = pl.ds(k * shapes[s][0], shapes[s][0])
+            return Move(sums[s].at[m % DEEP], outs[n].at[here], out_sem.at[m % DEEP])
+
+        def opening():
+            for m in range(DEEP - 1):
+                for move in load(m):
+                    move.start()
+
+        def add(m):
+            for move in load(m):
+                move.wait()
+            if m + DEEP - 1 < len(jobs):
+                for move in load(m + DEEP - 1):
+                    move.start()
+            if m >= DEEP:
+                leave(m - DEEP).wait()
+            s = jobs[m][2]
+            sums[s][m % DEEP] = owns[s][m % DEEP] + fars[s][m % DEEP].astype(full)
+            leave(m).start()
+
+        def closing():
+            for m in range(len(jobs) - DEEP, len(jobs)):
+                leave(m).wait()
+
+        return [opening] + [functools.partial(add, m) for m in range(len(jobs))] + [closing]
+
+    return Beside(
+        ins=[x for pair in pairs for x in pair],
+        in_specs=(ANYWHERE,) * (2 * len(pairs)),
+        outs=[jax.ShapeDtypeStruct(own.shape, full) for own, _ in pairs],
+        scratch=[pltpu.VMEM((DEEP,) + shape, full) for shape in shapes]
+        + [pltpu.VMEM((DEEP,) + shape, low) for shape in shapes]
+        + [pltpu.VMEM((DEEP,) + shape, full) for shape in shapes]
+        + [pltpu.SemaphoreType.DMA((DEEP, 2)), pltpu.SemaphoreType.DMA((DEEP,))],
+        steps=steps,
+    )
+
+
+def together(first, second):
+    cuts = [(len(getattr(first, kind)), len(getattr(second, kind))) for kind in ("ins", "outs", "scratch")]
+
+    def steps(ins, outs, scratch, arrivals):
+        groups = [(refs[:a], refs[a:]) for refs, (a, _) in zip((ins, outs, scratch), cuts)]
+        left = first.steps(*(group[0] for group in groups), arrivals)
+        right = second.steps(*(group[1] for group in groups), arrivals)
+        listed, done = [], 0
+        for n, step in enumerate(left):
+            listed.append(step)
+            until = (n + 1) * len(right) // len(left)
+            listed += right[done:until]
+            done = until
+        return listed
+
+    return Beside(
+        ins=list(first.ins) + list(second.ins),
+        in_specs=list(first.in_specs) + list(second.in_specs),
+        outs=list(first.outs) + list(second.outs),
+        scratch=list(first.scratch) + list(second.scratch),
+        steps=steps,
+    )
+
+
+WEIGHTS_LAG = 0.9
+ROWS_LAG = 0.9
 
 
 def gathered_body(
@@ -1499,13 +1627,6 @@
     small = jnp.concatenate(
         [w_router, gains.T, jnp.zeros((weight_rows, 128 - expert_count - 4), low)], axis=1
     )
-    qkv_all, small_all = gather(
-        [w_qkv, small], devices, cut(0, quarter, wide_orders) + cut(1, [weight_rows], wide_orders[2:3]), 1
-    )
-    small_all = small_all.reshape(D, 128)
-    router_weight = small_all[:, :expert_count]
-    gain_float = small_all[:, expert_count : expert_count + 4].T.astype(full)
-    qkv_weight = qkv_all.reshape(D, 3 * D)
     gate_own, up_own, down_own = w_gate[0], w_up[0], w_down[0]
     gate_far, up_far, down_far = (lax.ppermute(w, "dp", swap) for w in (gate_own, up_own, down_own))
 
@@ -1523,13 +1644,20 @@
     cosine, sine = (table[:, 0] for table in rope_tables(row_count, HEAD))
     sine = jnp.concatenate([-sine[:, : HEAD // 2], sine[:, HEAD // 2 :]], axis=1)
     early = row_count // 4
-    out_all, cot_early, normed, qk_parts, queries, keys_low, values_low, mixed_low, probs = gather(
-        [w_out, cotangent[0, :early]],
+    first_parts = cut(0, quarter, wide_orders) + cut(1, [weight_rows], wide_orders[2:3])
+    later_parts = cut(2, quarter, wide_orders) + cut(3, [early // 4] * 4, narrow_orders)
+    qkv_all, small_all, out_all, cot_early, normed, qk_parts, queries, keys_low, values_low, mixed_low, probs = gather(
+        [w_qkv, small, w_out, cotangent[0, :early]],
         devices,
-        cut(0, quarter, wide_orders) + cut(1, [early // 4] * 4, narrow_orders),
-        7,
-        attend_beside(tokens[0], gain_float, qkv_weight, live_slots[None, :].astype(full), cosine, sine),
-    )
+        first_parts + later_parts,
+        1,
+        attend_beside(tokens[0], weight_rows, expert_count, live_slots[None, :].astype(full), cosine, sine),
+        (0,) * len(first_parts) + (WEIGHTS_LAG,) * len(later_parts),
+    )
+    small_all = small_all.reshape(D, 128)
+    router_weight = small_all[:, :expert_count]
+    gain_float = small_all[:, expert_count : expert_count + 4].T.astype(full)
+    qkv_weight = qkv_all.reshape(D, 3 * D)
     out_weight = out_all.reshape(D, D)
     inputs = tokens[0].astype(full)
     _, attn_norm_back = jax.vjp(norm_scale, inputs, gain_float[0])
@@ -1549,11 +1677,16 @@
         axis=0,
     )
 
-    ffn_rows, aside_rows = gather(
-        [ffn_low, aside],
+    halves = (gate_own, gate_far, up_own, up_far, down_own, down_far)
+    first_parts = cut(0, row_shares, row_orders) + cut(1, [aside.shape[0]], row_orders[2:3])
+    later_parts = cut(2, late_shares, row_orders)
+    _, aside_rows, cot_late, rows_in, gate_pre, up_pre, units, expert_out, mixture_part = gather(
+        [ffn_low, aside, cotangent[0, early:]],
         chips,
-        cut(0, row_shares, row_orders) + cut(1, [aside.shape[0]], row_orders[2:3]),
-        3,
+        first_parts + later_parts,
+        2,
+        forward_beside((owners, row_count, D), (owners,) + aside.shape, halves, capacity),
+        (0,) * len(first_parts) + (ROWS_LAG,) * len(later_parts),
     )
     sums_core = jnp.sum(aside_rows[:, 2 * expert_count, : 2 * expert_count], axis=0)
     sums_all = sums_core + lax.ppermute(sums_core, "dp", swap)
@@ -1561,14 +1694,6 @@
     balance = jnp.sum(count_total * prob_total) * balance_factor
     weight_of = lax.dynamic_index_in_dim(aside_rows, expert, 1, keepdims=False)
     rank_of = lax.dynamic_index_in_dim(aside_rows, expert_count + expert, 1, keepdims=False)
-    halves = (gate_own, gate_far, up_own, up_far, down_own, down_far)
-    cot_late, rows_in, gate_pre, up_pre, units, expert_out, mixture_part = gather(
-        [cotangent[0, early:]],
-        chips,
-        cut(0, late_shares, row_orders),
-        2,
-        forward_beside(ffn_rows, rank_of, rank_of.T, weight_of.T, halves, capacity),
-    )
     mixture, grad_rows, grad_gate, grad_up, back_part, dot_route = scatter(
         [mixture_part],
         chips,
@@ -1586,10 +1711,7 @@
         4,
         outer_beside(rows_in, grad_rows, grad_gate, grad_up, units),
     )
-    expert_grads = [
-        (own + lax.ppermute(far, "dp", swap).astype(full))[None]
-        for own, far in zip(halves_grads[::2], halves_grads[1::2])
-    ]
+    far_grads = [lax.ppermute(far, "dp", swap) for far in halves_grads[1::2]]
     result = (live_float * (hidden_state + mixture)).astype(low)[None]
 
     balance_coef = BALANCE_WEIGHT * balance_factor
@@ -1605,9 +1727,12 @@
     grad_hidden_part, grad_gain_ffn = ffn_norm_back(grad_ffn)
     grad_hidden_state = grad_layer + grad_hidden_part
     grad_attn_low = grad_hidden_state.astype(low)
-    grad_projected, head_sums = alone(
-        attend_back_beside(
-            grad_attn_low, out_weight, queries, keys_low, values_low, probs, qk_parts, gain_float, cosine, sine
+    grad_projected, head_sums, *expert_grads = alone(
+        together(
+            attend_back_beside(
+                grad_attn_low, out_weight, queries, keys_low, values_low, probs, qk_parts, gain_float, cosine, sine
+            ),
+            total_beside(list(zip(halves_grads[::2], far_grads))),
         )
     )
     grad_gain_query, grad_gain_key = jnp.sum(head_sums, axis=1)
@@ -1641,7 +1766,7 @@
         grad_out,
         grad_small[:, :expert_count],
         grad_small[:, expert_count : expert_count + 4].T,
-        *expert_grads,
+        *(g[None] for g in expert_grads),
         balance,
     )
 

time: 946 us -> 928 us (0.981)
  other arithmetic: 34.1 us -> 18.2 us
    pallas_call x4 -> x2, Pallas kernels: 419 us -> 405 us  [gather(): pl.pallas_call(functools.partial(gather_kernel, grid, parts, lags, count,...]
    pallas_call x3, Pallas kernels: 393 us -> 406 us  [scatter(): pl.pallas_call(functools.partial(scatter_kernel, grid, parts, count, besi...]
    broadcast_in_dim x3 -> x0, other arithmetic: 13.5 us -> none  [gathered_body(): (own + lax.ppermute(far, 'dp', swap).astype(full))[None]]
  transfers between devices with their start and end apart: 7 -> 7, of which waited for: 0 -> 0; matrix products, arithmetic and copies ran while one was open for 8% -> 4% of each run, Pallas kernels for 48% -> 49%
where the time goes in v4:
time: 928 us; the launch traced here: 923 us
  Pallas kernels  841 us (91%)
  matrix products  42.7 us (5%)
  other arithmetic  18.2 us (2%)
  local copies, waits for them, and re-layouts  15.6 us (2%)
    pallas_call x3, Pallas kernels, scatter(): pl.pallas_call(functools.partial(scatter_kernel, grid, parts, count, besi...  406 us
    pallas_call x2, Pallas kernels, gather(): pl.pallas_call(functools.partial(gather_kernel, grid, parts, lags, count,...  405 us
    pallas_call x1, Pallas kernels, alone(): pl.pallas_call(kernel, out_shape=beside.outs, in_specs=list(beside.in_spe...  29.5 us
    dot_general x2, matrix products, outer(): return jnp.einsum('sa,sb->ab', left, right, preferred_element_type=full)  19.1 us
  transfers between devices with their start and end apart: 7, of which 0 were waited for; matrix products, arithmetic and copies ran while one was open for 4% of the time, Pallas kernels for 49%

profile of v4, /device:TPU:8, one launch (start us, length us, event | category | flops | bytes accessed | tf_op | source)
XLA Modules:
  0.0 922.9 jit_solution(6352175737420148126)
XLA Ops:
  1.4 1.2 fusion.14
  4.0 1.7 slice_bitcast_fusion.1.refs_3_
  5.6 0.8 copy.52
  6.4 0.8 copy.53
  7.2 0.8 pad_maximum_fusion.1.refs_7_.refs_9_
  8.7 186.8 %shard_map.195 = (bf16[32,64,6144]{2,1,0:T(8,128)(2,1)}, bf16[32,64,128]{2,1,0:T(8,128)(2,1)}, bf16[32,64,2048]{2,1,0:T(8,128)(2,1)}, bf16[32,64,2048]{2,1,0:T(8...) custom-call(bf16[64,6144]{1,0:T(8,128)(2,1)} %refs_0_.1, ...), custom_call_target="tpu_custom_call" | custom-call | tf_op jit(solution)/shard_map/pallas_call | solution.py:541
  195.6 6.2 multiply_reduce_fusion.2
  201.8 1.2 slice_convert_fusion
  203.0 1.6 copy.65
  206.9 1.0 slice_bitcast_fusion.refs_2_
  207.9 218.3 %shard_map.196 = (bf16[16,256,2048]{2,1,0:T(8,128)(2,1)}, f32[16,40,256]{2,1,0:T(8,128)}, bf16[16,192,2048]{2,1,0:T(8,128)(2,1)}, bf16[2048,2048]{1,0:T(8,128)(2...) custom-call(bf16[256,2048]{1,0:T(8,128)(2,1)} %copy-done.5, ...), custom_call_target="tpu_custom_call" | custom-call | tf_op jit(solution)/shard_map/pallas_call | solution.py:541
  426.2 0.9 slice_reduce_fusion
  427.0 1.0 constant_dynamic-slice_fusion
  430.0 139.9 %shard_map.197 = (f32[256,2048]{1,0:T(8,128)}, bf16[2048,2048]{1,0:T(8,128)(2,1)}, bf16[2048,1024]{1,0:T(8,128)(2,1)}, bf16[2048,1024]{1,0:T(8,128)(2,1)}, bf16[...) custom-call(bf16[16,256,2048]{2,1,0:T(8,128)(2,1)} %get-tuple-element.54.refs_0_, ...), custom_call_target="tpu_custom_call" | custom-call | tf_op jit(solution)/shard_map/pallas_call | solution.py:708
  569.9 1.5 broadcast_select_fusion.refs_1_
  571.4 128.0 %shard_map.198 = (f32[256,2048]{1,0:T(8,128)}, f32[16,256]{1,0:T(8,128)}, f32[2048,512]{1,0:T(8,128)}, bf16[2048,512]{1,0:T(8,128)(2,1)}, f32[2048,512]{1,0:T(8,...) custom-call(bf16[16,256,2048]{2,1,0:T(8,128)(2,1)} %get-tuple-element.62.refs_0_, ...), custom_call_target="tpu_custom_call" | custom-call | tf_op jit(solution)/shard_map/pallas_call | solution.py:708
  700.8 0.8 multiply_reduce_fusion.3
  701.6 0.8 multiply_convert_fusion.2
  703.1 2.5 multiply_reduce_fusion
  706.2 1.1 copy-done.11
  707.3 2.6 fusion.23
  709.9 5.6 convolution_convert_fusion.1
  715.6 29.5 %shard_map.199 = (bf16[256,6144]{1,0:T(8,128)(2,1)}, f32[2,8,2048]{2,1,0:T(8,128)S(1)}, f32[2048,512]{1,0:T(8,128)}, f32[2048,512]{1,0:T(8,128)}, f32[512,2048]{1,0:T(8,128)}) custom-call(bf16[256,2048]{1,0:T(8,128)(2,1)S(1)} %get-tuple-element.136.refs_0_, bf16[2048,2048]{1,0:T(8,128)(2,1)} %bitcast.101, bf16[256,2048]{1,0:T(8,128)(2,1)S(1)} %copy-done.2, ...), custom_call_target="tpu_custom_call" | custom-call | tf_op jit(solution)/shard_map/pallas_call | solution.py:1485
  745.1 13.8 %fusion.6 = (f32[2048]{0:T(1024)S(1)}, f32[256]{0:T(256)S(1)}, f32[256,2048]{1,0:T(8,128)}) fusion(f32[256]{0:T(256)S(1)} %fusion.21, bf16[1,256,2048]{2,1,0:T(8,128)(2,1)S(1)} %copy-done.9, f32[2048]{0:T(1024)S(1)} %bitcast.114, bf16[256,6144]{1,0:T(8,128)(2,1)} %get-tuple-element.82, bf16[2048,6144]{1,0:T(8,128)(2,1)} %bitcast.119), kind=kOutput, calls=%fused_computation.15 | convolution fusion | flops 6446118912 | bytes 31475712 | tf_op jit(solution)/shard_map/te,de->td/dot_general | solution.py:1739
  759.3 13.5 %convolution_convert_fusion = bf16[2048,6144]{1,0:T(8,128)(2,1)} fusion(bf16[256,2048]{1,0:T(8,128)(2,1)} %get-tuple-element.84, bf16[256,6144]{1,0:T(8,128)(2,1)} %get-tuple-element.82), kind=kOutput, calls=%fused_computation | convolution fusion | flops 6455033856 | bytes 29360128 | tf_op jit(solution)/shard_map/sa,sb->ab/dot_general | solution.py:1745
  772.8 1.3 maximum_maximum_fusion
  774.1 138.5 %shard_map.200 = (f32[64,6144]{1,0:T(8,128)}, f32[64,2048]{1,0:T(8,128)}, f32[64,128]{1,0:T(8,128)}) custom-call(bf16[32,64,6144]{2,1,0:T(8,128)(2,1)} %bitcast.88, bf16[32,64,2048]{2,1,0:T(8,128)(2,1)} %bitcast.89, f32[32,64,128]{2,1,0:T(8,128)} %bitcast.105), custom_call_target="tpu_custom_call" | custom-call | tf_op jit(solution)/shard_map/pallas_call | solution.py:708
  912.7 0.8 slice_bitcast_fusion.2
  914.2 1.4 copy.59
  915.6 3.6 fusion.2
  919.2 1.1 copy.73
  920.6 0.8 copy.74
  (93 shorter events, 9.5 us)
Async XLA Ops:
  0.6 207.2 %collective-permute-start = (bf16[2048,512]{1,0:T(8,128)(2,1)}, bf16[2048,512]{1,0:T(8,128)(2,1)}, u32[]{:S(2)}, u32[]{:S(2)}) collective-permute-start(bf16[2048,512]{1,0:T(8,128)(2,1)} %bitcast.91), channel_id=1, source_target_pairs={{0,16},{16,0},{1,17},{17,1},{2,18},{18,2},{3,19},{19,3},{4,20},{20... | collective-permute-start | bytes 6291464 | tf_op jit(solution)/shard_map/ppermute | solution.py:1631
  0.7 207.1 %collective-permute-start.1 = (bf16[2048,512]{1,0:T(8,128)(2,1)}, bf16[2048,512]{1,0:T(8,128)(2,1)}, u32[]{:S(2)}, u32[]{:S(2)}) collective-permute-start(bf16[2048,512]{1,0:T(8,128)(2,1)} %bitcast.94), channel_id=1, source_target_pairs={{0,16},{16,0},{1,17},{17,1},{2,18},{18,2},{3,19},{19,3},{4,20},{20... | collective-permute-start | bytes 6291464 | tf_op jit(solution)/shard_map/ppermute | solution.py:1631
  1.2 206.6 %collective-permute-start.2 = (bf16[512,2048]{1,0:T(8,128)(2,1)}, bf16[512,2048]{1,0:T(8,128)(2,1)}, u32[]{:S(2)}, u32[]{:S(2)}) collective-permute-start(bf16[512,2048]{1,0:T(8,128)(2,1)} %bitcast.97), channel_id=1, source_target_pairs={{0,16},{16,0},{1,17},{17,1},{2,18},{18,2},{3,19},{19,3},{4,20},{20... | collective-permute-start | bytes 6291464 | tf_op jit(solution)/shard_map/ppermute | solution.py:1631
  2.6 193.0 %copy-start.7 = (bf16[1,256,2048]{2,1,0:T(8,128)(2,1)S(1)}, bf16[1,256,2048]{2,1,0:T(8,128)(2,1)}, u32[]{:S(2)}) copy-start(bf16[1,256,2048]{2,1,0:T(8,128)(2,1)} %param.12) | copy-start | bytes 3145732
  195.6 6.3 copy-start.12
  203.0 2.0 copy-start.13
  204.8 0.9 copy-start.21
  204.8 1.0 copy-start.20
  204.8 1.8 copy-start.8
  205.0 2.8 copy-start.5
  205.0 1.8 copy-start.14
  429.4 270.7 %collective-permute-start.3 = (f32[32]{0:T(128)S(1)}, f32[32]{0:T(128)S(1)}, u32[]{:S(2)}, u32[]{:S(2)}) collective-permute-start(f32[32]{0:T(128)S(1)} %slice_reduce_fusion), channel_id=1, source_target_pairs={{0,16},{16,0},{1,17},{17,1},{2,18},{18,2},{3,19},{19,3},{4,20},{20... | collective-permute-start | bytes 392 | tf_op jit(solution)/shard_map/ppermute | solution.py:1692
  699.5 16.1 %collective-permute-start.4 = (bf16[2048,512]{1,0:T(8,128)(2,1)}, bf16[2048,512]{1,0:T(8,128)(2,1)}, u32[]{:S(2)}, u32[]{:S(2)}) collective-permute-start(bf16[2048,512]{1,0:T(8,128)(2,1)} %get-tuple-element.77), channel_id=1, source_target_pairs={{0,16},{16,0},{1,17},{17,1},{2,18},{18,2},{3,19},{19,3},{4,20},{20... | collective-permute-start | bytes 6291464 | tf_op jit(solution)/shard_map/ppermute | solution.py:1714
  699.5 16.0 %collective-permute-start.5 = (bf16[2048,512]{1,0:T(8,128)(2,1)}, bf16[2048,512]{1,0:T(8,128)(2,1)}, u32[]{:S(2)}, u32[]{:S(2)}) collective-permute-start(bf16[2048,512]{1,0:T(8,128)(2,1)} %get-tuple-element.79), channel_id=1, source_target_pairs={{0,16},{16,0},{1,17},{17,1},{2,18},{18,2},{3,19},{19,3},{4,20},{20... | collective-permute-start | bytes 6291464 | tf_op jit(solution)/shard_map/ppermute | solution.py:1714
  700.0 15.5 %collective-permute-start.6 = (bf16[512,2048]{1,0:T(8,128)(2,1)}, bf16[512,2048]{1,0:T(8,128)(2,1)}, u32[]{:S(2)}, u32[]{:S(2)}) collective-permute-start(bf16[512,2048]{1,0:T(8,128)(2,1)} %get-tuple-element.81), channel_id=1, source_target_pairs={{0,16},{16,0},{1,17},{17,1},{2,18},{18,2},{3,19},{19,3},{4,20},{20... | collective-permute-start | bytes 6291464 | tf_op jit(solution)/shard_map/ppermute | solution.py:1714
  703.0 2.6 copy-start.6
  703.1 3.1 copy-start.15
  703.1 3.1 copy-start.16
  705.6 1.7 copy-start.11
  707.3 2.6 copy-start.17
  709.9 5.7 copy-start
  709.9 5.7 copy-start.1
  709.9 5.7 copy-start.2
  709.9 5.7 copy-start.3
  709.9 5.7 copy-start.4
  715.6 29.5 %copy-start.9 = (bf16[1,256,2048]{2,1,0:T(8,128)(2,1)S(1)}, bf16[1,256,2048]{2,1,0:T(8,128)(2,1)}, u32[]{:S(2)}) copy-start(bf16[1,256,2048]{2,1,0:T(8,128)(2,1)} %param.12) | copy-start | bytes 3145732
  774.1 141.5 %copy-start.10 = (f32[256,2048]{1,0:T(8,128)S(1)}, f32[256,2048]{1,0:T(8,128)}, u32[]{:S(2)}) copy-start(f32[256,2048]{1,0:T(8,128)} %get-tuple-element.137) | copy-start | bytes 6291460
  915.6 3.6 copy-start.18
  919.2 1.4 copy-start.19

commit v5 on v4

--- a/solution.py
+++ b/solution.py
@@ -930,7 +930,8 @@
             pltpu.SemaphoreType.DMA,
         ],
         steps=steps,
-        span=0.7,
+        lead=0,
+        span=0.6,
     )
 
 
@@ -1091,6 +1092,7 @@
             pltpu.SemaphoreType.DMA((5,)),
         ],
         steps=steps,
+        lead=0,
         span=0.8,
     )
 
@@ -1229,6 +1231,7 @@
             pltpu.SemaphoreType.DMA((6,)),
         ],
         steps=steps,
+        lead=0,
         span=0.6,
     )
 
@@ -1368,6 +1371,7 @@
             pltpu.SemaphoreType.DMA,
         ],
         steps=steps,
+        lead=0,
         span=0.6,
     )
 
@@ -1583,7 +1587,7 @@
 
 
 WEIGHTS_LAG = 0.9
-ROWS_LAG = 0.9
+ROWS_LAG = 0.95
 
 
 def gathered_body(
@@ -1755,7 +1759,7 @@
         shares,
         devices,
         cut(0, quarter, wide_orders)
-        + cut(1, quarter, wide_orders[:2] * 2)
+        + cut(1, [weight_rows // 2] * 2, wide_orders[:2])
         + cut(2, [weight_rows], wide_orders[2:3]),
         6,
     )

time: 928 us -> 925 us (level)
  transfers between devices with their start and end apart: 7 -> 7, of which waited for: 0 -> 0; matrix products, arithmetic and copies ran while one was open for 4% -> 4% of each run, Pallas kernels for 49% -> 50%
where the time goes in v5:
time: 925 us; the launch traced here: 920 us
  Pallas kernels  838 us (91%)
  matrix products  42.7 us (5%)
  other arithmetic  18.2 us (2%)
  local copies, waits for them, and re-layouts  15.6 us (2%)
    pallas_call x3, Pallas kernels, scatter(): pl.pallas_call(functools.partial(scatter_kernel, grid, parts, count, besi...  406 us
    pallas_call x2, Pallas kernels, gather(): pl.pallas_call(functools.partial(gather_kernel, grid, parts, lags, count,...  403 us
    pallas_call x1, Pallas kernels, alone(): pl.pallas_call(kernel, out_shape=beside.outs, in_specs=list(beside.in_spe...  29.5 us
    dot_general x2, matrix products, outer(): return jnp.einsum('sa,sb->ab', left, right, preferred_element_type=full)  19.1 us
  transfers between devices with their start and end apart: 7, of which 0 were waited for; matrix products, arithmetic and copies ran while one was open for 4% of the time, Pallas kernels for 50%

profile of v5, /device:TPU:8, one launch (start us, length us, event | category | flops | bytes accessed | tf_op | source)
XLA Modules:
  0.0 919.6 jit_solution(17614289342912818934)
XLA Ops:
  1.4 1.2 fusion.14
  4.0 1.7 slice_bitcast_fusion.1.refs_3_
  5.6 0.8 copy.52
  6.4 0.8 copy.53
  7.2 0.8 pad_maximum_fusion.1.refs_7_.refs_9_
  8.7 186.8 %shard_map.195 = (bf16[32,64,6144]{2,1,0:T(8,128)(2,1)}, bf16[32,64,128]{2,1,0:T(8,128)(2,1)}, bf16[32,64,2048]{2,1,0:T(8,128)(2,1)}, bf16[32,64,2048]{2,1,0:T(8...) custom-call(bf16[64,6144]{1,0:T(8,128)(2,1)} %refs_0_.1, ...), custom_call_target="tpu_custom_call" | custom-call | tf_op jit(solution)/shard_map/pallas_call | solution.py:541
  195.5 6.2 multiply_reduce_fusion.2
  201.8 1.2 slice_convert_fusion
  202.9 1.6 copy.65
  206.8 1.0 slice_bitcast_fusion.refs_2_
  207.8 216.2 %shard_map.196 = (bf16[16,256,2048]{2,1,0:T(8,128)(2,1)}, f32[16,40,256]{2,1,0:T(8,128)}, bf16[16,192,2048]{2,1,0:T(8,128)(2,1)}, bf16[2048,2048]{1,0:T(8,128)(2...) custom-call(bf16[256,2048]{1,0:T(8,128)(2,1)} %copy-done.5, ...), custom_call_target="tpu_custom_call" | custom-call | tf_op jit(solution)/shard_map/pallas_call | solution.py:541
  424.0 0.9 slice_reduce_fusion
  424.8 1.0 constant_dynamic-slice_fusion
  427.8 139.7 %shard_map.197 = (f32[256,2048]{1,0:T(8,128)}, bf16[2048,2048]{1,0:T(8,128)(2,1)}, bf16[2048,1024]{1,0:T(8,128)(2,1)}, bf16[2048,1024]{1,0:T(8,128)(2,1)}, bf16[...) custom-call(bf16[16,256,2048]{2,1,0:T(8,128)(2,1)} %get-tuple-element.54.refs_0_, ...), custom_call_target="tpu_custom_call" | custom-call | tf_op jit(solution)/shard_map/pallas_call | solution.py:708
  567.5 1.5 broadcast_select_fusion.refs_1_
  569.1 128.7 %shard_map.198 = (f32[256,2048]{1,0:T(8,128)}, f32[16,256]{1,0:T(8,128)}, f32[2048,512]{1,0:T(8,128)}, bf16[2048,512]{1,0:T(8,128)(2,1)}, f32[2048,512]{1,0:T(8,...) custom-call(bf16[16,256,2048]{2,1,0:T(8,128)(2,1)} %get-tuple-element.62.refs_0_, ...), custom_call_target="tpu_custom_call" | custom-call | tf_op jit(solution)/shard_map/pallas_call | solution.py:708
  699.1 0.8 multiply_reduce_fusion.3
  699.9 0.8 multiply_convert_fusion.2
  701.4 2.5 multiply_reduce_fusion
  704.5 1.1 copy-done.11
  705.6 2.6 fusion.23
  708.3 5.6 convolution_convert_fusion.1
  714.0 29.5 %shard_map.199 = (bf16[256,6144]{1,0:T(8,128)(2,1)}, f32[2,8,2048]{2,1,0:T(8,128)S(1)}, f32[2048,512]{1,0:T(8,128)}, f32[2048,512]{1,0:T(8,128)}, f32[512,2048]{1,0:T(8,128)}) custom-call(bf16[256,2048]{1,0:T(8,128)(2,1)S(1)} %get-tuple-element.136.refs_0_, bf16[2048,2048]{1,0:T(8,128)(2,1)} %bitcast.101, bf16[256,2048]{1,0:T(8,128)(2,1)S(1)} %copy-done.2, ...), custom_call_target="tpu_custom_call" | custom-call | tf_op jit(solution)/shard_map/pallas_call | solution.py:1489
  743.5 13.8 %fusion.6 = (f32[2048]{0:T(1024)S(1)}, f32[256]{0:T(256)S(1)}, f32[256,2048]{1,0:T(8,128)}) fusion(f32[256]{0:T(256)S(1)} %fusion.21, bf16[1,256,2048]{2,1,0:T(8,128)(2,1)S(1)} %copy-done.9, f32[2048]{0:T(1024)S(1)} %bitcast.114, bf16[256,6144]{1,0:T(8,128)(2,1)} %get-tuple-element.82, bf16[2048,6144]{1,0:T(8,128)(2,1)} %bitcast.119), kind=kOutput, calls=%fused_computation.15 | convolution fusion | flops 6446118912 | bytes 31475712 | tf_op jit(solution)/shard_map/te,de->td/dot_general | solution.py:1743
  757.7 13.5 %convolution_convert_fusion = bf16[2048,6144]{1,0:T(8,128)(2,1)} fusion(bf16[256,2048]{1,0:T(8,128)(2,1)} %get-tuple-element.84, bf16[256,6144]{1,0:T(8,128)(2,1)} %get-tuple-element.82), kind=kOutput, calls=%fused_computation | convolution fusion | flops 6455033856 | bytes 29360128 | tf_op jit(solution)/shard_map/sa,sb->ab/dot_general | solution.py:1749
  771.2 1.3 maximum_maximum_fusion
  772.5 137.1 %shard_map.200 = (f32[64,6144]{1,0:T(8,128)}, f32[64,2048]{1,0:T(8,128)}, f32[64,128]{1,0:T(8,128)}) custom-call(bf16[32,64,6144]{2,1,0:T(8,128)(2,1)} %bitcast.88, bf16[32,64,2048]{2,1,0:T(8,128)(2,1)} %bitcast.89, f32[32,64,128]{2,1,0:T(8,128)} %bitcast.105), custom_call_target="tpu_custom_call" | custom-call | tf_op jit(solution)/shard_map/pallas_call | solution.py:708
  909.6 0.8 slice_bitcast_fusion.2
  911.0 1.4 copy.59
  912.5 3.6 fusion.2
  916.1 1.1 copy.73
  917.4 0.8 copy.74
  (93 shorter events, 9.5 us)
Async XLA Ops:
  0.6 207.1 %collective-permute-start = (bf16[2048,512]{1,0:T(8,128)(2,1)}, bf16[2048,512]{1,0:T(8,128)(2,1)}, u32[]{:S(2)}, u32[]{:S(2)}) collective-permute-start(bf16[2048,512]{1,0:T(8,128)(2,1)} %bitcast.91), channel_id=1, source_target_pairs={{0,16},{16,0},{1,17},{17,1},{2,18},{18,2},{3,19},{19,3},{4,20},{20... | collective-permute-start | bytes 6291464 | tf_op jit(solution)/shard_map/ppermute | solution.py:1635
  0.7 207.1 %collective-permute-start.1 = (bf16[2048,512]{1,0:T(8,128)(2,1)}, bf16[2048,512]{1,0:T(8,128)(2,1)}, u32[]{:S(2)}, u32[]{:S(2)}) collective-permute-start(bf16[2048,512]{1,0:T(8,128)(2,1)} %bitcast.94), channel_id=1, source_target_pairs={{0,16},{16,0},{1,17},{17,1},{2,18},{18,2},{3,19},{19,3},{4,20},{20... | collective-permute-start | bytes 6291464 | tf_op jit(solution)/shard_map/ppermute | solution.py:1635
  1.2 206.6 %collective-permute-start.2 = (bf16[512,2048]{1,0:T(8,128)(2,1)}, bf16[512,2048]{1,0:T(8,128)(2,1)}, u32[]{:S(2)}, u32[]{:S(2)}) collective-permute-start(bf16[512,2048]{1,0:T(8,128)(2,1)} %bitcast.97), channel_id=1, source_target_pairs={{0,16},{16,0},{1,17},{17,1},{2,18},{18,2},{3,19},{19,3},{4,20},{20... | collective-permute-start | bytes 6291464 | tf_op jit(solution)/shard_map/ppermute | solution.py:1635
  2.6 192.9 %copy-start.7 = (bf16[1,256,2048]{2,1,0:T(8,128)(2,1)S(1)}, bf16[1,256,2048]{2,1,0:T(8,128)(2,1)}, u32[]{:S(2)}) copy-start(bf16[1,256,2048]{2,1,0:T(8,128)(2,1)} %param.12) | copy-start | bytes 3145732
  195.5 6.3 copy-start.12
  202.9 2.0 copy-start.13
  204.7 0.9 copy-start.21
  204.7 1.0 copy-start.20
  204.7 1.8 copy-start.8
  205.0 2.8 copy-start.5
  205.0 1.8 copy-start.14
  427.2 271.3 %collective-permute-start.3 = (f32[32]{0:T(128)S(1)}, f32[32]{0:T(128)S(1)}, u32[]{:S(2)}, u32[]{:S(2)}) collective-permute-start(f32[32]{0:T(128)S(1)} %slice_reduce_fusion), channel_id=1, source_target_pairs={{0,16},{16,0},{1,17},{17,1},{2,18},{18,2},{3,19},{19,3},{4,20},{20... | collective-permute-start | bytes 392 | tf_op jit(solution)/shard_map/ppermute | solution.py:1696
  697.8 16.1 %collective-permute-start.4 = (bf16[2048,512]{1,0:T(8,128)(2,1)}, bf16[2048,512]{1,0:T(8,128)(2,1)}, u32[]{:S(2)}, u32[]{:S(2)}) collective-permute-start(bf16[2048,512]{1,0:T(8,128)(2,1)} %get-tuple-element.77), channel_id=1, source_target_pairs={{0,16},{16,0},{1,17},{17,1},{2,18},{18,2},{3,19},{19,3},{4,20},{20... | collective-permute-start | bytes 6291464 | tf_op jit(solution)/shard_map/ppermute | solution.py:1718
  697.9 16.0 %collective-permute-start.5 = (bf16[2048,512]{1,0:T(8,128)(2,1)}, bf16[2048,512]{1,0:T(8,128)(2,1)}, u32[]{:S(2)}, u32[]{:S(2)}) collective-permute-start(bf16[2048,512]{1,0:T(8,128)(2,1)} %get-tuple-element.79), channel_id=1, source_target_pairs={{0,16},{16,0},{1,17},{17,1},{2,18},{18,2},{3,19},{19,3},{4,20},{20... | collective-permute-start | bytes 6291464 | tf_op jit(solution)/shard_map/ppermute | solution.py:1718
  698.4 15.5 %collective-permute-start.6 = (bf16[512,2048]{1,0:T(8,128)(2,1)}, bf16[512,2048]{1,0:T(8,128)(2,1)}, u32[]{:S(2)}, u32[]{:S(2)}) collective-permute-start(bf16[512,2048]{1,0:T(8,128)(2,1)} %get-tuple-element.81), channel_id=1, source_target_pairs={{0,16},{16,0},{1,17},{17,1},{2,18},{18,2},{3,19},{19,3},{4,20},{20... | collective-permute-start | bytes 6291464 | tf_op jit(solution)/shard_map/ppermute | solution.py:1718
  701.4 2.6 copy-start.6
  701.4 3.1 copy-start.15
  701.4 3.1 copy-start.16
  704.0 1.7 copy-start.11
  705.6 2.6 copy-start.17
  708.3 5.7 copy-start
  708.3 5.7 copy-start.1
  708.3 5.7 copy-start.2
  708.3 5.7 copy-start.3
  708.3 5.7 copy-start.4
  714.0 29.5 %copy-start.9 = (bf16[1,256,2048]{2,1,0:T(8,128)(2,1)S(1)}, bf16[1,256,2048]{2,1,0:T(8,128)(2,1)}, u32[]{:S(2)}) copy-start(bf16[1,256,2048]{2,1,0:T(8,128)(2,1)} %param.12) | copy-start | bytes 3145732
  772.5 140.0 %copy-start.10 = (f32[256,2048]{1,0:T(8,128)S(1)}, f32[256,2048]{1,0:T(8,128)}, u32[]{:S(2)}) copy-start(f32[256,2048]{1,0:T(8,128)} %get-tuple-element.137) | copy-start | bytes 6291460
  912.5 3.6 copy-start.18
  916.1 1.4 copy-start.19
